TPU v7x, 128 devices: a whole 4x4x4 slice. The times are simulated.
128 devices in a mesh: side: 2 (over core), gx: 64 (over z, x, y).
Axes of the slice: x: 4, y: 4, z: 4, core: 2. Of those that a mesh axis runs over, the one named last changes fastest.
Arguments:
- query: bfloat16 [1024, 8192], P(('side', 'gx')), may hold values from -18 to 18
- new_key: bfloat16 [1024, 1024], P(('side', 'gx')), may hold values from -6 to 6
- new_value: bfloat16 [1024, 1024], P(('side', 'gx')), may hold values from -6 to 6
- key_cache: bfloat16 [1024, 384, 1024], P(('side', 'gx')), may hold values from -18 to 18
- value_cache: bfloat16 [1024, 384, 1024], P(('side', 'gx')), may hold values from -6 to 6
- lengths: int32 [1024], P(('side', 'gx')), may hold values from 1 to 384, as said below
- residual: float32 [1024, 8192], P(('side', 'gx')), may hold values from -6 to 6
- norm_gain: float32 [8192], replicated, may hold values from 0.25 to 1.75
- gate_weight: bfloat16 [8192, 28672], P('side', 'gx'), may hold values from -0.0625 to 0.0625
- up_weight: bfloat16 [8192, 28672], P('side', 'gx'), may hold values from -0.0625 to 0.0625
- down_weight: bfloat16 [28672, 8192], P('gx', 'side'), may hold values from -0.03125 to 0.03125
Outputs:
- mixed: bfloat16 [1024, 8192], P(('side', 'gx'))
Inputs may be any that keep to these rules, and one draw needn't show every extreme that they name: `lengths`: every request has at least one valid cached position; some request has all 384.
All inputs are finite; a program needn't handle non-finite values.
Results may differ from a plain program's by a relative error of at most 0.015.
Values may be sent and summed in bfloat16 or wider, within the bound.
No kernel may reach another device: no remote copies, remote signals or barrier semaphores. Data moves between devices by JAX's collectives and lax.ppermute only.
A program may use at most 128 MiB of HBM per device.

v0:
```python
import jax
import jax.numpy as jnp
from jax import lax
from jax.sharding import PartitionSpec as P

HD = 128
BLK = 128


def attend_local(query, new_key, new_value, key_cache, value_cache, lengths):
    slots = query.shape[0]
    kv_heads = new_key.shape[1] // HD
    groups = query.shape[1] // (kv_heads * HD)
    scale = 1.0 / HD**0.5
    query_heads = query.reshape(slots, kv_heads, groups, HD)
    key_now = new_key.reshape(slots, kv_heads, HD)
    value_now = new_value.reshape(slots, kv_heads, HD).astype(jnp.float32)
    score_new = (
        jnp.einsum("skgd,skd->skg", query_heads, key_now, preferred_element_type=jnp.float32)
        * scale
    )
    start_total = jnp.ones_like(score_new)
    start_acc = jnp.broadcast_to(value_now[:, :, None, :], (slots, kv_heads, groups, HD))
    blocks = (jnp.max(lengths) + BLK - 1) // BLK

    def one_block(index, state):
        peak, total, acc = state
        key_block = lax.dynamic_slice_in_dim(key_cache, index * BLK, BLK, 1).reshape(
            slots, BLK, kv_heads, HD
        )
        value_block = lax.dynamic_slice_in_dim(value_cache, index * BLK, BLK, 1).reshape(
            slots, BLK, kv_heads, HD
        )
        scores = (
            jnp.einsum(
                "skgd,sbkd->skgb", query_heads, key_block, preferred_element_type=jnp.float32
            )
            * scale
        )
        places = index * BLK + jnp.arange(BLK, dtype=jnp.int32)
        valid = places[None, :] < lengths[:, None]
        scores = jnp.where(valid[:, None, None, :], scores, -jnp.inf)
        new_peak = jnp.maximum(peak, jnp.max(scores, axis=-1))
        factor = jnp.exp(peak - new_peak)
        probs = jnp.exp(scores - new_peak[..., None])
        total = total * factor + jnp.sum(probs, axis=-1)
        weighted = jnp.einsum(
            "skgb,sbkd->skgd",
            probs.astype(jnp.bfloat16),
            value_block,
            preferred_element_type=jnp.float32,
        )
        acc = acc * factor[..., None] + weighted
        return (new_peak, total, acc)

    peak, total, acc = lax.fori_loop(0, blocks, one_block, (score_new, start_total, start_acc))
    return (acc / total[..., None]).reshape(slots, kv_heads * groups * HD)


def body(
    query,
    new_key,
    new_value,
    key_cache,
    value_cache,
    lengths,
    residual,
    norm_gain,
    gate_weight,
    up_weight,
    down_weight,
):
    slots = query.shape[0]
    width = residual.shape[1]
    half = gate_weight.shape[0]
    attn = attend_local(query, new_key, new_value, key_cache, value_cache, lengths)
    h_mid = residual + attn
    mean_sq = jnp.mean(h_mid * h_mid, axis=-1, keepdims=True)
    normed = (h_mid * lax.rsqrt(mean_sq + 1e-05) * norm_gain[None, :]).astype(jnp.bfloat16)
    framed = normed.reshape(1, 1, slots, width)
    by_gx = lax.all_gather(framed, "gx", axis=0, tiled=True)
    every = lax.all_gather(by_gx, "side", axis=1, tiled=True)
    columns = lax.dynamic_slice_in_dim(every, lax.axis_index("side") * half, half, 3)
    rows_all = columns.reshape(-1, half)
    gate_part = jnp.dot(rows_all, gate_weight, preferred_element_type=jnp.float32)
    up_part = jnp.dot(rows_all, up_weight, preferred_element_type=jnp.float32)
    gate, up = (
        lax.psum(gate_part.astype(jnp.bfloat16), "side").astype(jnp.float32),
        lax.psum(up_part.astype(jnp.bfloat16), "side").astype(jnp.float32),
    )
    hidden = (jax.nn.silu(gate) * up).astype(jnp.bfloat16)
    summed = lax.psum_scatter(
        jnp.dot(hidden, down_weight, preferred_element_type=jnp.float32),
        "gx",
        scatter_dimension=0,
        tiled=True,
    )
    ffn = lax.all_to_all(
        summed.astype(jnp.bfloat16), "side", split_axis=0, concat_axis=1, tiled=True
    ).astype(summed.dtype)
    return (h_mid + ffn).astype(jnp.bfloat16)


def solution(mesh):
    in_specs = (
        P(("side", "gx"), None),
        P(("side", "gx"), None),
        P(("side", "gx"), None),
        P(("side", "gx"), None, None),
        P(("side", "gx"), None, None),
        P(("side", "gx")),
        P(("side", "gx"), None),
        P(),
        P("side", "gx"),
        P("side", "gx"),
        P("gx", "side"),
    )
    out_specs = P(("side", "gx"), None)
    return jax.shard_map(body, mesh=mesh, in_specs=in_specs, out_specs=out_specs, check_vma=False)
```

profile of v0, /device:TPU:1, one launch (start us, length us, event | category | flops | bytes accessed | tf_op | source)
XLA Modules:
  0.0 633.6 jit_solution(12808372571905651781)
XLA Ops:
  6.5 1.3 reduce_max.18
  8.5 0.9 copy.36
  9.4 0.2 fusion.14
  9.7 0.7 bitcast_convert_fusion
  10.5 26.6 %while.14 = (s32[]{:T(128)}, f32[8,8,8]{2,1,0:T(8,128)S(1)}, f32[8,8,8]{2,1,0:T(8,128)S(1)}, f32[8,8,8,128]{3,2,1,0:T(8,128)S(1)}, s32[]{:T(128)}, /*index=5*/s3...) while((s32[]{:T(128)}, f32[8,8,8]{2,1,0:T(8,128)S(1)}, ...), condition=%wide.region_4.5_spmd, body=%wide.region_1.4_spmd.sunk | while | flops 34146436 | bytes 22449520 | solution.py:56
  10.5 4.8 constant_dynamic-slice_fusion.4
  15.3 3.0 copy.39
  18.5 0.7 fusion.37
  19.2 0.3 fusion.38
  19.5 3.0 copy.40
  22.6 1.2 convolution_add_fusion.2
  23.8 4.8 constant_dynamic-slice_fusion.4
  28.6 3.0 copy.39
  31.7 0.7 fusion.37
  32.5 0.3 fusion.38
  32.8 3.0 copy.40
  35.8 1.2 convolution_add_fusion.2
  37.0 0.2 divide_bitcast_fusion
  37.2 0.3 multiply_reduce_fusion
  37.5 0.8 multiply_convert_fusion
  38.4 95.1 %all-gather.6.cloned.1.call-done = bf16[512,8192]{1,0:T(8,128)(2,1)} async-done(((bf16[8,8192]{1,0:T(8,128)(2,1)}), bf16[512,8192]{1,0:T(8,128)(2,1)}) %all-gather.6.cloned.1.call-update) | async-done | bytes 8388624 | tf_op jit(solution)/shard_map/all_gather | solution.py:81
  133.6 34.4 %all-gather.4.cloned.1.call-done = bf16[64,2,8,8192]{3,2,1,0:T(8,128)(2,1)} async-done(((bf16[64,1,8,8192]{3,2,1,0:T(8,128)(2,1)}), bf16[64,2,8,8192]{3,2,1,0:T(8,128)(2,1)}) %all-gather.4.cloned.1.call-update) | async-done | bytes 16777232 | tf_op jit(solution)/shard_map/all_gather | solution.py:82
  168.0 7.7 %constant_dynamic-slice_fusion.2 = bf16[64,2,8,4096]{3,2,1,0:T(8,128)(2,1)} fusion(bf16[64,2,8,8192]{3,2,1,0:T(8,128)(2,1)} %all-gather.4.cloned.1.call-done, s32[]{:T(128)S(6)} %select_n.20), kind=kLoop, calls=%fused_computation.37 | loop fusion | bytes 16777220 | tf_op jit(solution)/shard_map/dynamic_slice | solution.py:83
  175.7 9.5 %convolution_convert_fusion = bf16[1024,448]{0,1:T(8,128)(2,1)} fusion(bf16[1024,4096]{1,0:T(8,128)(2,1)} %bitcast.57, bf16[4096,448]{0,1:T(8,128)(2,1)} %param.22), kind=kOutput, calls=%fused_computation.21 | convolution fusion | flops 3758555136 | bytes 12976128 | tf_op jit(solution)/shard_map/dot_general | solution.py:86
  185.2 4.9 convolution_convert_fusion.1
  190.2 0.2 reduce-scatter.2.cloned.1.call-start
  190.4 27.7 %all-reduce.3.cloned.1.call-done = (bf16[1024,448]{0,1:T(8,128)(2,1)}, bf16[1024,448]{0,1:T(8,128)(2,1)}) async-done(((bf16[1024,448]{0,1:T(8,128)(2,1)}, bf16[1024,448]{0,1:T(8,128)(2,1)}), (bf16[1024,448]{0,1:T(8,128)(2,1)}, bf16[1024,448]{0,1:T(8,128)(2,1)})) %all-reduce.3.cloned.1.call-update) | async-done | bytes 1835024 | tf_op jit(solution)/shard_map/psum | solution.py:89
  218.2 13.0 %fusion.11 = f32[1024,4096]{1,0:T(8,128)} fusion(bf16[448,4096]{1,0:T(8,128)(2,1)} %param.23, bf16[1024,448]{0,1:T(8,128)(2,1)} %get-tuple-element.83, bf16[1024,448]{0,1:T(8,128)(2,1)} %get-tuple-element.84), kind=kOutput, calls=%fused_computation.23 | convolution fusion | flops 3761766400 | bytes 22282240 | tf_op jit(solution)/shard_map/dot_general | solution.py:93
  231.2 340.4 %reduce-scatter.2.cloned.1.call-done = f32[16,4096]{1,0:T(8,128)} async-done(((f32[1024,4096]{1,0:T(8,128)}), f32[16,4096]{1,0:T(8,128)}) %reduce-scatter.2.cloned.1.call-update) | async-done | bytes 262160 | tf_op jit(solution)/shard_map/reduce_scatter | solution.py:92
  571.7 1.0 convert_bitcast_fusion
  572.6 53.6 %all_to_all.13 = bf16[2,8,4096]{2,1,0:T(8,128)(2,1)S(1)} all-to-all(bf16[2,8,4096]{2,1,0:T(8,128)(2,1)S(1)} %convert_bitcast_fusion), channel_id=1, replica_groups=mesh['side'=2,'gx'=64] {'side'}, dimensions={0} | all-to-all | bytes 262144 | tf_op jit(solution)/shard_map/all_to_all | solution.py:98
  626.2 0.8 add_convert_fusion
  (39 shorter events, 0.5 us)
Async XLA Ops:
  6.5 2.9 copy-start
  6.5 127.0 %all-gather.6.cloned.1.call-start = ((), (), s32[]{:S(2)}) async-start(), calls=%async_computation.4 | async-start | bytes 8519680 | tf_op jit(solution)/shard_map/all_gather | solution.py:81
  10.5 26.8 %copy-start.3 = (f32[8,8192]{1,0:T(8,128)S(1)}, f32[8,8192]{1,0:T(8,128)}, u32[]{:S(2)}) copy-start(f32[8,8192]{1,0:T(8,128)} %param.19) | copy-start | bytes 786436
  10.5 27.0 %copy-start.4 = (f32[8192]{0:T(1024)S(1)}, f32[8192]{0:T(1024)}, u32[]{:S(2)}) copy-start(f32[8192]{0:T(1024)} %param.20) | copy-start | bytes 98308
  15.3 3.1 copy-start.5
  28.6 3.1 copy-start.5
  38.3 129.7 %all-gather.4.cloned.1.call-start = ((), (), s32[]{:S(2)}) async-start(), calls=%async_computation.2 | async-start | bytes 25165824 | tf_op jit(solution)/shard_map/all_gather | solution.py:82
  133.6 84.6 %all-reduce.3.cloned.1.call-start = ((), (), s32[]{:S(2)}) async-start(), calls=%async_computation.5 | async-start | bytes 3670016 | tf_op jit(solution)/shard_map/psum | solution.py:89
  175.7 9.5 %copy-start.2 = (bf16[64,2,8,4096]{3,2,1,0:T(8,128)(2,1)S(1)}, bf16[64,2,8,4096]{3,2,1,0:T(8,128)(2,1)}, u32[]{:S(2)}) copy-start(bf16[64,2,8,4096]{3,2,1,0:T(8,128)(2,1)} %constant_dynamic-slice_fusion.2) | copy-start | bytes 25165828
  175.7 9.5 %copy-start.6 = (bf16[4096,448]{0,1:T(8,128)(2,1)S(1)}, bf16[4096,448]{0,1:T(8,128)(2,1)}, u32[]{:S(2)}) copy-start(bf16[4096,448]{0,1:T(8,128)(2,1)} %param.21) | copy-start | bytes 11010052
  190.2 381.4 %reduce-scatter.2.cloned.1.call-start = ((), (), s32[]{:S(2)}) async-start(), calls=%async_computation.3 | async-start | bytes 17039360 | tf_op jit(solution)/shard_map/reduce_scatter | solution.py:92
  231.2 395.8 %copy-start.1 = (bf16[8,1024]{1,0:T(8,128)(2,1)S(1)}, bf16[8,1024]{1,0:T(8,128)(2,1)}, u32[]{:S(2)}) copy-start(bf16[8,1024]{1,0:T(8,128)(2,1)} %param.14) | copy-start | bytes 49156
Sparse Core Ops, SparseCore 0:
  38.5 95.0 all-gather.5
  135.2 32.7 all-gather.3
  190.3 27.7 all-reduce.2
  231.3 340.2 reduce-scatter.1
where the time goes:
time: 634 us
  waiting for transfers between devices  498 us (79%)
  blocking collectives  53.6 us (8%)
  matrix products  31.6 us (5%)
  local copies, waits for them, and re-layouts  30.5 us (5%)
  between operations  13.9 us (2%)
    reduce_scatter x1, waiting for transfers between devices, body(): lax.psum_scatter(jnp.dot(hidden, down_weight, preferred_element_type=jnp....  340 us
    all_gather x1, waiting for transfers between devices, body(): by_gx = lax.all_gather(framed, 'gx', axis=0, tiled=True)  95.1 us
    all_to_all x1, blocking collectives, body(): lax.all_to_all(summed.astype(jnp.bfloat16), 'side', split_axis=0, concat_...  53.6 us
    all_gather x1, waiting for transfers between devices, body(): every = lax.all_gather(by_gx, 'side', axis=1, tiled=True)  34.4 us
    psum x1, waiting for transfers between devices, body(): lax.psum(up_part.astype(jnp.bfloat16), 'side').astype(jnp.float32)  27.7 us
    dynamic_slice x4, local copies, waits for them, and re-layouts, one_block(): lax.dynamic_slice_in_dim(value_cache, index * BLK, BLK, 1)  15.7 us
    dot_general x1, matrix products, body(): jnp.dot(hidden, down_weight, preferred_element_type=jnp.float32)  13 us
  transfers between devices with their start and end apart: 4, of which 4 were waited for; matrix products, arithmetic and copies ran while one was open for 0% of the time, Pallas kernels for 0%

commit v1 on v0

v1 whole, which is shorter than its diff:
```python
import jax
import jax.numpy as jnp
from jax import lax
from jax.experimental import pallas as pl
from jax.experimental.pallas import tpu as pltpu
from jax.sharding import PartitionSpec as P

HD = 128
SWAP = [(0, 1), (1, 0)]


def attend_kernel(
    lengths_ref, query_ref, new_key_ref, new_value_ref, key_ref, value_ref, residual_ref, gain_ref,
    mid_ref, normed_ref,
):
    per_step, heads, _ = query_ref.shape
    kv_heads = new_key_ref.shape[1]
    groups = heads // kv_heads
    ctx = key_ref.shape[1]
    scale = 1.0 / HD**0.5
    step = pl.program_id(0)
    row_group = lax.broadcasted_iota(jnp.int32, (heads, kv_heads * HD), 0) // groups
    col_group = lax.broadcasted_iota(jnp.int32, (heads, kv_heads * HD), 1) // HD
    own = row_group == col_group
    places = lax.broadcasted_iota(jnp.int32, (heads, ctx), 1)
    for slot in range(per_step):
        length = lengths_ref[step * per_step + slot]
        query = query_ref[slot]
        wide = jnp.where(own, jnp.concatenate([query] * kv_heads, axis=1), 0).astype(jnp.bfloat16)
        scores = (
            lax.dot_general(
                wide, key_ref[slot], (((1,), (1,)), ((), ())), preferred_element_type=jnp.float32
            )
            * scale
        )
        scores = jnp.where(places < length, scores, -jnp.inf)
        key_now = jnp.broadcast_to(
            new_key_ref[slot].astype(jnp.float32)[:, None, :], (kv_heads, groups, HD)
        ).reshape(heads, HD)
        value_now = jnp.broadcast_to(
            new_value_ref[slot].astype(jnp.float32)[:, None, :], (kv_heads, groups, HD)
        ).reshape(heads, HD)
        score_new = jnp.sum(query.astype(jnp.float32) * key_now, axis=1, keepdims=True) * scale
        peak = jnp.maximum(jnp.max(scores, axis=1, keepdims=True), score_new)
        probs = jnp.exp(scores - peak)
        prob_new = jnp.exp(score_new - peak)
        total = jnp.sum(probs, axis=1, keepdims=True) + prob_new
        spread = jnp.dot(
            probs.astype(jnp.bfloat16), value_ref[slot], preferred_element_type=jnp.float32
        )
        picked = jnp.concatenate(
            [
                spread[g * groups : (g + 1) * groups, g * HD : (g + 1) * HD]
                for g in range(kv_heads)
            ],
            axis=0,
        )
        summed = picked + prob_new.astype(jnp.bfloat16).astype(jnp.float32) * value_now
        mid = residual_ref[slot] + summed / total
        mid_ref[slot] = mid
        mean_sq = jnp.sum(jnp.sum(mid * mid, axis=1, keepdims=True), axis=0, keepdims=True) / (
            heads * HD
        )
        normed_ref[slot] = (mid * lax.rsqrt(mean_sq + 1e-05) * gain_ref[...]).astype(jnp.bfloat16)


def attend(query, new_key, new_value, key_cache, value_cache, lengths, residual, norm_gain):
    slots, width = query.shape
    heads = width // HD
    ctx, kv_width = key_cache.shape[1:]
    kv_heads = kv_width // HD
    per_step = 2 if slots % 2 == 0 else 1

    def rows(*shape):
        return pl.BlockSpec((per_step,) + shape, lambda i: (i,) + (0,) * len(shape))

    return pl.pallas_call(
        attend_kernel,
        grid=(slots // per_step,),
        in_specs=[
            pl.BlockSpec(memory_space=pltpu.SMEM),
            rows(heads, HD),
            rows(kv_heads, HD),
            rows(kv_heads, HD),
            rows(ctx, kv_width),
            rows(ctx, kv_width),
            rows(heads, HD),
            pl.BlockSpec((heads, HD), lambda i: (0, 0)),
        ],
        out_specs=[rows(heads, HD), rows(heads, HD)],
        out_shape=[
            jax.ShapeDtypeStruct((slots, heads, HD), jnp.float32),
            jax.ShapeDtypeStruct((slots, heads, HD), jnp.bfloat16),
        ],
        compiler_params=pltpu.CompilerParams(vmem_limit_bytes=40 * 1024 * 1024),
        name="attend",
    )(
        lengths,
        query.reshape(slots, heads, HD),
        new_key.reshape(slots, kv_heads, HD),
        new_value.reshape(slots, kv_heads, HD),
        key_cache,
        value_cache,
        residual.reshape(slots, heads, HD),
        norm_gain.reshape(heads, HD),
    )


def body(
    query,
    new_key,
    new_value,
    key_cache,
    value_cache,
    lengths,
    residual,
    norm_gain,
    gate_weight,
    up_weight,
    down_weight,
):
    slots, width = residual.shape
    half = gate_weight.shape[0]
    mid, normed = attend(
        query, new_key, new_value, key_cache, value_cache, lengths, residual, norm_gain
    )
    pair = lax.all_to_all(
        normed.reshape(slots, 2, half), "side", split_axis=1, concat_axis=0, tiled=True
    ).reshape(2 * slots, half)
    rows_all = lax.all_gather(pair, "gx", axis=0, tiled=True)
    gate_part = jnp.dot(rows_all, gate_weight, preferred_element_type=jnp.float32)
    up_part = jnp.dot(rows_all, up_weight, preferred_element_type=jnp.float32)
    gate_part, up_part = gate_part.astype(jnp.bfloat16), up_part.astype(jnp.bfloat16)
    gate = gate_part.astype(jnp.float32) + lax.ppermute(gate_part, "side", SWAP).astype(jnp.float32)
    up = up_part.astype(jnp.float32) + lax.ppermute(up_part, "side", SWAP).astype(jnp.float32)
    hidden = (jax.nn.silu(gate) * up).astype(jnp.bfloat16)
    partial = jnp.dot(hidden, down_weight, preferred_element_type=jnp.float32).astype(jnp.bfloat16)
    blocks = lax.all_to_all(
        partial.reshape(-1, 2 * slots, half), "gx", split_axis=0, concat_axis=0, tiled=True
    )
    summed = jnp.sum(blocks.astype(jnp.float32), axis=0).astype(jnp.bfloat16)
    ffn = lax.all_to_all(
        summed.reshape(2, slots, half), "side", split_axis=0, concat_axis=2, tiled=True
    ).reshape(slots, width)
    return (mid.reshape(slots, width) + ffn.astype(jnp.float32)).astype(jnp.bfloat16)


def solution(mesh):
    in_specs = (
        P(("side", "gx"), None),
        P(("side", "gx"), None),
        P(("side", "gx"), None),
        P(("side", "gx"), None, None),
        P(("side", "gx"), None, None),
        P(("side", "gx")),
        P(("side", "gx"), None),
        P(),
        P("side", "gx"),
        P("side", "gx"),
        P("gx", "side"),
    )
    out_specs = P(("side", "gx"), None)
    return jax.shard_map(body, mesh=mesh, in_specs=in_specs, out_specs=out_specs, check_vma=False)
```

time: 634 us -> 254 us (0.40)
  waiting for transfers between devices: 498 us -> 83.5 us
  blocking collectives: 53.6 us -> 115 us
  local copies, waits for them, and re-layouts: 30.5 us -> 9.78 us
  matrix products: 31.6 us -> 18.2 us
    reduce_scatter x1 -> x0, waiting for transfers between devices: 340 us -> none  [body(): lax.psum_scatter(jnp.dot(hidden, down_weight, preferred_element_type=jnp....]
    all_to_all x1 -> x3, blocking collectives: 53.6 us -> 115 us  [the longest x1 104 us: body(): lax.all_to_all(partial.reshape(-1, 2 * slots, half), 'gx', split_axis=0,...]
    all_gather x2 -> x1, waiting for transfers between devices: 130 us -> 81 us  [body(): rows_all = lax.all_gather(pair, 'gx', axis=0, tiled=True)]
    dynamic_slice x7 -> x0, local copies, waits for them, and re-layouts: 29.5 us -> none  [the longest x4 15.7 us: one_block(): lax.dynamic_slice_in_dim(value_cache, index * BLK, BLK, 1)]
    psum x1 -> x0, waiting for transfers between devices: 27.7 us -> none  [body(): lax.psum(up_part.astype(jnp.bfloat16), 'side').astype(jnp.float32)]
    unnamed x13 -> x16, local copies, waits for them, and re-layouts: 0.96 us -> 8.92 us
    dot_general x1, matrix products: 13 us -> 5.72 us  [body(): jnp.dot(hidden, down_weight, preferred_element_type=jnp.float32)]
  transfers between devices with their start and end apart: 4 -> 3, of which waited for: 4 -> 2; matrix products, arithmetic and copies ran while one was open for 0% -> 2% of each run, Pallas kernels for 0% -> 0%
where the time goes in v1:
time: 254 us; the launch traced here: 253 us
  blocking collectives  115 us (45%)
  waiting for transfers between devices  83.5 us (33%)
  matrix products  18.2 us (7%)
  between operations  13.5 us (5%)
  local copies, waits for them, and re-layouts  9.78 us (4%)
  Pallas kernels  6.26 us (2%)
  other arithmetic  5.64 us (2%)
    all_to_all x1, blocking collectives, body(): lax.all_to_all(partial.reshape(-1, 2 * slots, half), 'gx', split_axis=0,...  104 us
    all_gather x1, waiting for transfers between devices, body(): rows_all = lax.all_gather(pair, 'gx', axis=0, tiled=True)  81 us
    unnamed x16, local copies, waits for them, and re-layouts  8.92 us
    dot_general x1, matrix products, body(): jnp.dot(rows_all, gate_weight, preferred_element_type=jnp.float32)  8.55 us
    pallas_call x1, Pallas kernels, attend(): pl.pallas_call(attend_kernel, grid=(slots // per_step,), in_specs=[pl.Blo...  6.26 us
    dot_general x1, matrix products, body(): jnp.dot(hidden, down_weight, preferred_element_type=jnp.float32)  5.72 us
    all_to_all x1, blocking collectives, body(): lax.all_to_all(normed.reshape(slots, 2, half), 'side', split_axis=1, conc...  5.61 us
    all_to_all x1, blocking collectives, body(): lax.all_to_all(summed.reshape(2, slots, half), 'side', split_axis=0, conc...  5.48 us
  transfers between devices with their start and end apart: 3, of which 2 were waited for; matrix products, arithmetic and copies ran while one was open for 2% of the time, Pallas kernels for 0%

profile of v1, /device:TPU:1, one launch (start us, length us, event | category | flops | bytes accessed | tf_op | source)
XLA Modules:
  0.0 253.0 jit_solution(1421485496165944011)
XLA Ops:
  6.5 0.0 all-gather.2.cloned.1.call-start
  6.5 0.9 copy.24
  7.5 1.0 copy.23
  8.5 0.7 copy_bitcast_fusion.2
  9.2 0.0 copy-start
  9.2 2.8 %copy-done = bf16[8,384,1024]{2,1,0:T(8,128)(2,1)S(1)} copy-done((bf16[8,384,1024]{2,1,0:T(8,128)(2,1)S(1)}, bf16[8,384,1024]{2,1,0:T(8,128)(2,1)}, u32[]{:S(2)}) %copy-start) | copy-done | bytes 6291480
  12.0 0.0 copy-start.1
  12.0 2.8 %copy-done.1 = bf16[8,384,1024]{2,1,0:T(8,128)(2,1)S(1)} copy-done((bf16[8,384,1024]{2,1,0:T(8,128)(2,1)S(1)}, bf16[8,384,1024]{2,1,0:T(8,128)(2,1)}, u32[]{:S(2)}) %copy-start.1) | copy-done | bytes 6291480
  14.8 0.0 copy-start.2
  14.8 0.8 copy-done.2
  15.5 0.0 copy-start.3
  15.5 0.7 copy-done.3
  16.2 6.3 %attend.1 = (f32[8,64,128]{2,1,0:T(8,128)S(1)}, bf16[8,64,128]{2,1,0:T(8,128)(2,1)S(1)}) custom-call(s32[8]{0:T(128)S(1)} %copy-done.3, bf16[8,64,128]{2,1,0:T(8,128)(2,1)S(1)} %bitcast.39, bf16[8,8,128]{2,1,0:T(8,128)(2,1)S(1)} %get-tuple-element.10.new_key_ref, bf16[8,8,128]{2,1,0:T(8,128)(2,1)S(1)} %get-tuple-element.9.new_value_ref, ...), custom_call_target="tpu_custom_call" | custom-call | tf_op jit(solution)/shard_map/attend/pallas_call | solution.py:77
  22.5 0.1 copy.12
  22.6 5.6 %all_to_all.29 = bf16[8,2,4096]{2,0,1:T(8,128)(2,1)} all-to-all(bf16[8,2,4096]{2,0,1:T(8,128)(2,1)S(1)} %copy.12), channel_id=1, replica_groups=mesh['side'=2,'gx'=64] {'side'}, dimensions={1} | all-to-all | bytes 262144 | tf_op jit(solution)/shard_map/all_to_all | solution.py:127
  28.2 0.0 all-gather.2.cloned.1.call-update
  28.2 81.0 %all-gather.2.cloned.1.call-done = bf16[1024,4096]{1,0:T(8,128)(2,1)} async-done(((bf16[16,4096]{1,0:T(8,128)(2,1)}), bf16[1024,4096]{1,0:T(8,128)(2,1)}) %all-gather.2.cloned.1.call-update) | async-done | bytes 8388624 | tf_op jit(solution)/shard_map/all_gather | solution.py:130
  109.3 8.6 %convolution_convert_fusion.2 = bf16[1024,448]{0,1:T(8,128)(2,1)S(1)} fusion(bf16[1024,4096]{1,0:T(8,128)(2,1)} %all-gather.2.cloned.1.call-done, bf16[4096,448]{0,1:T(8,128)(2,1)} %param.19), kind=kOutput, calls=%fused_computation.3 | convolution fusion | flops 3758555136 | bytes 12976128 | tf_op jit(solution)/shard_map/dot_general | solution.py:131
  117.8 0.0 copy-start.6
  117.8 0.8 collective-permute-start
  118.6 0.0 copy-done.4
  118.6 0.0 copy-done.5
  118.6 4.0 %convolution_convert_fusion.1 = bf16[1024,448]{0,1:T(8,128)(2,1)S(1)} fusion(bf16[1024,4096]{1,0:T(8,128)(2,1)S(1)} %copy-done.4, bf16[4096,448]{0,1:T(8,128)(2,1)S(1)} %copy-done.5), kind=kOutput, calls=%fused_computation.2 | convolution fusion | flops 3758555136 | bytes 12976128 | tf_op jit(solution)/shard_map/dot_general | solution.py:132
  122.6 0.1 collective-permute-start.1
  122.7 0.0 collective-permute-done
  122.7 2.4 collective-permute-done.1
  125.1 0.0 copy-done.6
  125.1 5.7 %convolution_convert_fusion = bf16[1024,4096]{1,0:T(8,128)(2,1)S(1)} fusion(bf16[448,4096]{1,0:T(8,128)(2,1)S(1)} %copy-done.6, bf16[1024,448]{0,1:T(8,128)(2,1)S(1)} %collective-permute-done.1, bf16[1024,448]{0,1:T(8,128)(2,1)S(1)} %convolution_convert_fusion.1, bf16[1024,448]{0,1:T(8,128)(2,1)S(1)} %collective-permute-done, ...), kind=kOutput, calls=%fused_computation | convolution fusion | flops 3767795712 | bytes 15728640 | tf_op jit(solution)/shard_map/dot_general | solution.py:137
  130.9 104.2 %all_to_all.30 = bf16[64,16,4096]{2,1,0:T(8,128)(2,1)} all-to-all(bf16[64,16,4096]{2,1,0:T(8,128)(2,1)S(1)} %bitcast.42), channel_id=1, replica_groups=mesh['side'=2,'gx'=64] {'gx'}, dimensions={0} | all-to-all | bytes 16777216 | tf_op jit(solution)/shard_map/all_to_all | solution.py:138
  235.1 4.8 %reduce_sum.12 = bf16[16,4096]{1,0:T(8,128)(2,1)S(1)} reduce(bf16[64,16,4096]{2,1,0:T(8,128)(2,1)} %all_to_all.30, bf16[]{:T(256)} %constant.5.clone.1), dimensions={0}, to_apply=%region_0.1 | reduce | flops 4128768 | bytes 8519682 | tf_op jit(solution)/shard_map/reduce_sum | solution.py:141
  239.9 5.5 %all_to_all.31 = bf16[2,8,4096]{2,1,0:T(8,128)(2,1)S(1)} all-to-all(bf16[2,8,4096]{2,1,0:T(8,128)(2,1)S(1)} %bitcast.44), channel_id=1, replica_groups=mesh['side'=2,'gx'=64] {'side'}, dimensions={0} | all-to-all | bytes 262144 | tf_op jit(solution)/shard_map/all_to_all | solution.py:142
  245.4 0.8 fusion.1
  (4 shorter events, 0.1 us)
Async XLA Ops:
  6.5 102.7 %all-gather.2.cloned.1.call-start = ((), (), s32[]{:S(2)}) async-start(), calls=%async_computation.3 | async-start | bytes 8519680 | tf_op jit(solution)/shard_map/all_gather | solution.py:130
  9.2 2.8 %copy-start = (bf16[8,384,1024]{2,1,0:T(8,128)(2,1)S(1)}, bf16[8,384,1024]{2,1,0:T(8,128)(2,1)}, u32[]{:S(2)}) copy-start(bf16[8,384,1024]{2,1,0:T(8,128)(2,1)} %key_ref.1) | copy-start | bytes 18874372
  12.0 2.8 %copy-start.1 = (bf16[8,384,1024]{2,1,0:T(8,128)(2,1)S(1)}, bf16[8,384,1024]{2,1,0:T(8,128)(2,1)}, u32[]{:S(2)}) copy-start(bf16[8,384,1024]{2,1,0:T(8,128)(2,1)} %value_ref.1) | copy-start | bytes 18874372
  14.8 0.8 copy-start.2
  15.5 0.7 copy-start.3
  109.2 9.3 %copy-start.4 = (bf16[1024,4096]{1,0:T(8,128)(2,1)S(1)}, bf16[1024,4096]{1,0:T(8,128)(2,1)}, u32[]{:S(2)}) copy-start(bf16[1024,4096]{1,0:T(8,128)(2,1)} %all-gather.2.cloned.1.call-done) | copy-start | bytes 25165828
  109.3 9.3 %copy-start.5 = (bf16[4096,448]{0,1:T(8,128)(2,1)S(1)}, bf16[4096,448]{0,1:T(8,128)(2,1)}, u32[]{:S(2)}) copy-start(bf16[4096,448]{0,1:T(8,128)(2,1)} %param.20) | copy-start | bytes 11010052
  117.8 7.3 %copy-start.6 = (bf16[448,4096]{1,0:T(8,128)(2,1)S(1)}, bf16[448,4096]{1,0:T(8,128)(2,1)}, u32[]{:S(2)}) copy-start(bf16[448,4096]{1,0:T(8,128)(2,1)} %param.21) | copy-start | bytes 11010052
  117.8 4.9 %collective-permute-start = (bf16[1024,448]{0,1:T(8,128)(2,1)S(1)}, bf16[1024,448]{0,1:T(8,128)(2,1)S(1)}, u32[]{:S(2)}, u32[]{:S(2)}) collective-permute-start(bf16[1024,448]{0,1:T(8,128)(2,1)S(1)} %convolution_convert_fusion.2), channel_id=1, source_target_pairs={{0,64},{64,0},{1,65},{65,1},{2,66},{66,2},{3,67},{67,3},{4,68},{68... | collective-permute-start | bytes 2752520 | tf_op jit(solution)/shard_map/ppermute | solution.py:134
  122.6 2.6 %collective-permute-start.1 = (bf16[1024,448]{0,1:T(8,128)(2,1)S(1)}, bf16[1024,448]{0,1:T(8,128)(2,1)S(1)}, u32[]{:S(2)}, u32[]{:S(2)}) collective-permute-start(bf16[1024,448]{0,1:T(8,128)(2,1)S(1)} %convolution_convert_fusion.1), channel_id=1, source_target_pairs={{0,64},{64,0},{1,65},{65,1},{2,66},{66,2},{3,67},{67,3},{4,68},{68... | collective-permute-start | bytes 2752520 | tf_op jit(solution)/shard_map/ppermute | solution.py:135
Sparse Core Ops, SparseCore 0:
  28.3 80.8 all-gather.1

commit v2 on v1

--- a/solution.py
+++ b/solution.py
@@ -1,3 +1,5 @@
+import functools
+
 import jax
 import jax.numpy as jnp
 from jax import lax
@@ -7,6 +9,68 @@
 
 HD = 128
 SWAP = [(0, 1), (1, 0)]
+RING = 4
+VMEM = 60 * 1024 * 1024
+NEAR, FAR = (0, 1, 3), 2
+LINES = {"first": ("x", "z"), "second": ("z", "y"), "third": ("y", "x")}
+
+
+def chip(z, x, y):
+    return (z % RING) * RING * RING + (x % RING) * RING + y % RING
+
+
+def hops(line, distance):
+    pairs = []
+    for side in range(2):
+        dz, dx, dy = (distance * (axis == LINES[line][side]) for axis in "zxy")
+        for z in range(RING):
+            for x in range(RING):
+                for y in range(RING):
+                    here, there = chip(z, x, y), chip(z + dz, x + dx, y + dy)
+                    pairs.append((side * RING**3 + here, side * RING**3 + there))
+    return pairs
+
+
+def send(array, line, distance):
+    return lax.ppermute(array, ("side", "gx"), hops(line, distance))
+
+
+def fetch(array, line, distance):
+    return lax.ppermute(array, ("side", "gx"), [(there, here) for here, there in hops(line, distance)])
+
+
+def gather_line(array, line):
+    far = fetch(array, line, 2)
+    return [array, fetch(array, line, 1), far, fetch(array, line, 3)]
+
+
+def gather_ring(top, bottom, line):
+    after_top, before_bottom = fetch(top, line, 1), fetch(bottom, line, 3)
+    after_bottom, before_top = fetch(bottom, line, 1), fetch(top, line, 3)
+    far = [fetch(after_top, line, 1), fetch(before_bottom, line, 3)]
+    return [[top, bottom], [after_top, after_bottom], far, [before_top, before_bottom]]
+
+
+def behind(array, *others):
+    return lax.optimization_barrier((array, *others))[0]
+
+
+def add(*arrays):
+    return sum(array.astype(jnp.float32) for array in arrays).astype(jnp.bfloat16)
+
+
+def reduce_line(blocks, line):
+    far = send(blocks[2], line, 2)
+    return add(blocks[0], send(blocks[1], line, 1), far, send(blocks[3], line, 3))
+
+
+def parts(array):
+    rows = array.shape[0] // RING
+    return [array[i * rows : (i + 1) * rows] for i in range(RING)]
+
+
+def dot(left, right):
+    return jnp.dot(left, right, preferred_element_type=jnp.float32)
 
 
 def attend_kernel(
@@ -92,7 +156,7 @@
             jax.ShapeDtypeStruct((slots, heads, HD), jnp.float32),
             jax.ShapeDtypeStruct((slots, heads, HD), jnp.bfloat16),
         ],
-        compiler_params=pltpu.CompilerParams(vmem_limit_bytes=40 * 1024 * 1024),
+        compiler_params=pltpu.CompilerParams(vmem_limit_bytes=VMEM),
         name="attend",
     )(
         lengths,
@@ -104,6 +168,93 @@
         residual.reshape(slots, heads, HD),
         norm_gain.reshape(heads, HD),
     )
+
+
+def times(rows, weight):
+    return lax.dot_general(rows, weight, (((1,), (1,)), ((), ())), preferred_element_type=jnp.float32)
+
+
+def project_kernel(*refs):
+    *half_refs, gate_ref, up_ref, out_ref, gate_total, up_total = refs
+    step = pl.program_id(0)
+    units = gate_ref.shape[0]
+    rows = jnp.concatenate([ref[...] for ref in half_refs], axis=0)
+    gate, up = times(rows, gate_ref[...]), times(rows, up_ref[...])
+
+    @pl.when(step == 0)
+    def _():
+        gate_total[...] = gate
+        up_total[...] = up
+
+    @pl.when(step > 0)
+    def _():
+        gate_total[...] += gate
+        up_total[...] += up
+
+    @pl.when(step == pl.num_programs(0) - 1)
+    def _():
+        shape = out_ref.shape[:2] + (units,)
+        out_ref[:, :, :units] = gate_total[...].astype(jnp.bfloat16).reshape(shape)
+        out_ref[:, :, units:] = up_total[...].astype(jnp.bfloat16).reshape(shape)
+
+
+def project(blocks, gate_weight, up_weight, chunk):
+    cut, features = blocks[0][0].shape
+    units = gate_weight.shape[0]
+    count = len(blocks)
+    weights = pl.BlockSpec((units, chunk), lambda i: (0, i))
+    return pl.pallas_call(
+        project_kernel,
+        grid=(features // chunk,),
+        in_specs=[pl.BlockSpec((cut, chunk), lambda i: (0, i)) for _ in range(2 * count)]
+        + [weights, weights],
+        out_specs=pl.BlockSpec((count, 2 * cut, 2 * units), lambda i: (0, 0, 0)),
+        out_shape=jax.ShapeDtypeStruct((count, 2 * cut, 2 * units), jnp.bfloat16),
+        scratch_shapes=[pltpu.VMEM((count * 2 * cut, units), jnp.float32)] * 2,
+        compiler_params=pltpu.CompilerParams(vmem_limit_bytes=24 * 1024 * 1024),
+        cost_estimate=pl.CostEstimate(
+            flops=8 * count * cut * units * features,
+            bytes_accessed=4 * units * features,
+            transcendentals=0,
+        ),
+        name="project",
+    )(*[half for block in blocks for half in block], gate_weight, up_weight)
+
+
+def combine_kernel(side_ref, own_near, own_far, got_near, got_far, hidden_ref):
+    units = hidden_ref.shape[-1]
+    even = side_ref[0] == 0
+
+    def pick(near, far, third, second, first):
+        if third == FAR:
+            return far[0, second, first].astype(jnp.float32)
+        return near[NEAR.index(third), second, first].astype(jnp.float32)
+
+    for third in range(RING):
+        for second in range(RING):
+            for first in range(RING):
+                got = jnp.where(
+                    even,
+                    pick(got_near, got_far, first, third, second),
+                    pick(got_near, got_far, second, first, third),
+                )
+                both = pick(own_near, own_far, third, second, first) + got
+                gate, up = both[:, :units], both[:, units:]
+                hidden = gate / (1.0 + jnp.exp(-gate)) * up
+                hidden_ref[third, second, first] = hidden.astype(jnp.bfloat16)
+
+
+def combine(side, *halves):
+    rows, both = halves[0].shape[-2:]
+    return pl.pallas_call(
+        combine_kernel,
+        in_specs=[pl.BlockSpec(memory_space=pltpu.SMEM)]
+        + [pl.BlockSpec(memory_space=pltpu.VMEM) for _ in halves],
+        out_specs=pl.BlockSpec(memory_space=pltpu.VMEM),
+        out_shape=jax.ShapeDtypeStruct((RING, RING, RING, rows, both // 2), jnp.bfloat16),
+        compiler_params=pltpu.CompilerParams(vmem_limit_bytes=24 * 1024 * 1024),
+        name="combine",
+    )(side, *halves)
 
 
 def body(
@@ -121,27 +272,56 @@
 ):
     slots, width = residual.shape
     half = gate_weight.shape[0]
+    hidden_units = gate_weight.shape[1]
+    rows = 2 * slots
+    side = lax.axis_index("side")
     mid, normed = attend(
         query, new_key, new_value, key_cache, value_cache, lengths, residual, norm_gain
     )
     pair = lax.all_to_all(
         normed.reshape(slots, 2, half), "side", split_axis=1, concat_axis=0, tiled=True
-    ).reshape(2 * slots, half)
-    rows_all = lax.all_gather(pair, "gx", axis=0, tiled=True)
-    gate_part = jnp.dot(rows_all, gate_weight, preferred_element_type=jnp.float32)
-    up_part = jnp.dot(rows_all, up_weight, preferred_element_type=jnp.float32)
-    gate_part, up_part = gate_part.astype(jnp.bfloat16), up_part.astype(jnp.bfloat16)
-    gate = gate_part.astype(jnp.float32) + lax.ppermute(gate_part, "side", SWAP).astype(jnp.float32)
-    up = up_part.astype(jnp.float32) + lax.ppermute(up_part, "side", SWAP).astype(jnp.float32)
-    hidden = (jax.nn.silu(gate) * up).astype(jnp.bfloat16)
-    partial = jnp.dot(hidden, down_weight, preferred_element_type=jnp.float32).astype(jnp.bfloat16)
-    blocks = lax.all_to_all(
-        partial.reshape(-1, 2 * slots, half), "gx", split_axis=0, concat_axis=0, tiled=True
+    ).reshape(rows, half)
+
+    near = jnp.concatenate(gather_line(pair, "first"), axis=0)
+    planes = gather_line(near, "second")
+    top, bottom = jnp.concatenate(planes[:2], axis=0), jnp.concatenate(planes[2:], axis=0)
+    blocks = gather_ring(top, bottom, "third")
+
+    near = project([blocks[third] for third in NEAR], gate_weight.T, up_weight.T, half // 8)
+    far = [behind(run, near) for run in blocks[FAR]]
+    far = project([far], gate_weight.T, up_weight.T, half // 4)
+    halves = [near, far, lax.ppermute(near, "side", SWAP), lax.ppermute(far, "side", SWAP)]
+    hidden = combine(
+        side.reshape(1), *[h.reshape(-1, RING, RING, rows, 2 * hidden_units) for h in halves]
     )
-    summed = jnp.sum(blocks.astype(jnp.float32), axis=0).astype(jnp.bfloat16)
-    ffn = lax.all_to_all(
-        summed.reshape(2, slots, half), "side", split_axis=0, concat_axis=2, tiled=True
-    ).reshape(slots, width)
+
+    cut = RING * RING * rows // 2
+    runs = [hidden[third].reshape(2, cut, hidden_units) for third in range(RING)]
+
+    def down(run):
+        return dot(run.reshape(-1, hidden_units), down_weight).astype(jnp.bfloat16)
+
+    part_far = down(runs[FAR])
+    after, before = send(part_far[:cut], "third", 1), send(part_far[cut:], "third", 3)
+    one_bottom = send(down(behind(runs[1][1], part_far)), "third", 1)
+    three_top = send(down(behind(runs[3][0], part_far)), "third", 3)
+    one_top = down(behind(runs[1][0], part_far))
+    three_bottom = down(behind(runs[3][1], part_far))
+    part_own = down(behind(runs[0], part_far))
+    one_top = send(add(one_top, after), "third", 1)
+    three_bottom = send(add(three_bottom, before), "third", 3)
+    summed = [
+        add(part_own[:cut], one_top, three_top),
+        add(part_own[cut:], one_bottom, three_bottom),
+    ]
+    summed = [run for part in summed for run in (part[: cut // 2], part[cut // 2 :])]
+    summed = reduce_line(summed, "second")
+    summed = reduce_line(parts(summed), "first")
+
+    by_side = summed.reshape(2, slots, half)
+    kept = lax.dynamic_index_in_dim(by_side, side, 0, keepdims=False)
+    got = lax.ppermute(lax.dynamic_index_in_dim(by_side, 1 - side, 0, keepdims=False), "side", SWAP)
+    ffn = jnp.concatenate([jnp.where(side == 0, kept, got), jnp.where(side == 0, got, kept)], axis=1)
     return (mid.reshape(slots, width) + ffn.astype(jnp.float32)).astype(jnp.bfloat16)
 
 

time: 254 us -> 173 us (0.68)
  blocking collectives: 115 us -> 4.9 us
  starting transfers between devices: 0.87 us -> 36.3 us
  Pallas kernels: 6.26 us -> 27.4 us
  between operations: 13.5 us -> 0.27 us
  matrix products: 18.2 us -> 5.43 us
  waiting for transfers between devices: 83.5 us -> 87.4 us
  other arithmetic: 5.64 us -> 2.26 us
    all_to_all x2 -> x0, blocking collectives: 110 us -> none  [the longest x1 104 us: body(): lax.all_to_all(partial.reshape(-1, 2 * slots, half), 'gx', split_axis=0,...]
    ppermute x2 -> x27, waiting for transfers between devices: 2.44 us -> 87.4 us  [the longest x12 46.3 us: send(): return lax.ppermute(array, ('side', 'gx'), hops(line, distance))]
    all_gather x1 -> x0, waiting for transfers between devices: 81 us -> none  [body(): rows_all = lax.all_gather(pair, 'gx', axis=0, tiled=True)]
    ppermute x2 -> x27, starting transfers between devices: 0.86 us -> 36.3 us  [the longest x12 16.8 us: fetch(): lax.ppermute(array, ('side', 'gx'), [(there, here) for here, there in hop...]
    pallas_call x0 -> x3, Pallas kernels: none -> 18.2 us  [the longest x2 15.9 us: project(): pl.pallas_call(project_kernel, grid=(features // chunk,), in_specs=[pl.Bl...]
    dot_general x3 -> x6, matrix products: 18.2 us -> 5.43 us  [dot(): return jnp.dot(left, right, preferred_element_type=jnp.float32)]
    reduce_sum x1 -> x0, other arithmetic: 4.8 us -> none  [body(): summed = jnp.sum(blocks.astype(jnp.float32), axis=0).astype(jnp.bfloat16)]
    unnamed x16 -> x17, local copies, waits for them, and re-layouts: 8.92 us -> 5.42 us
  transfers between devices with their start and end apart: 3 -> 27, of which waited for: 2 -> 20; matrix products, arithmetic and copies ran while one was open for 2% -> 3% of each run, Pallas kernels for 0% -> 9%
where the time goes in v2:
time: 173 us; the launch traced here: 172 us
  waiting for transfers between devices  87.4 us (51%)
  starting transfers between devices  36.3 us (21%)
  Pallas kernels  27.4 us (16%)
  local copies, waits for them, and re-layouts  8.26 us (5%)
  matrix products  5.43 us (3%)
  blocking collectives  4.9 us (3%)
  other arithmetic  2.26 us (1%)
    ppermute x12, waiting for transfers between devices, send(): return lax.ppermute(array, ('side', 'gx'), hops(line, distance))  46.3 us
    ppermute x12, waiting for transfers between devices, fetch(): lax.ppermute(array, ('side', 'gx'), [(there, here) for here, there in hop...  38.3 us
    ppermute x12, starting transfers between devices, fetch(): lax.ppermute(array, ('side', 'gx'), [(there, here) for here, there in hop...  16.8 us
    pallas_call x2, Pallas kernels, project(): pl.pallas_call(project_kernel, grid=(features // chunk,), in_specs=[pl.Bl...  15.9 us
    ppermute x12, starting transfers between devices, send(): return lax.ppermute(array, ('side', 'gx'), hops(line, distance))  12.1 us
    pallas_call x1, Pallas kernels, attend(): pl.pallas_call(attend_kernel, grid=(slots // per_step,), in_specs=[pl.Blo...  9.21 us
    dot_general x6, matrix products, dot(): return jnp.dot(left, right, preferred_element_type=jnp.float32)  5.43 us
    unnamed x17, local copies, waits for them, and re-layouts  5.42 us
  transfers between devices with their start and end apart: 27, of which 20 were waited for; matrix products, arithmetic and copies ran while one was open for 3% of the time, Pallas kernels for 9%

profile of v2, /device:TPU:1, one launch (start us, length us, event | category | flops | bytes accessed | tf_op | source)
XLA Modules:
  0.0 172.2 jit_solution(8096797670523429897)
XLA Ops:
  1.6 1.7 copy.23
  4.6 9.2 %attend.1 = (f32[8,64,128]{2,1,0:T(8,128)}, bf16[8,64,128]{2,1,0:T(8,128)(2,1)}) custom-call(s32[8]{0:T(128)} %lengths_ref.1, bf16[8,64,128]{2,1,0:T(8,128)(2,1)} %bitcast.75, bf16[8,8,128]{2,1,0:T(8,128)(2,1)} %get-tuple-element.41.new_key_ref, bf16[8,8,128]{2,1,0:T(8,128)(2,1)} %get-tuple-element.40.new_value_ref, bf16[8,384,1024]{2,1,0:T(8,128)(2,1)} %key_ref.1, ...), custom_call_target="tpu_custom_call" | custom-call | tf_op jit(solution)/shard_map/attend/pallas_call | solution.py:141
  14.9 4.9 %all_to_all.15 = bf16[8,2,4096]{2,0,1:T(8,128)(2,1)S(1)} all-to-all(bf16[8,2,4096]{2,0,1:T(8,128)(2,1)S(1)} %copy.12), channel_id=1, replica_groups=mesh['side'=2,'gx'=64] {'side'}, dimensions={1} | all-to-all | bytes 262144 | tf_op jit(solution)/shard_map/all_to_all | solution.py:281
  19.8 3.8 %collective-permute-start = (bf16[16,4096]{1,0:T(8,128)(2,1)S(1)}, bf16[16,4096]{1,0:T(8,128)(2,1)S(1)}, u32[]{:S(2)}, u32[]{:S(2)}) collective-permute-start(bf16[16,4096]{1,0:T(8,128)(2,1)S(1)} %bitcast.66), channel_id=1, source_target_pairs={{4,0},{5,1},{6,2},{7,3},{8,4},{9,5},{10,6},{11,7},{12,8},{13,9},{1... | collective-permute-start | bytes 393224 | tf_op jit(solution)/shard_map/ppermute | solution.py:39
  24.3 2.6 %collective-permute-done = bf16[16,4096]{1,0:T(8,128)(2,1)S(1)} collective-permute-done((bf16[16,4096]{1,0:T(8,128)(2,1)S(1)}, bf16[16,4096]{1,0:T(8,128)(2,1)S(1)}, u32[]{:S(2)}, u32[]{:S(2)}) %collective-permute-start) | collective-permute-done | bytes 131104 | tf_op jit(solution)/shard_map/ppermute | solution.py:39
  26.9 2.1 %collective-permute-done.1 = bf16[16,4096]{1,0:T(8,128)(2,1)S(1)} collective-permute-done((bf16[16,4096]{1,0:T(8,128)(2,1)S(1)}, bf16[16,4096]{1,0:T(8,128)(2,1)S(1)}, u32[]{:S(2)}, u32[]{:S(2)}) %collective-permute-start.1) | collective-permute-done | bytes 131104 | tf_op jit(solution)/shard_map/ppermute | solution.py:39
  30.4 2.8 %collective-permute-start.3 = (bf16[64,4096]{1,0:T(8,128)(2,1)S(1)}, bf16[64,4096]{1,0:T(8,128)(2,1)S(1)}, u32[]{:S(2)}, u32[]{:S(2)}) collective-permute-start(bf16[64,4096]{1,0:T(8,128)(2,1)S(1)} %pad_maximum_fusion), channel_id=1, source_target_pairs={{16,0},{17,1},{18,2},{19,3},{20,4},{21,5},{22,6},{23,7},{24,8},{25... | collective-permute-start | bytes 1572872 | tf_op jit(solution)/shard_map/ppermute | solution.py:39
  34.3 10.7 %collective-permute-done.3 = bf16[64,4096]{1,0:T(8,128)(2,1)S(1)} collective-permute-done((bf16[64,4096]{1,0:T(8,128)(2,1)S(1)}, bf16[64,4096]{1,0:T(8,128)(2,1)S(1)}, u32[]{:S(2)}, u32[]{:S(2)}) %collective-permute-start.3) | collective-permute-done | bytes 524320 | tf_op jit(solution)/shard_map/ppermute | solution.py:39
  45.0 2.3 %collective-permute-start.6 = (bf16[128,4096]{1,0:T(8,128)(2,1)S(1)}, bf16[128,4096]{1,0:T(8,128)(2,1)S(1)}, u32[]{:S(2)}, u32[]{:S(2)}) collective-permute-start(bf16[128,4096]{1,0:T(8,128)(2,1)S(1)} %constant_dynamic-update-slice_fusion.refs_0_), channel_id=1, source_target_pairs={{1,0},{2,1},{3,2},{0,3},{5,4},{6,5},{7,6},{4,7},{9,8},{10,9},{11,1... | collective-permute-start | bytes 3145736 | tf_op jit(solution)/shard_map/ppermute | solution.py:39
  49.7 1.8 %collective-permute-start.7 = (bf16[128,4096]{1,0:T(8,128)(2,1)S(1)}, bf16[128,4096]{1,0:T(8,128)(2,1)S(1)}, u32[]{:S(2)}, u32[]{:S(2)}) collective-permute-start(bf16[128,4096]{1,0:T(8,128)(2,1)S(1)} %constant_dynamic-update-slice_fusion.5.refs_1_), channel_id=1, source_target_pairs={{1,0},{2,1},{3,2},{0,3},{5,4},{6,5},{7,6},{4,7},{9,8},{10,9},{11,1... | collective-permute-start | bytes 3145736 | tf_op jit(solution)/shard_map/ppermute | solution.py:39
  51.4 7.6 %collective-permute-done.6.refs_2_ = bf16[128,4096]{1,0:T(8,128)(2,1)S(1)} collective-permute-done((bf16[128,4096]{1,0:T(8,128)(2,1)S(1)}, bf16[128,4096]{1,0:T(8,128)(2,1)S(1)}, u32[]{:S(2)}, u32[]{:S(2)}) %collective-permute-start.6) | collective-permute-done | bytes 1048608 | tf_op jit(solution)/shard_map/ppermute | solution.py:39
  59.0 3.4 %collective-permute-start.10 = (bf16[128,4096]{1,0:T(8,128)(2,1)S(1)}, bf16[128,4096]{1,0:T(8,128)(2,1)S(1)}, u32[]{:S(2)}, u32[]{:S(2)}) collective-permute-start(bf16[128,4096]{1,0:T(8,128)(2,1)S(1)} %collective-permute-done.6.refs_2_), channel_id=1, source_target_pairs={{1,0},{2,1},{3,2},{0,3},{5,4},{6,5},{7,6},{4,7},{9,8},{10,9},{11,1... | collective-permute-start | bytes 3145736 | tf_op jit(solution)/shard_map/ppermute | solution.py:39
  63.9 6.3 %collective-permute-done.7.refs_3_ = bf16[128,4096]{1,0:T(8,128)(2,1)S(1)} collective-permute-done((bf16[128,4096]{1,0:T(8,128)(2,1)S(1)}, bf16[128,4096]{1,0:T(8,128)(2,1)S(1)}, u32[]{:S(2)}, u32[]{:S(2)}) %collective-permute-start.7) | collective-permute-done | bytes 1048608 | tf_op jit(solution)/shard_map/ppermute | solution.py:39
  70.2 4.9 %collective-permute-done.8.refs_4_ = bf16[128,4096]{1,0:T(8,128)(2,1)S(1)} collective-permute-done((bf16[128,4096]{1,0:T(8,128)(2,1)S(1)}, bf16[128,4096]{1,0:T(8,128)(2,1)S(1)}, u32[]{:S(2)}, u32[]{:S(2)}) %collective-permute-start.8) | collective-permute-done | bytes 1048608 | tf_op jit(solution)/shard_map/ppermute | solution.py:39
  75.2 2.0 %copy-done.1 = bf16[4096,448]{0,1:T(8,128)(2,1)S(1)} copy-done((bf16[4096,448]{0,1:T(8,128)(2,1)S(1)}, bf16[4096,448]{0,1:T(8,128)(2,1)}, u32[]{:S(2)}) %copy-start.1) | copy-done | bytes 3670040
  77.2 11.8 %project.2 = bf16[3,256,896]{2,1,0:T(8,128)(2,1)S(1)} custom-call(bf16[128,4096]{1,0:T(8,128)(2,1)S(1)} %constant_dynamic-update-slice_fusion.refs_0_, bf16[128,4096]{1,0:T(8,128)(2,1)S(1)} %constant_dynamic-update-slice_fusion.5.refs_1_, bf16[128,4096]{1,0:T(8,128)(2,1)S(1)} %collective-permute-done.6.refs_2_, ...), custom_call_target="tpu_custom_call" | custom-call | flops 5637144576 | bytes 7340032 | tf_op jit(solution)/shard_map/project/pallas_call | solution.py:206
  89.0 3.3 %collective-permute-start.12 = (bf16[3,256,896]{2,1,0:T(8,128)(2,1)S(1)}, bf16[3,256,896]{2,1,0:T(8,128)(2,1)S(1)}, u32[]{:S(2)}, u32[]{:S(2)}) collective-permute-start(bf16[3,256,896]{2,1,0:T(8,128)(2,1)S(1)} %project.2), channel_id=1, source_target_pairs={{0,64},{64,0},{1,65},{65,1},{2,66},{66,2},{3,67},{67,3},{4,68},{68... | collective-permute-start | bytes 4128776 | tf_op jit(solution)/shard_map/ppermute | solution.py:293
  92.3 4.1 %project.3 = bf16[1,256,896]{2,1,0:T(8,128)(2,1)S(1)} custom-call(bf16[128,4096]{1,0:T(8,128)(2,1)S(1)} %collective-permute-done.10.refs_0_, bf16[128,4096]{1,0:T(8,128)(2,1)S(1)} %collective-permute-done.11.refs_1_, bf16[448,4096]{1,0:T(8,128)(2,1)S(1)} %bitcast.60, bf16[448,4096]{1,0:T(8,128)(2,1)S(1)} %bitcast.62), custom_call_target="tpu_custom_call" | custom-call | flops 1879048192 | bytes 7340032 | tf_op jit(solution)/shard_map/project/pallas_call | solution.py:206
  96.5 1.9 %collective-permute-done.13 = bf16[1,256,896]{2,1,0:T(8,128)(2,1)} collective-permute-done((bf16[1,256,896]{2,1,0:T(8,128)(2,1)S(1)}, bf16[1,256,896]{2,1,0:T(8,128)(2,1)}, u32[]{:S(2)}, u32[]{:S(2)}) %collective-permute-start.13) | collective-permute-done | bytes 458784 | tf_op jit(solution)/shard_map/ppermute | solution.py:293
  98.4 2.3 %combine.1 = bf16[4,4,4,16,448]{4,3,2,1,0:T(8,128)(2,1)S(1)} custom-call(s32[1]{0:T(128)} %bitcast.1.side_ref, bf16[3,4,4,16,896]{4,3,2,1,0:T(8,128)(2,1)S(1)} %bitcast.64, bf16[1,4,4,16,896]{4,3,2,1,0:T(8,128)(2,1)S(1)} %bitcast.63, bf16[3,4,4,16,896]{4,3,2,1,0:T(8,128)(2,1)S(1)} %bitcast.65, bf16[1,4,4,16,896]{4,3,2,1,0:T(8,128)(2,1)} %bitcast.12.got_far), custom_call_target="tpu_custom_call" | custom-call | tf_op jit(solution)/shard_map/combine/pallas_call | solution.py:249
  102.4 2.9 %collective-permute-start.19 = (bf16[128,4096]{1,0:T(8,128)(2,1)S(1)}, bf16[128,4096]{1,0:T(8,128)(2,1)S(1)}, u32[]{:S(2)}, u32[]{:S(2)}) collective-permute-start(bf16[128,4096]{1,0:T(8,128)(2,1)S(1)} %get-tuple-element.26), channel_id=1, source_target_pairs={{0,3},{1,0},{2,1},{3,2},{4,7},{5,4},{6,5},{7,6},{8,11},{9,8},{10,9... | collective-permute-start | bytes 3145736 | tf_op jit(solution)/shard_map/ppermute | solution.py:35
  108.4 9.1 %collective-permute-done.14 = bf16[128,4096]{1,0:T(8,128)(2,1)S(1)} collective-permute-done((bf16[128,4096]{1,0:T(8,128)(2,1)S(1)}, bf16[128,4096]{1,0:T(8,128)(2,1)S(1)}, u32[]{:S(2)}, u32[]{:S(2)}) %collective-permute-start.14) | collective-permute-done | bytes 1048608 | tf_op jit(solution)/shard_map/ppermute | solution.py:35
  119.1 2.7 %collective-permute-start.20 = (bf16[128,4096]{1,0:T(8,128)(2,1)S(1)}, bf16[128,4096]{1,0:T(8,128)(2,1)S(1)}, u32[]{:S(2)}, u32[]{:S(2)}) collective-permute-start(bf16[128,4096]{1,0:T(8,128)(2,1)S(1)} %add_convert_fusion.1), channel_id=1, source_target_pairs={{0,3},{1,0},{2,1},{3,2},{4,7},{5,4},{6,5},{7,6},{8,11},{9,8},{10,9... | collective-permute-start | bytes 3145736 | tf_op jit(solution)/shard_map/ppermute | solution.py:35
  123.1 5.2 %collective-permute-done.16 = bf16[128,4096]{1,0:T(8,128)(2,1)S(1)} collective-permute-done((bf16[128,4096]{1,0:T(8,128)(2,1)S(1)}, bf16[128,4096]{1,0:T(8,128)(2,1)S(1)}, u32[]{:S(2)}, u32[]{:S(2)}) %collective-permute-start.16) | collective-permute-done | bytes 1048608 | tf_op jit(solution)/shard_map/ppermute | solution.py:35
  128.7 11.2 %collective-permute-done.15 = bf16[128,4096]{1,0:T(8,128)(2,1)S(1)} collective-permute-done((bf16[128,4096]{1,0:T(8,128)(2,1)S(1)}, bf16[128,4096]{1,0:T(8,128)(2,1)S(1)}, u32[]{:S(2)}, u32[]{:S(2)}) %collective-permute-start.15) | collective-permute-done | bytes 1048608 | tf_op jit(solution)/shard_map/ppermute | solution.py:35
  141.1 1.6 collective-permute-start.22
  143.6 10.9 %collective-permute-done.22 = bf16[64,4096]{1,0:T(8,128)(2,1)S(1)} collective-permute-done((bf16[64,4096]{1,0:T(8,128)(2,1)S(1)}, bf16[64,4096]{1,0:T(8,128)(2,1)S(1)}, u32[]{:S(2)}, u32[]{:S(2)}) %collective-permute-start.22) | collective-permute-done | bytes 524320 | tf_op jit(solution)/shard_map/ppermute | solution.py:35
  154.5 3.6 %collective-permute-done.17 = bf16[64,4096]{1,0:T(8,128)(2,1)S(1)} collective-permute-done((bf16[64,4096]{1,0:T(8,128)(2,1)S(1)}, bf16[64,4096]{1,0:T(8,128)(2,1)S(1)}, u32[]{:S(2)}, u32[]{:S(2)}) %collective-permute-start.17) | collective-permute-done | bytes 524320 | tf_op jit(solution)/shard_map/ppermute | solution.py:35
  158.4 1.7 collective-permute-start.25
  160.7 2.6 %collective-permute-done.25 = bf16[16,4096]{1,0:T(8,128)(2,1)S(1)} collective-permute-done((bf16[16,4096]{1,0:T(8,128)(2,1)S(1)}, bf16[16,4096]{1,0:T(8,128)(2,1)S(1)}, u32[]{:S(2)}, u32[]{:S(2)}) %collective-permute-start.25) | collective-permute-done | bytes 131104 | tf_op jit(solution)/shard_map/ppermute | solution.py:35
  163.3 2.1 %collective-permute-done.24 = bf16[16,4096]{1,0:T(8,128)(2,1)S(1)} collective-permute-done((bf16[16,4096]{1,0:T(8,128)(2,1)S(1)}, bf16[16,4096]{1,0:T(8,128)(2,1)S(1)}, u32[]{:S(2)}, u32[]{:S(2)}) %collective-permute-start.24) | collective-permute-done | bytes 131104 | tf_op jit(solution)/shard_map/ppermute | solution.py:35
  166.6 3.9 %collective-permute-start.26 = (bf16[8,4096]{1,0:T(8,128)(2,1)S(1)}, bf16[8,4096]{1,0:T(8,128)(2,1)S(1)}, u32[]{:S(2)}, u32[]{:S(2)}) collective-permute-start(bf16[8,4096]{1,0:T(8,128)(2,1)S(1)} %dynamic-slice_bitcast_fusion), channel_id=1, source_target_pairs={{0,64},{64,0},{1,65},{65,1},{2,66},{66,2},{3,67},{67,3},{4,68},{68... | collective-permute-start | bytes 196616 | tf_op jit(solution)/shard_map/ppermute | solution.py:323
  (68 shorter events, 24.8 us)
Async XLA Ops:
  19.8 7.2 %collective-permute-start = (bf16[16,4096]{1,0:T(8,128)(2,1)S(1)}, bf16[16,4096]{1,0:T(8,128)(2,1)S(1)}, u32[]{:S(2)}, u32[]{:S(2)}) collective-permute-start(bf16[16,4096]{1,0:T(8,128)(2,1)S(1)} %bitcast.66), channel_id=1, source_target_pairs={{4,0},{5,1},{6,2},{7,3},{8,4},{9,5},{10,6},{11,7},{12,8},{13,9},{1... | collective-permute-start | bytes 393224 | tf_op jit(solution)/shard_map/ppermute | solution.py:39
  23.6 5.4 %collective-permute-start.1 = (bf16[16,4096]{1,0:T(8,128)(2,1)S(1)}, bf16[16,4096]{1,0:T(8,128)(2,1)S(1)}, u32[]{:S(2)}, u32[]{:S(2)}) collective-permute-start(bf16[16,4096]{1,0:T(8,128)(2,1)S(1)} %bitcast.67), channel_id=1, source_target_pairs={{8,0},{9,1},{10,2},{11,3},{12,4},{13,5},{14,6},{15,7},{0,8},{1,9},... | collective-permute-start | bytes 393224 | tf_op jit(solution)/shard_map/ppermute | solution.py:39
  23.6 6.7 %collective-permute-start.2 = (bf16[16,4096]{1,0:T(8,128)(2,1)S(1)}, bf16[16,4096]{1,0:T(8,128)(2,1)S(1)}, u32[]{:S(2)}, u32[]{:S(2)}) collective-permute-start(bf16[16,4096]{1,0:T(8,128)(2,1)S(1)} %bitcast.68), channel_id=1, source_target_pairs={{12,0},{13,1},{14,2},{15,3},{0,4},{1,5},{2,6},{3,7},{4,8},{5,9},{6... | collective-permute-start | bytes 393224 | tf_op jit(solution)/shard_map/ppermute | solution.py:39
  30.4 44.8 %copy-start = (bf16[4096,448]{0,1:T(8,128)(2,1)S(1)}, bf16[4096,448]{0,1:T(8,128)(2,1)}, u32[]{:S(2)}) copy-start(bf16[4096,448]{0,1:T(8,128)(2,1)} %param.19) | copy-start | bytes 11010052
  30.4 14.5 %collective-permute-start.3 = (bf16[64,4096]{1,0:T(8,128)(2,1)S(1)}, bf16[64,4096]{1,0:T(8,128)(2,1)S(1)}, u32[]{:S(2)}, u32[]{:S(2)}) collective-permute-start(bf16[64,4096]{1,0:T(8,128)(2,1)S(1)} %pad_maximum_fusion), channel_id=1, source_target_pairs={{16,0},{17,1},{18,2},{19,3},{20,4},{21,5},{22,6},{23,7},{24,8},{25... | collective-permute-start | bytes 1572872 | tf_op jit(solution)/shard_map/ppermute | solution.py:39
  33.2 14.0 %collective-permute-start.4 = (bf16[64,4096]{1,0:T(8,128)(2,1)S(1)}, bf16[64,4096]{1,0:T(8,128)(2,1)S(1)}, u32[]{:S(2)}, u32[]{:S(2)}) collective-permute-start(bf16[64,4096]{1,0:T(8,128)(2,1)S(1)} %pad_maximum_fusion), channel_id=1, source_target_pairs={{32,0},{33,1},{34,2},{35,3},{36,4},{37,5},{38,6},{39,7},{40,8},{41... | collective-permute-start | bytes 1572872 | tf_op jit(solution)/shard_map/ppermute | solution.py:39
  33.6 15.1 %collective-permute-start.5 = (bf16[64,4096]{1,0:T(8,128)(2,1)S(1)}, bf16[64,4096]{1,0:T(8,128)(2,1)S(1)}, u32[]{:S(2)}, u32[]{:S(2)}) collective-permute-start(bf16[64,4096]{1,0:T(8,128)(2,1)S(1)} %pad_maximum_fusion), channel_id=1, source_target_pairs={{48,0},{49,1},{50,2},{51,3},{52,4},{53,5},{54,6},{55,7},{56,8},{57... | collective-permute-start | bytes 1572872 | tf_op jit(solution)/shard_map/ppermute | solution.py:39
  45.0 14.0 %collective-permute-start.6 = (bf16[128,4096]{1,0:T(8,128)(2,1)S(1)}, bf16[128,4096]{1,0:T(8,128)(2,1)S(1)}, u32[]{:S(2)}, u32[]{:S(2)}) collective-permute-start(bf16[128,4096]{1,0:T(8,128)(2,1)S(1)} %constant_dynamic-update-slice_fusion.refs_0_), channel_id=1, source_target_pairs={{1,0},{2,1},{3,2},{0,3},{5,4},{6,5},{7,6},{4,7},{9,8},{10,9},{11,1... | collective-permute-start | bytes 3145736 | tf_op jit(solution)/shard_map/ppermute | solution.py:39
  48.7 15.2 %collective-permute-start.9 = (bf16[128,4096]{1,0:T(8,128)(2,1)S(1)}, bf16[128,4096]{1,0:T(8,128)(2,1)S(1)}, u32[]{:S(2)}, u32[]{:S(2)}) collective-permute-start(bf16[128,4096]{1,0:T(8,128)(2,1)S(1)} %constant_dynamic-update-slice_fusion.5.refs_1_), channel_id=1, source_target_pairs={{3,0},{0,1},{1,2},{2,3},{7,4},{4,5},{5,6},{6,7},{11,8},{8,9},{9,10... | collective-permute-start | bytes 3145736 | tf_op jit(solution)/shard_map/ppermute | solution.py:39
  49.7 20.6 %collective-permute-start.7 = (bf16[128,4096]{1,0:T(8,128)(2,1)S(1)}, bf16[128,4096]{1,0:T(8,128)(2,1)S(1)}, u32[]{:S(2)}, u32[]{:S(2)}) collective-permute-start(bf16[128,4096]{1,0:T(8,128)(2,1)S(1)} %constant_dynamic-update-slice_fusion.5.refs_1_), channel_id=1, source_target_pairs={{1,0},{2,1},{3,2},{0,3},{5,4},{6,5},{7,6},{4,7},{9,8},{10,9},{11,1... | collective-permute-start | bytes 3145736 | tf_op jit(solution)/shard_map/ppermute | solution.py:39
  51.4 23.7 %collective-permute-start.8 = (bf16[128,4096]{1,0:T(8,128)(2,1)S(1)}, bf16[128,4096]{1,0:T(8,128)(2,1)S(1)}, u32[]{:S(2)}, u32[]{:S(2)}) collective-permute-start(bf16[128,4096]{1,0:T(8,128)(2,1)S(1)} %constant_dynamic-update-slice_fusion.refs_0_), channel_id=1, source_target_pairs={{3,0},{0,1},{1,2},{2,3},{7,4},{4,5},{5,6},{6,7},{11,8},{8,9},{9,10... | collective-permute-start | bytes 3145736 | tf_op jit(solution)/shard_map/ppermute | solution.py:39
  59.0 33.3 %collective-permute-start.10 = (bf16[128,4096]{1,0:T(8,128)(2,1)S(1)}, bf16[128,4096]{1,0:T(8,128)(2,1)S(1)}, u32[]{:S(2)}, u32[]{:S(2)}) collective-permute-start(bf16[128,4096]{1,0:T(8,128)(2,1)S(1)} %collective-permute-done.6.refs_2_), channel_id=1, source_target_pairs={{1,0},{2,1},{3,2},{0,3},{5,4},{6,5},{7,6},{4,7},{9,8},{10,9},{11,1... | collective-permute-start | bytes 3145736 | tf_op jit(solution)/shard_map/ppermute | solution.py:39
  63.9 28.4 %collective-permute-start.11 = (bf16[128,4096]{1,0:T(8,128)(2,1)S(1)}, bf16[128,4096]{1,0:T(8,128)(2,1)S(1)}, u32[]{:S(2)}, u32[]{:S(2)}) collective-permute-start(bf16[128,4096]{1,0:T(8,128)(2,1)S(1)} %collective-permute-done.9.refs_5_), channel_id=1, source_target_pairs={{3,0},{0,1},{1,2},{2,3},{7,4},{4,5},{5,6},{6,7},{11,8},{8,9},{9,10... | collective-permute-start | bytes 3145736 | tf_op jit(solution)/shard_map/ppermute | solution.py:39
  75.2 2.0 %copy-start.1 = (bf16[4096,448]{0,1:T(8,128)(2,1)S(1)}, bf16[4096,448]{0,1:T(8,128)(2,1)}, u32[]{:S(2)}) copy-start(bf16[4096,448]{0,1:T(8,128)(2,1)} %param.20) | copy-start | bytes 11010052
  77.2 15.1 %copy-start.2 = (bf16[4096,448]{0,1:T(8,128)(2,1)S(1)}, bf16[4096,448]{0,1:T(8,128)(2,1)}, u32[]{:S(2)}) copy-start(bf16[4096,448]{0,1:T(8,128)(2,1)} %param.20) | copy-start | bytes 11010052
  89.0 7.6 %collective-permute-start.12 = (bf16[3,256,896]{2,1,0:T(8,128)(2,1)S(1)}, bf16[3,256,896]{2,1,0:T(8,128)(2,1)S(1)}, u32[]{:S(2)}, u32[]{:S(2)}) collective-permute-start(bf16[3,256,896]{2,1,0:T(8,128)(2,1)S(1)} %project.2), channel_id=1, source_target_pairs={{0,64},{64,0},{1,65},{65,1},{2,66},{66,2},{3,67},{67,3},{4,68},{68... | collective-permute-start | bytes 4128776 | tf_op jit(solution)/shard_map/ppermute | solution.py:293
  96.4 2.0 %collective-permute-start.13 = (bf16[1,256,896]{2,1,0:T(8,128)(2,1)S(1)}, bf16[1,256,896]{2,1,0:T(8,128)(2,1)}, u32[]{:S(2)}, u32[]{:S(2)}) collective-permute-start(bf16[1,256,896]{2,1,0:T(8,128)(2,1)S(1)} %project.3), channel_id=1, source_target_pairs={{0,64},{64,0},{1,65},{65,1},{2,66},{66,2},{3,67},{67,3},{4,68},{68... | collective-permute-start | bytes 1376264 | tf_op jit(solution)/shard_map/ppermute | solution.py:293
  98.4 2.4 %copy-start.3 = (bf16[448,4096]{1,0:T(8,128)(2,1)S(1)}, bf16[448,4096]{1,0:T(8,128)(2,1)}, u32[]{:S(2)}) copy-start(bf16[448,4096]{1,0:T(8,128)(2,1)} %param.21) | copy-start | bytes 11010052
  102.3 15.2 %collective-permute-start.14 = (bf16[128,4096]{1,0:T(8,128)(2,1)S(1)}, bf16[128,4096]{1,0:T(8,128)(2,1)S(1)}, u32[]{:S(2)}, u32[]{:S(2)}) collective-permute-start(bf16[128,4096]{1,0:T(8,128)(2,1)S(1)} %get-tuple-element.25), channel_id=1, source_target_pairs={{0,1},{1,2},{2,3},{3,0},{4,5},{5,6},{6,7},{7,4},{8,9},{9,10},{10,1... | collective-permute-start | bytes 3145736 | tf_op jit(solution)/shard_map/ppermute | solution.py:35
  102.4 15.9 %collective-permute-start.19 = (bf16[128,4096]{1,0:T(8,128)(2,1)S(1)}, bf16[128,4096]{1,0:T(8,128)(2,1)S(1)}, u32[]{:S(2)}, u32[]{:S(2)}) collective-permute-start(bf16[128,4096]{1,0:T(8,128)(2,1)S(1)} %get-tuple-element.26), channel_id=1, source_target_pairs={{0,3},{1,0},{2,1},{3,2},{4,7},{5,4},{6,5},{7,6},{8,11},{9,8},{10,9... | collective-permute-start | bytes 3145736 | tf_op jit(solution)/shard_map/ppermute | solution.py:35
  106.1 22.3 %collective-permute-start.16 = (bf16[128,4096]{1,0:T(8,128)(2,1)S(1)}, bf16[128,4096]{1,0:T(8,128)(2,1)S(1)}, u32[]{:S(2)}, u32[]{:S(2)}) collective-permute-start(bf16[128,4096]{1,0:T(8,128)(2,1)S(1)} %convolution_convert_fusion.4), channel_id=1, source_target_pairs={{0,3},{1,0},{2,1},{3,2},{4,7},{5,4},{6,5},{7,6},{8,11},{9,8},{10,9... | collective-permute-start | bytes 3145736 | tf_op jit(solution)/shard_map/ppermute | solution.py:35
  106.9 21.9 %collective-permute-start.18 = (bf16[128,4096]{1,0:T(8,128)(2,1)S(1)}, bf16[128,4096]{1,0:T(8,128)(2,1)S(1)}, u32[]{:S(2)}, u32[]{:S(2)}) collective-permute-start(bf16[128,4096]{1,0:T(8,128)(2,1)S(1)} %convolution_convert_fusion.3), channel_id=1, source_target_pairs={{0,1},{1,2},{2,3},{3,0},{4,5},{5,6},{6,7},{7,4},{8,9},{9,10},{10,1... | collective-permute-start | bytes 3145736 | tf_op jit(solution)/shard_map/ppermute | solution.py:35
  118.2 21.8 %collective-permute-start.15 = (bf16[128,4096]{1,0:T(8,128)(2,1)S(1)}, bf16[128,4096]{1,0:T(8,128)(2,1)S(1)}, u32[]{:S(2)}, u32[]{:S(2)}) collective-permute-start(bf16[128,4096]{1,0:T(8,128)(2,1)S(1)} %add_convert_fusion.3), channel_id=1, source_target_pairs={{0,1},{1,2},{2,3},{3,0},{4,5},{5,6},{6,7},{7,4},{8,9},{9,10},{10,1... | collective-permute-start | bytes 3145736 | tf_op jit(solution)/shard_map/ppermute | solution.py:35
  119.1 20.9 %collective-permute-start.20 = (bf16[128,4096]{1,0:T(8,128)(2,1)S(1)}, bf16[128,4096]{1,0:T(8,128)(2,1)S(1)}, u32[]{:S(2)}, u32[]{:S(2)}) collective-permute-start(bf16[128,4096]{1,0:T(8,128)(2,1)S(1)} %add_convert_fusion.1), channel_id=1, source_target_pairs={{0,3},{1,0},{2,1},{3,2},{4,7},{5,4},{6,5},{7,6},{8,11},{9,8},{10,9... | collective-permute-start | bytes 3145736 | tf_op jit(solution)/shard_map/ppermute | solution.py:35
  141.1 13.3 %collective-permute-start.22 = (bf16[64,4096]{1,0:T(8,128)(2,1)S(1)}, bf16[64,4096]{1,0:T(8,128)(2,1)S(1)}, u32[]{:S(2)}, u32[]{:S(2)}) collective-permute-start(bf16[64,4096]{1,0:T(8,128)(2,1)S(1)} %get-tuple-element.32), channel_id=1, source_target_pairs={{0,48},{1,49},{2,50},{3,51},{4,52},{5,53},{6,54},{7,55},{8,56},{9,... | collective-permute-start | bytes 1572872 | tf_op jit(solution)/shard_map/ppermute | solution.py:35
  142.7 11.7 %collective-permute-start.21 = (bf16[64,4096]{1,0:T(8,128)(2,1)S(1)}, bf16[64,4096]{1,0:T(8,128)(2,1)S(1)}, u32[]{:S(2)}, u32[]{:S(2)}) collective-permute-start(bf16[64,4096]{1,0:T(8,128)(2,1)S(1)} %get-tuple-element.31), channel_id=1, source_target_pairs={{0,32},{1,33},{2,34},{3,35},{4,36},{5,37},{6,38},{7,39},{8,40},{9,... | collective-permute-start | bytes 1572872 | tf_op jit(solution)/shard_map/ppermute | solution.py:35
  142.8 28.6 %copy-start.4 = (f32[8,64,128]{2,1,0:T(8,128)S(1)}, f32[8,64,128]{2,1,0:T(8,128)}, u32[]{:S(2)}) copy-start(f32[8,64,128]{2,1,0:T(8,128)} %get-tuple-element.14) | copy-start | bytes 786436
  142.8 15.2 %collective-permute-start.17 = (bf16[64,4096]{1,0:T(8,128)(2,1)S(1)}, bf16[64,4096]{1,0:T(8,128)(2,1)S(1)}, u32[]{:S(2)}, u32[]{:S(2)}) collective-permute-start(bf16[64,4096]{1,0:T(8,128)(2,1)S(1)} %slice.89), channel_id=1, source_target_pairs={{0,16},{1,17},{2,18},{3,19},{4,20},{5,21},{6,22},{7,23},{8,24},{9,... | collective-permute-start | bytes 1572872 | tf_op jit(solution)/shard_map/ppermute | solution.py:35
  158.4 5.0 %collective-permute-start.25 = (bf16[16,4096]{1,0:T(8,128)(2,1)S(1)}, bf16[16,4096]{1,0:T(8,128)(2,1)S(1)}, u32[]{:S(2)}, u32[]{:S(2)}) collective-permute-start(bf16[16,4096]{1,0:T(8,128)(2,1)S(1)} %get-tuple-element.36), channel_id=1, source_target_pairs={{0,12},{1,13},{2,14},{3,15},{4,0},{5,1},{6,2},{7,3},{8,4},{9,5},{1... | collective-permute-start | bytes 393224 | tf_op jit(solution)/shard_map/ppermute | solution.py:35
  160.0 5.4 %collective-permute-start.24 = (bf16[16,4096]{1,0:T(8,128)(2,1)S(1)}, bf16[16,4096]{1,0:T(8,128)(2,1)S(1)}, u32[]{:S(2)}, u32[]{:S(2)}) collective-permute-start(bf16[16,4096]{1,0:T(8,128)(2,1)S(1)} %get-tuple-element.37), channel_id=1, source_target_pairs={{0,8},{1,9},{2,10},{3,11},{4,12},{5,13},{6,14},{7,15},{8,0},{9,1},... | collective-permute-start | bytes 393224 | tf_op jit(solution)/shard_map/ppermute | solution.py:35
  160.0 6.4 %collective-permute-start.23 = (bf16[16,4096]{1,0:T(8,128)(2,1)S(1)}, bf16[16,4096]{1,0:T(8,128)(2,1)S(1)}, u32[]{:S(2)}, u32[]{:S(2)}) collective-permute-start(bf16[16,4096]{1,0:T(8,128)(2,1)S(1)} %get-tuple-element.35), channel_id=1, source_target_pairs={{0,4},{1,5},{2,6},{3,7},{4,8},{5,9},{6,10},{7,11},{8,12},{9,13},{1... | collective-permute-start | bytes 393224 | tf_op jit(solution)/shard_map/ppermute | solution.py:35
  166.6 4.8 %collective-permute-start.26 = (bf16[8,4096]{1,0:T(8,128)(2,1)S(1)}, bf16[8,4096]{1,0:T(8,128)(2,1)S(1)}, u32[]{:S(2)}, u32[]{:S(2)}) collective-permute-start(bf16[8,4096]{1,0:T(8,128)(2,1)S(1)} %dynamic-slice_bitcast_fusion), channel_id=1, source_target_pairs={{0,64},{64,0},{1,65},{65,1},{2,66},{66,2},{3,67},{67,3},{4,68},{68... | collective-permute-start | bytes 196616 | tf_op jit(solution)/shard_map/ppermute | solution.py:323

commit v3 on v2

v3 whole, which is shorter than its diff:
```python
import functools

import jax
import jax.numpy as jnp
from jax import lax
from jax.experimental import pallas as pl
from jax.experimental.pallas import tpu as pltpu
from jax.sharding import PartitionSpec as P

HD = 128
SWAP = [(0, 1), (1, 0)]
RING = 4
VMEM = 60 * 1024 * 1024
TOGETHER = 4
FAR = 2
PLACE = {(0, 0): (0, 0), (0, 1): (0, 1), (1, 0): (1, 0), (3, 1): (1, 1), (1, 1): (2, 0), (3, 0): (2, 1)}
LINES = {"first": ("x", "z"), "second": ("z", "y"), "third": ("y", "x")}


def chip(z, x, y):
    return (z % RING) * RING * RING + (x % RING) * RING + y % RING


def hops(line, distance):
    pairs = []
    for side in range(2):
        dz, dx, dy = (distance * (axis == LINES[line][side]) for axis in "zxy")
        for z in range(RING):
            for x in range(RING):
                for y in range(RING):
                    here, there = chip(z, x, y), chip(z + dz, x + dx, y + dy)
                    pairs.append((side * RING**3 + here, side * RING**3 + there))
    return pairs


def send(array, line, distance):
    return lax.ppermute(array, ("side", "gx"), hops(line, distance))


def fetch(array, line, distance):
    return lax.ppermute(array, ("side", "gx"), [(there, here) for here, there in hops(line, distance)])


def gather_line(array, line):
    far = fetch(array, line, 2)
    return [array, fetch(array, line, 1), far, fetch(array, line, 3)]


def gather_ring(top, bottom, line):
    after_top, before_bottom = fetch(top, line, 1), fetch(bottom, line, 3)
    after_bottom, before_top = fetch(bottom, line, 1), fetch(top, line, 3)
    far = [fetch(after_top, line, 1), fetch(before_bottom, line, 3)]
    return [[top, bottom], [after_top, after_bottom], far, [before_top, before_bottom]]


def behind(array, *others):
    return lax.optimization_barrier((array, *others))[0]


def add(*arrays):
    return sum(array.astype(jnp.float32) for array in arrays).astype(jnp.bfloat16)


def reduce_line(blocks, line):
    far = send(blocks[2], line, 2)
    return add(blocks[0], send(blocks[1], line, 1), far, send(blocks[3], line, 3))


def parts(array):
    rows = array.shape[0] // RING
    return [array[i * rows : (i + 1) * rows] for i in range(RING)]


def dot(left, right):
    return jnp.dot(left, right, preferred_element_type=jnp.float32)


def attend_kernel(
    side_ref, lengths_ref, query_ref, new_key_ref, new_value_ref, residual_ref, gain_ref,
    key_cache, value_cache, mid_ref, own_ref, other_ref,
    key_ref, value_ref, copied, queries, keys_now, values_now,
):
    heads, slots, _ = query_ref.shape
    kv_heads = new_key_ref.shape[0]
    groups = heads // kv_heads
    ctx = key_ref.shape[1]
    scale = 1.0 / HD**0.5
    runs = [range(start, min(start + TOGETHER, slots)) for start in range(0, slots, TOGETHER)]

    def copy(kind, slot):
        cache, held = ((key_cache, key_ref), (value_cache, value_ref))[kind]
        return pltpu.make_async_copy(cache.at[slot], held.at[slot], copied.at[kind, slot])

    for run in runs:
        for kind in range(2):
            for slot in run:
                copy(kind, slot).start()
    queries[...] = query_ref[...].astype(jnp.float32)
    keys_now[...] = new_key_ref[...].astype(jnp.float32)
    values_now[...] = new_value_ref[...].astype(jnp.float32)

    def spread_heads(rows):
        return jnp.broadcast_to(rows[:, None, :], (kv_heads, groups, HD)).reshape(heads, HD)

    row_group = lax.broadcasted_iota(jnp.int32, (heads, kv_heads * HD), 0) // groups
    col_group = lax.broadcasted_iota(jnp.int32, (heads, kv_heads * HD), 1) // HD
    own = row_group == col_group
    places = lax.broadcasted_iota(jnp.int32, (heads, ctx), 1)
    for run in runs:
        query_of, scores_of, probs_of, new_of, total_of = {}, {}, {}, {}, {}
        for slot in run:
            copy(0, slot).wait()
        for slot in run:
            query_of[slot] = queries[:, slot, :]
            wide = jnp.where(own, jnp.concatenate([query_of[slot]] * kv_heads, axis=1), 0)
            scores_of[slot] = lax.dot_general(
                wide.astype(jnp.bfloat16),
                key_ref[slot],
                (((1,), (1,)), ((), ())),
                preferred_element_type=jnp.float32,
            )
        for slot in run:
            scores = jnp.where(places < lengths_ref[slot], scores_of[slot] * scale, -jnp.inf)
            key_now = spread_heads(keys_now[:, slot, :])
            score_new = jnp.sum(query_of[slot] * key_now, axis=1, keepdims=True) * scale
            peak = jnp.maximum(jnp.max(scores, axis=1, keepdims=True), score_new)
            probs = jnp.exp(scores - peak)
            prob_new = jnp.exp(score_new - peak)
            total_of[slot] = jnp.sum(probs, axis=1, keepdims=True) + prob_new
            probs_of[slot] = probs.astype(jnp.bfloat16)
            new_of[slot] = prob_new.astype(jnp.bfloat16).astype(jnp.float32)
        for slot in run:
            copy(1, slot).wait()
        for slot in run:
            value_now = spread_heads(values_now[:, slot, :])
            spread = jnp.dot(probs_of[slot], value_ref[slot], preferred_element_type=jnp.float32)
            picked = jnp.concatenate(
                [
                    spread[g * groups : (g + 1) * groups, g * HD : (g + 1) * HD]
                    for g in range(kv_heads)
                ],
                axis=0,
            )
            summed = picked + new_of[slot] * value_now
            mid_ref[:, slot, :] = summed / total_of[slot]

    mid = residual_ref[...] + mid_ref[...]
    mid_ref[...] = mid
    squares = jnp.sum(jnp.sum(mid * mid, axis=0, keepdims=True), axis=2, keepdims=True)
    mean_sq = squares / (heads * HD)
    normed = (mid * lax.rsqrt(mean_sq + 1e-05) * gain_ref[...]).astype(jnp.bfloat16)
    halves = normed[: heads // 2], normed[heads // 2 :]
    even = side_ref[0] == 0
    own_ref[...] = jnp.where(even, halves[0], halves[1])
    other_ref[...] = jnp.where(even, halves[1], halves[0])


def attend(side, query, new_key, new_value, key_cache, value_cache, lengths, residual, norm_gain):
    slots, width = query.shape
    heads = width // HD

    def by_head(array):
        return array.reshape(slots, -1, HD).transpose(1, 0, 2)

    smem, vmem = (pl.BlockSpec(memory_space=space) for space in (pltpu.SMEM, pltpu.VMEM))
    kv_shape = (new_key.shape[1] // HD, slots, HD)
    half = jax.ShapeDtypeStruct((heads // 2, slots, HD), jnp.bfloat16)
    return pl.pallas_call(
        attend_kernel,
        in_specs=[smem, smem] + [vmem] * 5 + [pl.BlockSpec(memory_space=pl.ANY)] * 2,
        out_specs=[vmem] * 3,
        out_shape=[jax.ShapeDtypeStruct((heads, slots, HD), jnp.float32), half, half],
        scratch_shapes=[
            pltpu.VMEM(key_cache.shape, jnp.bfloat16),
            pltpu.VMEM(value_cache.shape, jnp.bfloat16),
            pltpu.SemaphoreType.DMA((2, slots)),
            pltpu.VMEM((heads, slots, HD), jnp.float32),
            pltpu.VMEM(kv_shape, jnp.float32),
            pltpu.VMEM(kv_shape, jnp.float32),
        ],
        compiler_params=pltpu.CompilerParams(vmem_limit_bytes=VMEM),
        name="attend",
    )(
        side.reshape(1),
        lengths,
        by_head(query),
        by_head(new_key),
        by_head(new_value),
        by_head(residual),
        norm_gain.reshape(heads, 1, HD),
        key_cache,
        value_cache,
    )


def times(rows, weight):
    return lax.dot_general(rows, weight, (((1,), (1,)), ((), ())), preferred_element_type=jnp.float32)


def project_kernel(*refs):
    top_ref, bottom_ref, gate_ref, up_ref, out_ref = refs[-5:]
    units = gate_ref.shape[0]
    shape = out_ref.shape[1:3] + (units,)
    rows = jnp.concatenate([top_ref[...], bottom_ref[...]], axis=0)
    out_ref[0, :, :, :units] = times(rows, gate_ref[...]).astype(jnp.bfloat16).reshape(shape)
    out_ref[0, :, :, units:] = times(rows, up_ref[...]).astype(jnp.bfloat16).reshape(shape)


def project(found, place, count, halves, gate_weight, up_weight):
    cut, features = halves[0].shape
    units = gate_weight.shape[0]
    vmem = pl.BlockSpec(memory_space=pltpu.VMEM)
    earlier = [] if found is None else [found]
    return pl.pallas_call(
        project_kernel,
        grid=(1,),
        in_specs=[pl.BlockSpec(memory_space=pl.ANY) for _ in earlier] + [vmem] * 4,
        out_specs=pl.BlockSpec((1, 2, cut, 2 * units), lambda i: (place, 0, 0, 0)),
        out_shape=jax.ShapeDtypeStruct((count, 2, cut, 2 * units), jnp.bfloat16),
        input_output_aliases={0: 0} if earlier else {},
        compiler_params=pltpu.CompilerParams(vmem_limit_bytes=24 * 1024 * 1024),
        cost_estimate=pl.CostEstimate(
            flops=8 * cut * units * features, bytes_accessed=4 * units * features, transcendentals=0
        ),
        name="project",
    )(*earlier, *halves, gate_weight, up_weight)


def combine_kernel(side_ref, own_near, own_far, got_near, got_far, hidden_ref):
    units = hidden_ref.shape[-1]
    even = side_ref[0] == 0

    def pick(near, far, third, second, first):
        half, inner = divmod(second, RING // 2)
        if third == FAR:
            return far[0, half, inner, first].astype(jnp.float32)
        place, at = PLACE[third, half]
        return near[place, at, inner, first].astype(jnp.float32)

    for third in range(RING):
        for second in range(RING):
            for first in range(RING):
                got = jnp.where(
                    even,
                    pick(got_near, got_far, first, third, second),
                    pick(got_near, got_far, second, first, third),
                )
                both = pick(own_near, own_far, third, second, first) + got
                gate, up = both[:, :units], both[:, units:]
                hidden = gate / (1.0 + jnp.exp(-gate)) * up
                hidden_ref[third, second, first] = hidden.astype(jnp.bfloat16)


def combine(side, *halves):
    rows, both = halves[0].shape[-2:]
    return pl.pallas_call(
        combine_kernel,
        in_specs=[pl.BlockSpec(memory_space=pltpu.SMEM)]
        + [pl.BlockSpec(memory_space=pltpu.VMEM) for _ in halves],
        out_specs=pl.BlockSpec(memory_space=pltpu.VMEM),
        out_shape=jax.ShapeDtypeStruct((RING, RING, RING, rows, both // 2), jnp.bfloat16),
        compiler_params=pltpu.CompilerParams(vmem_limit_bytes=24 * 1024 * 1024),
        name="combine",
    )(side, *halves)


def body(
    query,
    new_key,
    new_value,
    key_cache,
    value_cache,
    lengths,
    residual,
    norm_gain,
    gate_weight,
    up_weight,
    down_weight,
):
    slots, width = residual.shape
    half = gate_weight.shape[0]
    hidden_units = gate_weight.shape[1]
    rows = 2 * slots
    side = lax.axis_index("side")
    even = side == 0
    mid, own, other = attend(
        side, query, new_key, new_value, key_cache, value_cache, lengths, residual, norm_gain
    )
    got = lax.ppermute(other, "side", SWAP)
    pair = jnp.stack([jnp.where(even, own, got), jnp.where(even, got, own)])
    pair = pair.transpose(0, 2, 1, 3).reshape(rows, half)

    near = jnp.concatenate(gather_line(pair, "first"), axis=0)
    planes = gather_line(near, "second")
    top, bottom = jnp.concatenate(planes[:2], axis=0), jnp.concatenate(planes[2:], axis=0)
    blocks = gather_ring(top, bottom, "third")

    weights = gate_weight.T, up_weight.T
    near = None
    for place in range(3):
        pieces = [blocks[third][part] for (third, part), at in PLACE.items() if at[0] == place]
        near = project(near, place, 3, pieces, *weights)
    far = project(None, 0, 1, [behind(run, near) for run in blocks[FAR]], *weights)
    halves = [near, far, lax.ppermute(near, "side", SWAP), lax.ppermute(far, "side", SWAP)]
    hidden = combine(
        side.reshape(1), *[h.reshape(-1, 2, RING // 2, RING, rows, 2 * hidden_units) for h in halves]
    )

    cut = RING * RING * rows // 2
    runs = [hidden[third].reshape(2, cut, hidden_units) for third in range(RING)]

    def down(run):
        return dot(run.reshape(-1, hidden_units), down_weight).astype(jnp.bfloat16)

    part_far = down(runs[FAR])
    after, before = send(part_far[:cut], "third", 1), send(part_far[cut:], "third", 3)
    one_bottom = send(down(behind(runs[1][1], part_far)), "third", 1)
    three_top = send(down(behind(runs[3][0], part_far)), "third", 3)
    one_top = down(behind(runs[1][0], part_far))
    three_bottom = down(behind(runs[3][1], part_far))
    part_own = down(behind(runs[0], part_far))
    one_top = send(add(one_top, after), "third", 1)
    three_bottom = send(add(three_bottom, before), "third", 3)
    summed = [
        add(part_own[:cut], one_top, three_top),
        add(part_own[cut:], one_bottom, three_bottom),
    ]
    summed = [run for part in summed for run in (part[: cut // 2], part[cut // 2 :])]
    summed = reduce_line(summed, "second")
    summed = reduce_line(parts(summed), "first")

    by_side = summed.reshape(2, slots, half)
    kept = lax.dynamic_index_in_dim(by_side, side, 0, keepdims=False)
    got = lax.ppermute(lax.dynamic_index_in_dim(by_side, 1 - side, 0, keepdims=False), "side", SWAP)
    ffn = jnp.concatenate([jnp.where(even, kept, got), jnp.where(even, got, kept)], axis=1)
    mid = mid.transpose(1, 0, 2).reshape(slots, width)
    return (mid + ffn.astype(jnp.float32)).astype(jnp.bfloat16)


def solution(mesh):
    in_specs = (
        P(("side", "gx"), None),
        P(("side", "gx"), None),
        P(("side", "gx"), None),
        P(("side", "gx"), None, None),
        P(("side", "gx"), None, None),
        P(("side", "gx")),
        P(("side", "gx"), None),
        P(),
        P("side", "gx"),
        P("side", "gx"),
        P("gx", "side"),
    )
    out_specs = P(("side", "gx"), None)
    return jax.shard_map(body, mesh=mesh, in_specs=in_specs, out_specs=out_specs, check_vma=False)
```

time: 173 us -> 159 us (0.919)
  Pallas kernels: 27.4 us -> 18.3 us
  starting transfers between devices: 36.3 us -> 41.3 us
  local copies, waits for them, and re-layouts: 8.26 us -> 3.36 us
  blocking collectives: 4.9 us -> 0 us
    pallas_call x3 -> x5, Pallas kernels: 25.1 us -> 17.1 us  [the longest x4 9.64 us: project(): pl.pallas_call(project_kernel, grid=(1,), in_specs=[pl.BlockSpec(memory_s...]
    all_to_all x1 -> x0, blocking collectives: 4.9 us -> none  [body(): lax.all_to_all(normed.reshape(slots, 2, half), 'side', split_axis=1, conc...]
    ppermute x1, starting transfers between devices: 0.11 us -> 3.3 us  [body(): lax.ppermute(far, 'side', SWAP)]
    unnamed x17 -> x12, local copies, waits for them, and re-layouts: 5.42 us -> 2.93 us
    reshape x3 -> x0, local copies, waits for them, and re-layouts: 2.37 us -> none  [the longest x1 1.35 us: attend(): new_value.reshape(slots, kv_heads, HD)]
  transfers between devices with their start and end apart: 27 -> 28, of which waited for: 20 -> 23; matrix products, arithmetic and copies ran while one was open for 3% -> 3% of each run, Pallas kernels for 9% -> 6%
where the time goes in v3:
time: 159 us; the launch traced here: 158 us
  waiting for transfers between devices  86.5 us (54%)
  starting transfers between devices  41.3 us (26%)
  Pallas kernels  18.3 us (12%)
  matrix products  5.55 us (3%)
  local copies, waits for them, and re-layouts  3.36 us (2%)
  other arithmetic  3.09 us (2%)
    ppermute x12, waiting for transfers between devices, send(): return lax.ppermute(array, ('side', 'gx'), hops(line, distance))  46.1 us
    ppermute x12, waiting for transfers between devices, fetch(): lax.ppermute(array, ('side', 'gx'), [(there, here) for here, there in hop...  37 us
    ppermute x12, starting transfers between devices, fetch(): lax.ppermute(array, ('side', 'gx'), [(there, here) for here, there in hop...  16.8 us
    ppermute x12, starting transfers between devices, send(): return lax.ppermute(array, ('side', 'gx'), hops(line, distance))  12.1 us
    pallas_call x4, Pallas kernels, project(): pl.pallas_call(project_kernel, grid=(1,), in_specs=[pl.BlockSpec(memory_s...  9.64 us
    pallas_call x1, Pallas kernels, attend(): pl.pallas_call(attend_kernel, in_specs=[smem, smem] + [vmem] * 5 + [pl.Bl...  7.49 us
    dot_general x6, matrix products, dot(): return jnp.dot(left, right, preferred_element_type=jnp.float32)  5.55 us
    ppermute x1, starting transfers between devices, body(): lax.ppermute(lax.dynamic_index_in_dim(by_side, 1 - side, 0, keepdims=Fals...  4.18 us
  transfers between devices with their start and end apart: 28, of which 23 were waited for; matrix products, arithmetic and copies ran while one was open for 3% of the time, Pallas kernels for 6%

profile of v3, /device:TPU:1, one launch (start us, length us, event | category | flops | bytes accessed | tf_op | source)
XLA Modules:
  0.0 158.4 jit_solution(3377417133023928398)
XLA Ops:
  0.0 7.5 %attend.1 = (f32[64,8,128]{2,1,0:T(8,128)}, bf16[32,8,128]{2,1,0:T(8,128)(2,1)}, bf16[32,8,128]{2,1,0:T(8,128)(2,1)}) custom-call(s32[1]{0:T(128)} %bitcast.side_ref, s32[8]{0:T(128)} %lengths_ref.1, bf16[64,8,128]{2,1,0:T(8,128)(2,1)} %bitcast.81, bf16[8,8,128]{2,1,0:T(8,128)(2,1)} %bitcast.83, bf16[8,8,128]{2,1,0:T(8,128)(2,1)} %bitcast.84, ...), custom_call_target="tpu_custom_call" | custom-call | tf_op jit(solution)/shard_map/attend/pallas_call | solution.py:168
  11.0 3.9 %collective-permute-start.1 = (bf16[16,4096]{1,0:T(8,128)(2,1)S(1)}, bf16[16,4096]{1,0:T(8,128)(2,1)S(1)}, u32[]{:S(2)}, u32[]{:S(2)}) collective-permute-start(bf16[16,4096]{1,0:T(8,128)(2,1)S(1)} %maximum_bitcast_fusion), channel_id=1, source_target_pairs={{4,0},{5,1},{6,2},{7,3},{8,4},{9,5},{10,6},{11,7},{12,8},{13,9},{1... | collective-permute-start | bytes 393224 | tf_op jit(solution)/shard_map/ppermute | solution.py:41
  15.6 2.6 %collective-permute-done.1 = bf16[16,4096]{1,0:T(8,128)(2,1)S(1)} collective-permute-done((bf16[16,4096]{1,0:T(8,128)(2,1)S(1)}, bf16[16,4096]{1,0:T(8,128)(2,1)S(1)}, u32[]{:S(2)}, u32[]{:S(2)}) %collective-permute-start.1) | collective-permute-done | bytes 131104 | tf_op jit(solution)/shard_map/ppermute | solution.py:41
  18.2 2.1 %collective-permute-done.2 = bf16[16,4096]{1,0:T(8,128)(2,1)S(1)} collective-permute-done((bf16[16,4096]{1,0:T(8,128)(2,1)S(1)}, bf16[16,4096]{1,0:T(8,128)(2,1)S(1)}, u32[]{:S(2)}, u32[]{:S(2)}) %collective-permute-start.2) | collective-permute-done | bytes 131104 | tf_op jit(solution)/shard_map/ppermute | solution.py:41
  21.7 2.8 %collective-permute-start.4 = (bf16[64,4096]{1,0:T(8,128)(2,1)S(1)}, bf16[64,4096]{1,0:T(8,128)(2,1)S(1)}, u32[]{:S(2)}, u32[]{:S(2)}) collective-permute-start(bf16[64,4096]{1,0:T(8,128)(2,1)S(1)} %pad_maximum_fusion), channel_id=1, source_target_pairs={{16,0},{17,1},{18,2},{19,3},{20,4},{21,5},{22,6},{23,7},{24,8},{25... | collective-permute-start | bytes 1572872 | tf_op jit(solution)/shard_map/ppermute | solution.py:41
  25.6 10.7 %collective-permute-done.4 = bf16[64,4096]{1,0:T(8,128)(2,1)S(1)} collective-permute-done((bf16[64,4096]{1,0:T(8,128)(2,1)S(1)}, bf16[64,4096]{1,0:T(8,128)(2,1)S(1)}, u32[]{:S(2)}, u32[]{:S(2)}) %collective-permute-start.4) | collective-permute-done | bytes 524320 | tf_op jit(solution)/shard_map/ppermute | solution.py:41
  36.3 2.3 %collective-permute-start.7 = (bf16[128,4096]{1,0:T(8,128)(2,1)S(1)}, bf16[128,4096]{1,0:T(8,128)(2,1)S(1)}, u32[]{:S(2)}, u32[]{:S(2)}) collective-permute-start(bf16[128,4096]{1,0:T(8,128)(2,1)S(1)} %constant_dynamic-update-slice_fusion.refs_0_), channel_id=1, source_target_pairs={{1,0},{2,1},{3,2},{0,3},{5,4},{6,5},{7,6},{4,7},{9,8},{10,9},{11,1... | collective-permute-start | bytes 3145736 | tf_op jit(solution)/shard_map/ppermute | solution.py:41
  41.0 1.8 %collective-permute-start.9 = (bf16[128,4096]{1,0:T(8,128)(2,1)S(1)}, bf16[128,4096]{1,0:T(8,128)(2,1)S(1)}, u32[]{:S(2)}, u32[]{:S(2)}) collective-permute-start(bf16[128,4096]{1,0:T(8,128)(2,1)S(1)} %constant_dynamic-update-slice_fusion.5.refs_1_), channel_id=1, source_target_pairs={{1,0},{2,1},{3,2},{0,3},{5,4},{6,5},{7,6},{4,7},{9,8},{10,9},{11,1... | collective-permute-start | bytes 3145736 | tf_op jit(solution)/shard_map/ppermute | solution.py:41
  42.7 2.0 %copy-done.1 = bf16[4096,448]{0,1:T(8,128)(2,1)S(1)} copy-done((bf16[4096,448]{0,1:T(8,128)(2,1)S(1)}, bf16[4096,448]{0,1:T(8,128)(2,1)}, u32[]{:S(2)}) %copy-start.1) | copy-done | bytes 3670040
  44.8 2.4 %project.4.refs_0_ = bf16[3,2,128,896]{3,2,1,0:T(8,128)(2,1)S(1)} custom-call(bf16[128,4096]{1,0:T(8,128)(2,1)S(1)} %constant_dynamic-update-slice_fusion.refs_0_, bf16[128,4096]{1,0:T(8,128)(2,1)S(1)} %constant_dynamic-update-slice_fusion.5.refs_1_, bf16[448,4096]{1,0:T(8,128)(2,1)S(1)} %bitcast.62, bf16[448,4096]{1,0:T(8,128)(2,1)S(1)} %bitcast.66), custom_call_target="tpu_custom_call" | custom-call | flops 1879048192 | bytes 7340032 | tf_op jit(solution)/shard_map/project/pallas_call | solution.py:214
  47.2 3.1 %collective-permute-done.7.refs_1_ = bf16[128,4096]{1,0:T(8,128)(2,1)S(1)} collective-permute-done((bf16[128,4096]{1,0:T(8,128)(2,1)S(1)}, bf16[128,4096]{1,0:T(8,128)(2,1)S(1)}, u32[]{:S(2)}, u32[]{:S(2)}) %collective-permute-start.7) | collective-permute-done | bytes 1048608 | tf_op jit(solution)/shard_map/ppermute | solution.py:41
  50.3 3.4 %collective-permute-start.11 = (bf16[128,4096]{1,0:T(8,128)(2,1)S(1)}, bf16[128,4096]{1,0:T(8,128)(2,1)S(1)}, u32[]{:S(2)}, u32[]{:S(2)}) collective-permute-start(bf16[128,4096]{1,0:T(8,128)(2,1)S(1)} %collective-permute-done.7.refs_1_), channel_id=1, source_target_pairs={{1,0},{2,1},{3,2},{0,3},{5,4},{6,5},{7,6},{4,7},{9,8},{10,9},{11,1... | collective-permute-start | bytes 3145736 | tf_op jit(solution)/shard_map/ppermute | solution.py:41
  55.2 2.4 %project.5.refs_0_ = bf16[3,2,128,896]{3,2,1,0:T(8,128)(2,1)S(1)} custom-call(bf16[3,2,128,896]{3,2,1,0:T(8,128)(2,1)S(1)} %project.4.refs_0_, bf16[128,4096]{1,0:T(8,128)(2,1)S(1)} %collective-permute-done.7.refs_1_, bf16[128,4096]{1,0:T(8,128)(2,1)S(1)} %collective-permute-done.8.refs_2_, ...), custom_call_target="tpu_custom_call", output_to_operand_aliasing={{}: (0, {})} | custom-call | flops 1879048192 | bytes 7340032 | tf_op jit(solution)/shard_map/project/pallas_call | solution.py:214
  57.6 3.9 %collective-permute-done.9.refs_1_ = bf16[128,4096]{1,0:T(8,128)(2,1)S(1)} collective-permute-done((bf16[128,4096]{1,0:T(8,128)(2,1)S(1)}, bf16[128,4096]{1,0:T(8,128)(2,1)S(1)}, u32[]{:S(2)}, u32[]{:S(2)}) %collective-permute-start.9) | collective-permute-done | bytes 1048608 | tf_op jit(solution)/shard_map/ppermute | solution.py:41
  61.5 4.9 %collective-permute-done.10.refs_2_ = bf16[128,4096]{1,0:T(8,128)(2,1)S(1)} collective-permute-done((bf16[128,4096]{1,0:T(8,128)(2,1)S(1)}, bf16[128,4096]{1,0:T(8,128)(2,1)S(1)}, u32[]{:S(2)}, u32[]{:S(2)}) %collective-permute-start.10) | collective-permute-done | bytes 1048608 | tf_op jit(solution)/shard_map/ppermute | solution.py:41
  66.4 2.4 %project.6 = bf16[3,2,128,896]{3,2,1,0:T(8,128)(2,1)S(1)} custom-call(bf16[3,2,128,896]{3,2,1,0:T(8,128)(2,1)S(1)} %project.5.refs_0_, bf16[128,4096]{1,0:T(8,128)(2,1)S(1)} %collective-permute-done.9.refs_1_, bf16[128,4096]{1,0:T(8,128)(2,1)S(1)} %collective-permute-done.10.refs_2_, bf16[448,4096]{1,0:T(8,128)(2,1)S(1)} %bitcast.64, ...), custom_call_target="tpu_custom_call", output_to_operand_aliasing={{}: (0, {})} | custom-call | flops 1879048192 | bytes 7340032 | tf_op jit(solution)/shard_map/project/pallas_call | solution.py:214
  68.8 3.3 %collective-permute-start.13 = (bf16[3,2,128,896]{3,2,1,0:T(8,128)(2,1)S(1)}, bf16[3,2,128,896]{3,2,1,0:T(8,128)(2,1)S(1)}, u32[]{:S(2)}, u32[]{:S(2)}) collective-permute-start(bf16[3,2,128,896]{3,2,1,0:T(8,128)(2,1)S(1)} %project.6), channel_id=1, source_target_pairs={{0,64},{64,0},{1,65},{65,1},{2,66},{66,2},{3,67},{67,3},{4,68},{68... | collective-permute-start | bytes 4128776 | tf_op jit(solution)/shard_map/ppermute | solution.py:304
  72.8 4.9 %collective-permute-done.12.refs_1_ = bf16[128,4096]{1,0:T(8,128)(2,1)S(1)} collective-permute-done((bf16[128,4096]{1,0:T(8,128)(2,1)S(1)}, bf16[128,4096]{1,0:T(8,128)(2,1)S(1)}, u32[]{:S(2)}, u32[]{:S(2)}) %collective-permute-start.12) | collective-permute-done | bytes 1048608 | tf_op jit(solution)/shard_map/ppermute | solution.py:41
  77.7 2.4 %project.7 = bf16[1,2,128,896]{3,2,1,0:T(8,128)(2,1)S(1)} custom-call(bf16[128,4096]{1,0:T(8,128)(2,1)S(1)} %collective-permute-done.11.refs_0_, bf16[128,4096]{1,0:T(8,128)(2,1)S(1)} %collective-permute-done.12.refs_1_, bf16[448,4096]{1,0:T(8,128)(2,1)S(1)} %bitcast.65, bf16[448,4096]{1,0:T(8,128)(2,1)S(1)} %bitcast.69), custom_call_target="tpu_custom_call" | custom-call | flops 1879048192 | bytes 7340032 | tf_op jit(solution)/shard_map/project/pallas_call | solution.py:214
  80.1 3.3 %collective-permute-start.14 = (bf16[1,2,128,896]{3,2,1,0:T(8,128)(2,1)S(1)}, bf16[1,2,128,896]{3,2,1,0:T(8,128)(2,1)S(1)}, u32[]{:S(2)}, u32[]{:S(2)}) collective-permute-start(bf16[1,2,128,896]{3,2,1,0:T(8,128)(2,1)S(1)} %project.7), channel_id=1, source_target_pairs={{0,64},{64,0},{1,65},{65,1},{2,66},{66,2},{3,67},{67,3},{4,68},{68... | collective-permute-start | bytes 1376264 | tf_op jit(solution)/shard_map/ppermute | solution.py:304
  88.4 2.7 %collective-permute-start.20 = (bf16[128,4096]{1,0:T(8,128)(2,1)S(1)}, bf16[128,4096]{1,0:T(8,128)(2,1)S(1)}, u32[]{:S(2)}, u32[]{:S(2)}) collective-permute-start(bf16[128,4096]{1,0:T(8,128)(2,1)S(1)} %get-tuple-element.28), channel_id=1, source_target_pairs={{0,3},{1,0},{2,1},{3,2},{4,7},{5,4},{6,5},{7,6},{8,11},{9,8},{10,9... | collective-permute-start | bytes 3145736 | tf_op jit(solution)/shard_map/ppermute | solution.py:37
  94.3 9.2 %collective-permute-done.15 = bf16[128,4096]{1,0:T(8,128)(2,1)S(1)} collective-permute-done((bf16[128,4096]{1,0:T(8,128)(2,1)S(1)}, bf16[128,4096]{1,0:T(8,128)(2,1)S(1)}, u32[]{:S(2)}, u32[]{:S(2)}) %collective-permute-start.15) | collective-permute-done | bytes 1048608 | tf_op jit(solution)/shard_map/ppermute | solution.py:37
  105.4 2.7 %collective-permute-start.21 = (bf16[128,4096]{1,0:T(8,128)(2,1)S(1)}, bf16[128,4096]{1,0:T(8,128)(2,1)S(1)}, u32[]{:S(2)}, u32[]{:S(2)}) collective-permute-start(bf16[128,4096]{1,0:T(8,128)(2,1)S(1)} %add_convert_fusion.1), channel_id=1, source_target_pairs={{0,3},{1,0},{2,1},{3,2},{4,7},{5,4},{6,5},{7,6},{8,11},{9,8},{10,9... | collective-permute-start | bytes 3145736 | tf_op jit(solution)/shard_map/ppermute | solution.py:37
  109.3 4.8 %collective-permute-done.17 = bf16[128,4096]{1,0:T(8,128)(2,1)S(1)} collective-permute-done((bf16[128,4096]{1,0:T(8,128)(2,1)S(1)}, bf16[128,4096]{1,0:T(8,128)(2,1)S(1)}, u32[]{:S(2)}, u32[]{:S(2)}) %collective-permute-start.17) | collective-permute-done | bytes 1048608 | tf_op jit(solution)/shard_map/ppermute | solution.py:37
  114.7 11.2 %collective-permute-done.16 = bf16[128,4096]{1,0:T(8,128)(2,1)S(1)} collective-permute-done((bf16[128,4096]{1,0:T(8,128)(2,1)S(1)}, bf16[128,4096]{1,0:T(8,128)(2,1)S(1)}, u32[]{:S(2)}, u32[]{:S(2)}) %collective-permute-start.16) | collective-permute-done | bytes 1048608 | tf_op jit(solution)/shard_map/ppermute | solution.py:37
  127.2 1.6 %collective-permute-start.23 = (bf16[64,4096]{1,0:T(8,128)(2,1)S(1)}, bf16[64,4096]{1,0:T(8,128)(2,1)S(1)}, u32[]{:S(2)}, u32[]{:S(2)}) collective-permute-start(bf16[64,4096]{1,0:T(8,128)(2,1)S(1)} %get-tuple-element.34), channel_id=1, source_target_pairs={{0,48},{1,49},{2,50},{3,51},{4,52},{5,53},{6,54},{7,55},{8,56},{9,... | collective-permute-start | bytes 1572872 | tf_op jit(solution)/shard_map/ppermute | solution.py:37
  129.7 10.9 %collective-permute-done.23 = bf16[64,4096]{1,0:T(8,128)(2,1)S(1)} collective-permute-done((bf16[64,4096]{1,0:T(8,128)(2,1)S(1)}, bf16[64,4096]{1,0:T(8,128)(2,1)S(1)}, u32[]{:S(2)}, u32[]{:S(2)}) %collective-permute-start.23) | collective-permute-done | bytes 524320 | tf_op jit(solution)/shard_map/ppermute | solution.py:37
  140.5 3.6 %collective-permute-done.18 = bf16[64,4096]{1,0:T(8,128)(2,1)S(1)} collective-permute-done((bf16[64,4096]{1,0:T(8,128)(2,1)S(1)}, bf16[64,4096]{1,0:T(8,128)(2,1)S(1)}, u32[]{:S(2)}, u32[]{:S(2)}) %collective-permute-start.18) | collective-permute-done | bytes 524320 | tf_op jit(solution)/shard_map/ppermute | solution.py:37
  144.4 1.7 %collective-permute-start.26 = (bf16[16,4096]{1,0:T(8,128)(2,1)S(1)}, bf16[16,4096]{1,0:T(8,128)(2,1)S(1)}, u32[]{:S(2)}, u32[]{:S(2)}) collective-permute-start(bf16[16,4096]{1,0:T(8,128)(2,1)S(1)} %get-tuple-element.38), channel_id=1, source_target_pairs={{0,12},{1,13},{2,14},{3,15},{4,0},{5,1},{6,2},{7,3},{8,4},{9,5},{1... | collective-permute-start | bytes 393224 | tf_op jit(solution)/shard_map/ppermute | solution.py:37
  146.8 2.6 %collective-permute-done.26 = bf16[16,4096]{1,0:T(8,128)(2,1)S(1)} collective-permute-done((bf16[16,4096]{1,0:T(8,128)(2,1)S(1)}, bf16[16,4096]{1,0:T(8,128)(2,1)S(1)}, u32[]{:S(2)}, u32[]{:S(2)}) %collective-permute-start.26) | collective-permute-done | bytes 131104 | tf_op jit(solution)/shard_map/ppermute | solution.py:37
  149.4 2.1 %collective-permute-done.25 = bf16[16,4096]{1,0:T(8,128)(2,1)S(1)} collective-permute-done((bf16[16,4096]{1,0:T(8,128)(2,1)S(1)}, bf16[16,4096]{1,0:T(8,128)(2,1)S(1)}, u32[]{:S(2)}, u32[]{:S(2)}) %collective-permute-start.25) | collective-permute-done | bytes 131104 | tf_op jit(solution)/shard_map/ppermute | solution.py:37
  152.6 4.2 %collective-permute-start.27 = (bf16[8,4096]{1,0:T(8,128)(2,1)S(1)}, bf16[8,4096]{1,0:T(8,128)(2,1)S(1)}, u32[]{:S(2)}, u32[]{:S(2)}) collective-permute-start(bf16[8,4096]{1,0:T(8,128)(2,1)S(1)} %dynamic-slice_bitcast_fusion), channel_id=1, source_target_pairs={{0,64},{64,0},{1,65},{65,1},{2,66},{66,2},{3,67},{67,3},{4,68},{68... | collective-permute-start | bytes 196616 | tf_op jit(solution)/shard_map/ppermute | solution.py:334
  (66 shorter events, 28.7 us)
Async XLA Ops:
  7.5 2.6 %collective-permute-start = (bf16[32,8,128]{2,1,0:T(8,128)(2,1)}, bf16[32,8,128]{2,1,0:T(8,128)(2,1)S(1)}, u32[]{:S(2)}, u32[]{:S(2)}) collective-permute-start(bf16[32,8,128]{2,1,0:T(8,128)(2,1)} %get-tuple-element.17), channel_id=1, source_target_pairs={{0,64},{64,0},{1,65},{65,1},{2,66},{66,2},{3,67},{67,3},{4,68},{68... | collective-permute-start | bytes 196616 | tf_op jit(solution)/shard_map/ppermute | solution.py:289
  11.0 7.2 %collective-permute-start.1 = (bf16[16,4096]{1,0:T(8,128)(2,1)S(1)}, bf16[16,4096]{1,0:T(8,128)(2,1)S(1)}, u32[]{:S(2)}, u32[]{:S(2)}) collective-permute-start(bf16[16,4096]{1,0:T(8,128)(2,1)S(1)} %maximum_bitcast_fusion), channel_id=1, source_target_pairs={{4,0},{5,1},{6,2},{7,3},{8,4},{9,5},{10,6},{11,7},{12,8},{13,9},{1... | collective-permute-start | bytes 393224 | tf_op jit(solution)/shard_map/ppermute | solution.py:41
  14.9 5.4 %collective-permute-start.2 = (bf16[16,4096]{1,0:T(8,128)(2,1)S(1)}, bf16[16,4096]{1,0:T(8,128)(2,1)S(1)}, u32[]{:S(2)}, u32[]{:S(2)}) collective-permute-start(bf16[16,4096]{1,0:T(8,128)(2,1)S(1)} %maximum_bitcast_fusion), channel_id=1, source_target_pairs={{8,0},{9,1},{10,2},{11,3},{12,4},{13,5},{14,6},{15,7},{0,8},{1,9},... | collective-permute-start | bytes 393224 | tf_op jit(solution)/shard_map/ppermute | solution.py:41
  14.9 6.7 %collective-permute-start.3 = (bf16[16,4096]{1,0:T(8,128)(2,1)S(1)}, bf16[16,4096]{1,0:T(8,128)(2,1)S(1)}, u32[]{:S(2)}, u32[]{:S(2)}) collective-permute-start(bf16[16,4096]{1,0:T(8,128)(2,1)S(1)} %maximum_bitcast_fusion), channel_id=1, source_target_pairs={{12,0},{13,1},{14,2},{15,3},{0,4},{1,5},{2,6},{3,7},{4,8},{5,9},{6... | collective-permute-start | bytes 393224 | tf_op jit(solution)/shard_map/ppermute | solution.py:41
  21.7 21.0 %copy-start = (bf16[4096,448]{0,1:T(8,128)(2,1)S(1)}, bf16[4096,448]{0,1:T(8,128)(2,1)}, u32[]{:S(2)}) copy-start(bf16[4096,448]{0,1:T(8,128)(2,1)} %param.19) | copy-start | bytes 11010052
  21.7 14.5 %collective-permute-start.4 = (bf16[64,4096]{1,0:T(8,128)(2,1)S(1)}, bf16[64,4096]{1,0:T(8,128)(2,1)S(1)}, u32[]{:S(2)}, u32[]{:S(2)}) collective-permute-start(bf16[64,4096]{1,0:T(8,128)(2,1)S(1)} %pad_maximum_fusion), channel_id=1, source_target_pairs={{16,0},{17,1},{18,2},{19,3},{20,4},{21,5},{22,6},{23,7},{24,8},{25... | collective-permute-start | bytes 1572872 | tf_op jit(solution)/shard_map/ppermute | solution.py:41
  24.5 14.0 %collective-permute-start.5 = (bf16[64,4096]{1,0:T(8,128)(2,1)S(1)}, bf16[64,4096]{1,0:T(8,128)(2,1)S(1)}, u32[]{:S(2)}, u32[]{:S(2)}) collective-permute-start(bf16[64,4096]{1,0:T(8,128)(2,1)S(1)} %pad_maximum_fusion), channel_id=1, source_target_pairs={{32,0},{33,1},{34,2},{35,3},{36,4},{37,5},{38,6},{39,7},{40,8},{41... | collective-permute-start | bytes 1572872 | tf_op jit(solution)/shard_map/ppermute | solution.py:41
  24.8 15.1 %collective-permute-start.6 = (bf16[64,4096]{1,0:T(8,128)(2,1)S(1)}, bf16[64,4096]{1,0:T(8,128)(2,1)S(1)}, u32[]{:S(2)}, u32[]{:S(2)}) collective-permute-start(bf16[64,4096]{1,0:T(8,128)(2,1)S(1)} %pad_maximum_fusion), channel_id=1, source_target_pairs={{48,0},{49,1},{50,2},{51,3},{52,4},{53,5},{54,6},{55,7},{56,8},{57... | collective-permute-start | bytes 1572872 | tf_op jit(solution)/shard_map/ppermute | solution.py:41
  36.3 14.0 %collective-permute-start.7 = (bf16[128,4096]{1,0:T(8,128)(2,1)S(1)}, bf16[128,4096]{1,0:T(8,128)(2,1)S(1)}, u32[]{:S(2)}, u32[]{:S(2)}) collective-permute-start(bf16[128,4096]{1,0:T(8,128)(2,1)S(1)} %constant_dynamic-update-slice_fusion.refs_0_), channel_id=1, source_target_pairs={{1,0},{2,1},{3,2},{0,3},{5,4},{6,5},{7,6},{4,7},{9,8},{10,9},{11,1... | collective-permute-start | bytes 3145736 | tf_op jit(solution)/shard_map/ppermute | solution.py:41
  40.0 15.2 %collective-permute-start.8 = (bf16[128,4096]{1,0:T(8,128)(2,1)S(1)}, bf16[128,4096]{1,0:T(8,128)(2,1)S(1)}, u32[]{:S(2)}, u32[]{:S(2)}) collective-permute-start(bf16[128,4096]{1,0:T(8,128)(2,1)S(1)} %constant_dynamic-update-slice_fusion.5.refs_1_), channel_id=1, source_target_pairs={{3,0},{0,1},{1,2},{2,3},{7,4},{4,5},{5,6},{6,7},{11,8},{8,9},{9,10... | collective-permute-start | bytes 3145736 | tf_op jit(solution)/shard_map/ppermute | solution.py:41
  41.0 20.6 %collective-permute-start.9 = (bf16[128,4096]{1,0:T(8,128)(2,1)S(1)}, bf16[128,4096]{1,0:T(8,128)(2,1)S(1)}, u32[]{:S(2)}, u32[]{:S(2)}) collective-permute-start(bf16[128,4096]{1,0:T(8,128)(2,1)S(1)} %constant_dynamic-update-slice_fusion.5.refs_1_), channel_id=1, source_target_pairs={{1,0},{2,1},{3,2},{0,3},{5,4},{6,5},{7,6},{4,7},{9,8},{10,9},{11,1... | collective-permute-start | bytes 3145736 | tf_op jit(solution)/shard_map/ppermute | solution.py:41
  42.7 23.7 %collective-permute-start.10 = (bf16[128,4096]{1,0:T(8,128)(2,1)S(1)}, bf16[128,4096]{1,0:T(8,128)(2,1)S(1)}, u32[]{:S(2)}, u32[]{:S(2)}) collective-permute-start(bf16[128,4096]{1,0:T(8,128)(2,1)S(1)} %constant_dynamic-update-slice_fusion.refs_0_), channel_id=1, source_target_pairs={{3,0},{0,1},{1,2},{2,3},{7,4},{4,5},{5,6},{6,7},{11,8},{8,9},{9,10... | collective-permute-start | bytes 3145736 | tf_op jit(solution)/shard_map/ppermute | solution.py:41
  42.7 2.0 %copy-start.1 = (bf16[4096,448]{0,1:T(8,128)(2,1)S(1)}, bf16[4096,448]{0,1:T(8,128)(2,1)}, u32[]{:S(2)}) copy-start(bf16[4096,448]{0,1:T(8,128)(2,1)} %param.20) | copy-start | bytes 11010052
  50.3 22.5 %collective-permute-start.11 = (bf16[128,4096]{1,0:T(8,128)(2,1)S(1)}, bf16[128,4096]{1,0:T(8,128)(2,1)S(1)}, u32[]{:S(2)}, u32[]{:S(2)}) collective-permute-start(bf16[128,4096]{1,0:T(8,128)(2,1)S(1)} %collective-permute-done.7.refs_1_), channel_id=1, source_target_pairs={{1,0},{2,1},{3,2},{0,3},{5,4},{6,5},{7,6},{4,7},{9,8},{10,9},{11,1... | collective-permute-start | bytes 3145736 | tf_op jit(solution)/shard_map/ppermute | solution.py:41
  55.2 22.5 %collective-permute-start.12 = (bf16[128,4096]{1,0:T(8,128)(2,1)S(1)}, bf16[128,4096]{1,0:T(8,128)(2,1)S(1)}, u32[]{:S(2)}, u32[]{:S(2)}) collective-permute-start(bf16[128,4096]{1,0:T(8,128)(2,1)S(1)} %collective-permute-done.8.refs_2_), channel_id=1, source_target_pairs={{3,0},{0,1},{1,2},{2,3},{7,4},{4,5},{5,6},{6,7},{11,8},{8,9},{9,10... | collective-permute-start | bytes 3145736 | tf_op jit(solution)/shard_map/ppermute | solution.py:41
  68.8 14.5 %collective-permute-start.13 = (bf16[3,2,128,896]{3,2,1,0:T(8,128)(2,1)S(1)}, bf16[3,2,128,896]{3,2,1,0:T(8,128)(2,1)S(1)}, u32[]{:S(2)}, u32[]{:S(2)}) collective-permute-start(bf16[3,2,128,896]{3,2,1,0:T(8,128)(2,1)S(1)} %project.6), channel_id=1, source_target_pairs={{0,64},{64,0},{1,65},{65,1},{2,66},{66,2},{3,67},{67,3},{4,68},{68... | collective-permute-start | bytes 4128776 | tf_op jit(solution)/shard_map/ppermute | solution.py:304
  80.1 4.7 %collective-permute-start.14 = (bf16[1,2,128,896]{3,2,1,0:T(8,128)(2,1)S(1)}, bf16[1,2,128,896]{3,2,1,0:T(8,128)(2,1)S(1)}, u32[]{:S(2)}, u32[]{:S(2)}) collective-permute-start(bf16[1,2,128,896]{3,2,1,0:T(8,128)(2,1)S(1)} %project.7), channel_id=1, source_target_pairs={{0,64},{64,0},{1,65},{65,1},{2,66},{66,2},{3,67},{67,3},{4,68},{68... | collective-permute-start | bytes 1376264 | tf_op jit(solution)/shard_map/ppermute | solution.py:304
  84.8 2.0 %copy-start.2 = (bf16[448,4096]{1,0:T(8,128)(2,1)S(1)}, bf16[448,4096]{1,0:T(8,128)(2,1)}, u32[]{:S(2)}) copy-start(bf16[448,4096]{1,0:T(8,128)(2,1)} %param.21) | copy-start | bytes 11010052
  88.3 15.2 %collective-permute-start.15 = (bf16[128,4096]{1,0:T(8,128)(2,1)S(1)}, bf16[128,4096]{1,0:T(8,128)(2,1)S(1)}, u32[]{:S(2)}, u32[]{:S(2)}) collective-permute-start(bf16[128,4096]{1,0:T(8,128)(2,1)S(1)} %get-tuple-element.27), channel_id=1, source_target_pairs={{0,1},{1,2},{2,3},{3,0},{4,5},{5,6},{6,7},{7,4},{8,9},{9,10},{10,1... | collective-permute-start | bytes 3145736 | tf_op jit(solution)/shard_map/ppermute | solution.py:37
  88.4 16.2 %collective-permute-start.20 = (bf16[128,4096]{1,0:T(8,128)(2,1)S(1)}, bf16[128,4096]{1,0:T(8,128)(2,1)S(1)}, u32[]{:S(2)}, u32[]{:S(2)}) collective-permute-start(bf16[128,4096]{1,0:T(8,128)(2,1)S(1)} %get-tuple-element.28), channel_id=1, source_target_pairs={{0,3},{1,0},{2,1},{3,2},{4,7},{5,4},{6,5},{7,6},{8,11},{9,8},{10,9... | collective-permute-start | bytes 3145736 | tf_op jit(solution)/shard_map/ppermute | solution.py:37
  91.9 22.2 %collective-permute-start.17 = (bf16[128,4096]{1,0:T(8,128)(2,1)S(1)}, bf16[128,4096]{1,0:T(8,128)(2,1)S(1)}, u32[]{:S(2)}, u32[]{:S(2)}) collective-permute-start(bf16[128,4096]{1,0:T(8,128)(2,1)S(1)} %convolution_convert_fusion.4), channel_id=1, source_target_pairs={{0,3},{1,0},{2,1},{3,2},{4,7},{5,4},{6,5},{7,6},{8,11},{9,8},{10,9... | collective-permute-start | bytes 3145736 | tf_op jit(solution)/shard_map/ppermute | solution.py:37
  92.8 22.0 %collective-permute-start.19 = (bf16[128,4096]{1,0:T(8,128)(2,1)S(1)}, bf16[128,4096]{1,0:T(8,128)(2,1)S(1)}, u32[]{:S(2)}, u32[]{:S(2)}) collective-permute-start(bf16[128,4096]{1,0:T(8,128)(2,1)S(1)} %convolution_convert_fusion.3), channel_id=1, source_target_pairs={{0,1},{1,2},{2,3},{3,0},{4,5},{5,6},{6,7},{7,4},{8,9},{9,10},{10,1... | collective-permute-start | bytes 3145736 | tf_op jit(solution)/shard_map/ppermute | solution.py:37
  104.3 21.7 %collective-permute-start.16 = (bf16[128,4096]{1,0:T(8,128)(2,1)S(1)}, bf16[128,4096]{1,0:T(8,128)(2,1)S(1)}, u32[]{:S(2)}, u32[]{:S(2)}) collective-permute-start(bf16[128,4096]{1,0:T(8,128)(2,1)S(1)} %add_convert_fusion.3), channel_id=1, source_target_pairs={{0,1},{1,2},{2,3},{3,0},{4,5},{5,6},{6,7},{7,4},{8,9},{9,10},{10,1... | collective-permute-start | bytes 3145736 | tf_op jit(solution)/shard_map/ppermute | solution.py:37
  105.4 20.6 %collective-permute-start.21 = (bf16[128,4096]{1,0:T(8,128)(2,1)S(1)}, bf16[128,4096]{1,0:T(8,128)(2,1)S(1)}, u32[]{:S(2)}, u32[]{:S(2)}) collective-permute-start(bf16[128,4096]{1,0:T(8,128)(2,1)S(1)} %add_convert_fusion.1), channel_id=1, source_target_pairs={{0,3},{1,0},{2,1},{3,2},{4,7},{5,4},{6,5},{7,6},{8,11},{9,8},{10,9... | collective-permute-start | bytes 3145736 | tf_op jit(solution)/shard_map/ppermute | solution.py:37
  127.2 13.3 %collective-permute-start.23 = (bf16[64,4096]{1,0:T(8,128)(2,1)S(1)}, bf16[64,4096]{1,0:T(8,128)(2,1)S(1)}, u32[]{:S(2)}, u32[]{:S(2)}) collective-permute-start(bf16[64,4096]{1,0:T(8,128)(2,1)S(1)} %get-tuple-element.34), channel_id=1, source_target_pairs={{0,48},{1,49},{2,50},{3,51},{4,52},{5,53},{6,54},{7,55},{8,56},{9,... | collective-permute-start | bytes 1572872 | tf_op jit(solution)/shard_map/ppermute | solution.py:37
  128.8 11.7 %collective-permute-start.22 = (bf16[64,4096]{1,0:T(8,128)(2,1)S(1)}, bf16[64,4096]{1,0:T(8,128)(2,1)S(1)}, u32[]{:S(2)}, u32[]{:S(2)}) collective-permute-start(bf16[64,4096]{1,0:T(8,128)(2,1)S(1)} %get-tuple-element.33), channel_id=1, source_target_pairs={{0,32},{1,33},{2,34},{3,35},{4,36},{5,37},{6,38},{7,39},{8,40},{9,... | collective-permute-start | bytes 1572872 | tf_op jit(solution)/shard_map/ppermute | solution.py:37
  128.9 28.8 %copy-start.3 = (f32[64,8,128]{2,1,0:T(8,128)S(1)}, f32[64,8,128]{2,1,0:T(8,128)}, u32[]{:S(2)}) copy-start(f32[64,8,128]{2,1,0:T(8,128)} %get-tuple-element.15) | copy-start | bytes 786436
  128.9 15.2 %collective-permute-start.18 = (bf16[64,4096]{1,0:T(8,128)(2,1)S(1)}, bf16[64,4096]{1,0:T(8,128)(2,1)S(1)}, u32[]{:S(2)}, u32[]{:S(2)}) collective-permute-start(bf16[64,4096]{1,0:T(8,128)(2,1)S(1)} %slice.89), channel_id=1, source_target_pairs={{0,16},{1,17},{2,18},{3,19},{4,20},{5,21},{6,22},{7,23},{8,24},{9,... | collective-permute-start | bytes 1572872 | tf_op jit(solution)/shard_map/ppermute | solution.py:37
  144.4 5.0 %collective-permute-start.26 = (bf16[16,4096]{1,0:T(8,128)(2,1)S(1)}, bf16[16,4096]{1,0:T(8,128)(2,1)S(1)}, u32[]{:S(2)}, u32[]{:S(2)}) collective-permute-start(bf16[16,4096]{1,0:T(8,128)(2,1)S(1)} %get-tuple-element.38), channel_id=1, source_target_pairs={{0,12},{1,13},{2,14},{3,15},{4,0},{5,1},{6,2},{7,3},{8,4},{9,5},{1... | collective-permute-start | bytes 393224 | tf_op jit(solution)/shard_map/ppermute | solution.py:37
  146.1 5.4 %collective-permute-start.25 = (bf16[16,4096]{1,0:T(8,128)(2,1)S(1)}, bf16[16,4096]{1,0:T(8,128)(2,1)S(1)}, u32[]{:S(2)}, u32[]{:S(2)}) collective-permute-start(bf16[16,4096]{1,0:T(8,128)(2,1)S(1)} %get-tuple-element.39), channel_id=1, source_target_pairs={{0,8},{1,9},{2,10},{3,11},{4,12},{5,13},{6,14},{7,15},{8,0},{9,1},... | collective-permute-start | bytes 393224 | tf_op jit(solution)/shard_map/ppermute | solution.py:37
  146.1 6.4 %collective-permute-start.24 = (bf16[16,4096]{1,0:T(8,128)(2,1)S(1)}, bf16[16,4096]{1,0:T(8,128)(2,1)S(1)}, u32[]{:S(2)}, u32[]{:S(2)}) collective-permute-start(bf16[16,4096]{1,0:T(8,128)(2,1)S(1)} %get-tuple-element.37), channel_id=1, source_target_pairs={{0,4},{1,5},{2,6},{3,7},{4,8},{5,9},{6,10},{7,11},{8,12},{9,13},{1... | collective-permute-start | bytes 393224 | tf_op jit(solution)/shard_map/ppermute | solution.py:37
  152.6 5.1 %collective-permute-start.27 = (bf16[8,4096]{1,0:T(8,128)(2,1)S(1)}, bf16[8,4096]{1,0:T(8,128)(2,1)S(1)}, u32[]{:S(2)}, u32[]{:S(2)}) collective-permute-start(bf16[8,4096]{1,0:T(8,128)(2,1)S(1)} %dynamic-slice_bitcast_fusion), channel_id=1, source_target_pairs={{0,64},{64,0},{1,65},{65,1},{2,66},{66,2},{3,67},{67,3},{4,68},{68... | collective-permute-start | bytes 196616 | tf_op jit(solution)/shard_map/ppermute | solution.py:334

commit v4 on v3

--- a/solution.py
+++ b/solution.py
@@ -12,6 +12,9 @@
 RING = 4
 VMEM = 60 * 1024 * 1024
 TOGETHER = 4
+FAR = 2
+ORDER = (0, 1, 3, 2)
+STEPS = (0, 1, 3, 2)
 FAR = 2
 PLACE = {(0, 0): (0, 0), (0, 1): (0, 1), (1, 0): (1, 0), (3, 1): (1, 1), (1, 1): (2, 0), (3, 0): (2, 1)}
 LINES = {"first": ("x", "z"), "second": ("z", "y"), "third": ("y", "x")}
@@ -46,11 +49,16 @@
     return [array, fetch(array, line, 1), far, fetch(array, line, 3)]
 
 
-def gather_ring(top, bottom, line):
-    after_top, before_bottom = fetch(top, line, 1), fetch(bottom, line, 3)
-    after_bottom, before_top = fetch(bottom, line, 1), fetch(top, line, 3)
-    far = [fetch(after_top, line, 1), fetch(before_bottom, line, 3)]
-    return [[top, bottom], [after_top, after_bottom], far, [before_top, before_bottom]]
+def gather_ring(early, late, line):
+    step = late.shape[0]
+    after, before = fetch(early, line, 1), fetch(early, line, 3)
+    after_late, before_late = fetch(late, line, 1), fetch(late, line, 3)
+    far = [
+        fetch(after[: 2 * step], line, 1),
+        fetch(before[2 * step :], line, 3),
+        fetch(behind(before_late, after_late), line, 3),
+    ]
+    return [[early, late], [after, after_late], far, [before, before_late]]
 
 
 def behind(array, *others):
@@ -197,55 +205,51 @@
     return lax.dot_general(rows, weight, (((1,), (1,)), ((), ())), preferred_element_type=jnp.float32)
 
 
-def project_kernel(*refs):
-    top_ref, bottom_ref, gate_ref, up_ref, out_ref = refs[-5:]
+def project_kernel(count, *refs):
+    *runs, gate_ref, up_ref, out_ref = refs[-3 - count :]
     units = gate_ref.shape[0]
-    shape = out_ref.shape[1:3] + (units,)
-    rows = jnp.concatenate([top_ref[...], bottom_ref[...]], axis=0)
-    out_ref[0, :, :, :units] = times(rows, gate_ref[...]).astype(jnp.bfloat16).reshape(shape)
-    out_ref[0, :, :, units:] = times(rows, up_ref[...]).astype(jnp.bfloat16).reshape(shape)
-
-
-def project(found, place, count, halves, gate_weight, up_weight):
-    cut, features = halves[0].shape
+    rows = jnp.concatenate([run[...] for run in runs], axis=0)
+    out_ref[0, :, :units] = times(rows, gate_ref[...]).astype(jnp.bfloat16)
+    out_ref[0, :, units:] = times(rows, up_ref[...]).astype(jnp.bfloat16)
+
+
+def project(found, place, count, runs, gate_weight, up_weight):
+    features = runs[0].shape[1]
+    size = sum(run.shape[0] for run in runs)
     units = gate_weight.shape[0]
     vmem = pl.BlockSpec(memory_space=pltpu.VMEM)
     earlier = [] if found is None else [found]
     return pl.pallas_call(
-        project_kernel,
+        functools.partial(project_kernel, len(runs)),
         grid=(1,),
-        in_specs=[pl.BlockSpec(memory_space=pl.ANY) for _ in earlier] + [vmem] * 4,
-        out_specs=pl.BlockSpec((1, 2, cut, 2 * units), lambda i: (place, 0, 0, 0)),
-        out_shape=jax.ShapeDtypeStruct((count, 2, cut, 2 * units), jnp.bfloat16),
+        in_specs=[pl.BlockSpec(memory_space=pl.ANY) for _ in earlier] + [vmem] * (len(runs) + 2),
+        out_specs=pl.BlockSpec((1, size, 2 * units), lambda i: (place, 0, 0)),
+        out_shape=jax.ShapeDtypeStruct((count, size, 2 * units), jnp.bfloat16),
         input_output_aliases={0: 0} if earlier else {},
         compiler_params=pltpu.CompilerParams(vmem_limit_bytes=24 * 1024 * 1024),
         cost_estimate=pl.CostEstimate(
-            flops=8 * cut * units * features, bytes_accessed=4 * units * features, transcendentals=0
+            flops=4 * size * units * features, bytes_accessed=4 * units * features, transcendentals=0
         ),
         name="project",
-    )(*earlier, *halves, gate_weight, up_weight)
-
-
-def combine_kernel(side_ref, own_near, own_far, got_near, got_far, hidden_ref):
+    )(*earlier, *runs, gate_weight, up_weight)
+
+
+def combine_kernel(side_ref, own, other, hidden_ref):
     units = hidden_ref.shape[-1]
     even = side_ref[0] == 0
 
-    def pick(near, far, third, second, first):
-        half, inner = divmod(second, RING // 2)
-        if third == FAR:
-            return far[0, half, inner, first].astype(jnp.float32)
-        place, at = PLACE[third, half]
-        return near[place, at, inner, first].astype(jnp.float32)
+    def pick(found, third, second, first):
+        return found[ORDER.index(third), STEPS.index(second), first].astype(jnp.float32)
 
     for third in range(RING):
         for second in range(RING):
             for first in range(RING):
                 got = jnp.where(
                     even,
-                    pick(got_near, got_far, first, third, second),
-                    pick(got_near, got_far, second, first, third),
+                    pick(other, first, third, second),
+                    pick(other, second, first, third),
                 )
-                both = pick(own_near, own_far, third, second, first) + got
+                both = pick(own, third, second, first) + got
                 gate, up = both[:, :units], both[:, units:]
                 hidden = gate / (1.0 + jnp.exp(-gate)) * up
                 hidden_ref[third, second, first] = hidden.astype(jnp.bfloat16)
@@ -291,19 +295,23 @@
     pair = pair.transpose(0, 2, 1, 3).reshape(rows, half)
 
     near = jnp.concatenate(gather_line(pair, "first"), axis=0)
-    planes = gather_line(near, "second")
-    top, bottom = jnp.concatenate(planes[:2], axis=0), jnp.concatenate(planes[2:], axis=0)
-    blocks = gather_ring(top, bottom, "third")
+    after, before = fetch(near, "second", 1), fetch(near, "second", 3)
+    cut = near.shape[0] // 2
+    relayed = [fetch(after[:cut], "second", 1), fetch(before[cut:], "second", 3)]
+    early = jnp.concatenate([near, after, before], axis=0)
+    late = jnp.concatenate(relayed, axis=0)
+    blocks = gather_ring(early, late, "third")
 
     weights = gate_weight.T, up_weight.T
-    near = None
-    for place in range(3):
-        pieces = [blocks[third][part] for (third, part), at in PLACE.items() if at[0] == place]
-        near = project(near, place, 3, pieces, *weights)
-    far = project(None, 0, 1, [behind(run, near) for run in blocks[FAR]], *weights)
-    halves = [near, far, lax.ppermute(near, "side", SWAP), lax.ppermute(far, "side", SWAP)]
+    found = None
+    for place, third in enumerate(ORDER):
+        runs = blocks[third]
+        if place == 0:
+            runs = [behind(run, blocks[FAR][1]) for run in runs]
+        found = project(found, place, RING, runs, *weights)
+    halves = [found, lax.ppermute(found, "side", SWAP)]
     hidden = combine(
-        side.reshape(1), *[h.reshape(-1, 2, RING // 2, RING, rows, 2 * hidden_units) for h in halves]
+        side.reshape(1), *[h.reshape(-1, RING, RING, rows, 2 * hidden_units) for h in halves]
     )
 
     cut = RING * RING * rows // 2

time: 159 us -> 157 us (0.987)
  starting transfers between devices: 41.3 us -> 38.6 us
  waiting for transfers between devices: 86.5 us -> 89 us
  local copies, waits for them, and re-layouts: 3.36 us -> 1.54 us
    unnamed x12 -> x13, local copies, waits for them, and re-layouts: 2.93 us -> 0.94 us
    ppermute x2 -> x1, waiting for transfers between devices: 1.44 us -> 3.41 us  [body(): halves = [found, lax.ppermute(found, 'side', SWAP)]]
    ppermute x12 -> x14, waiting for transfers between devices: 37 us -> 37.7 us  [fetch(): lax.ppermute(array, ('side', 'gx'), [(there, here) for here, there in hop...]
    ppermute x2 -> x1, starting transfers between devices: 6.61 us -> 6.21 us  [body(): halves = [found, lax.ppermute(found, 'side', SWAP)]]
    ppermute x12 -> x14, starting transfers between devices: 16.8 us -> 17 us  [fetch(): lax.ppermute(array, ('side', 'gx'), [(there, here) for here, there in hop...]
  transfers between devices with their start and end apart: 28 -> 29, of which waited for: 23 -> 24; matrix products, arithmetic and copies ran while one was open for 3% -> 3% of each run, Pallas kernels for 6% -> 5%
where the time goes in v4:
time: 157 us; the launch traced here: 156 us
  waiting for transfers between devices  89 us (57%)
  starting transfers between devices  38.6 us (25%)
  Pallas kernels  18.4 us (12%)
  matrix products  5.41 us (3%)
  other arithmetic  2.98 us (2%)
    ppermute x12, waiting for transfers between devices, send(): return lax.ppermute(array, ('side', 'gx'), hops(line, distance))  45.9 us
    ppermute x14, waiting for transfers between devices, fetch(): lax.ppermute(array, ('side', 'gx'), [(there, here) for here, there in hop...  37.7 us
    ppermute x14, starting transfers between devices, fetch(): lax.ppermute(array, ('side', 'gx'), [(there, here) for here, there in hop...  17 us
    ppermute x12, starting transfers between devices, send(): return lax.ppermute(array, ('side', 'gx'), hops(line, distance))  10.8 us
    pallas_call x4, Pallas kernels, project(): pl.pallas_call(functools.partial(project_kernel, len(runs)), grid=(1,), i...  9.71 us
    pallas_call x1, Pallas kernels, attend(): pl.pallas_call(attend_kernel, in_specs=[smem, smem] + [vmem] * 5 + [pl.Bl...  7.5 us
    ppermute x1, starting transfers between devices, body(): halves = [found, lax.ppermute(found, 'side', SWAP)]  6.21 us
    dot_general x6, matrix products, dot(): return jnp.dot(left, right, preferred_element_type=jnp.float32)  5.41 us
  transfers between devices with their start and end apart: 29, of which 24 were waited for; matrix products, arithmetic and copies ran while one was open for 3% of the time, Pallas kernels for 5%

profile of v4, /device:TPU:1, one launch (start us, length us, event | category | flops | bytes accessed | tf_op | source)
XLA Modules:
  0.0 156.3 jit_solution(4054192770133188147)
XLA Ops:
  0.0 7.5 %attend.1 = (f32[64,8,128]{2,1,0:T(8,128)}, bf16[32,8,128]{2,1,0:T(8,128)(2,1)}, bf16[32,8,128]{2,1,0:T(8,128)(2,1)}) custom-call(s32[1]{0:T(128)} %bitcast.side_ref, s32[8]{0:T(128)} %lengths_ref.1, bf16[64,8,128]{2,1,0:T(8,128)(2,1)} %bitcast.77, bf16[8,8,128]{2,1,0:T(8,128)(2,1)} %bitcast.79, bf16[8,8,128]{2,1,0:T(8,128)(2,1)} %bitcast.80, ...), custom_call_target="tpu_custom_call" | custom-call | tf_op jit(solution)/shard_map/attend/pallas_call | solution.py:176
  11.0 3.9 %collective-permute-start.1 = (bf16[16,4096]{1,0:T(8,128)(2,1)S(1)}, bf16[16,4096]{1,0:T(8,128)(2,1)S(1)}, u32[]{:S(2)}, u32[]{:S(2)}) collective-permute-start(bf16[16,4096]{1,0:T(8,128)(2,1)S(1)} %maximum_bitcast_fusion), channel_id=1, source_target_pairs={{4,0},{5,1},{6,2},{7,3},{8,4},{9,5},{10,6},{11,7},{12,8},{13,9},{1... | collective-permute-start | bytes 393224 | tf_op jit(solution)/shard_map/ppermute | solution.py:44
  15.6 2.6 %collective-permute-done.1 = bf16[16,4096]{1,0:T(8,128)(2,1)S(1)} collective-permute-done((bf16[16,4096]{1,0:T(8,128)(2,1)S(1)}, bf16[16,4096]{1,0:T(8,128)(2,1)S(1)}, u32[]{:S(2)}, u32[]{:S(2)}) %collective-permute-start.1) | collective-permute-done | bytes 131104 | tf_op jit(solution)/shard_map/ppermute | solution.py:44
  18.2 2.1 %collective-permute-done.2 = bf16[16,4096]{1,0:T(8,128)(2,1)S(1)} collective-permute-done((bf16[16,4096]{1,0:T(8,128)(2,1)S(1)}, bf16[16,4096]{1,0:T(8,128)(2,1)S(1)}, u32[]{:S(2)}, u32[]{:S(2)}) %collective-permute-start.2) | collective-permute-done | bytes 131104 | tf_op jit(solution)/shard_map/ppermute | solution.py:44
  21.7 2.8 %collective-permute-start.4 = (bf16[64,4096]{1,0:T(8,128)(2,1)S(1)}, bf16[64,4096]{1,0:T(8,128)(2,1)S(1)}, u32[]{:S(2)}, u32[]{:S(2)}) collective-permute-start(bf16[64,4096]{1,0:T(8,128)(2,1)S(1)} %pad_maximum_fusion), channel_id=1, source_target_pairs={{16,0},{17,1},{18,2},{19,3},{20,4},{21,5},{22,6},{23,7},{24,8},{25... | collective-permute-start | bytes 1572872 | tf_op jit(solution)/shard_map/ppermute | solution.py:44
  24.5 6.1 %collective-permute-done.4 = bf16[64,4096]{1,0:T(8,128)(2,1)S(1)} collective-permute-done((bf16[64,4096]{1,0:T(8,128)(2,1)S(1)}, bf16[64,4096]{1,0:T(8,128)(2,1)S(1)}, u32[]{:S(2)}, u32[]{:S(2)}) %collective-permute-start.4) | collective-permute-done | bytes 524320 | tf_op jit(solution)/shard_map/ppermute | solution.py:44
  30.6 3.4 %collective-permute-done.5 = bf16[64,4096]{1,0:T(8,128)(2,1)S(1)} collective-permute-done((bf16[64,4096]{1,0:T(8,128)(2,1)S(1)}, bf16[64,4096]{1,0:T(8,128)(2,1)S(1)}, u32[]{:S(2)}, u32[]{:S(2)}) %collective-permute-start.5) | collective-permute-done | bytes 524320 | tf_op jit(solution)/shard_map/ppermute | solution.py:44
  35.0 1.8 %collective-permute-start.10 = (bf16[192,4096]{1,0:T(8,128)(2,1)S(1)}, bf16[192,4096]{1,0:T(8,128)(2,1)S(1)}, u32[]{:S(2)}, u32[]{:S(2)}) collective-permute-start(bf16[192,4096]{1,0:T(8,128)(2,1)S(1)} %constant_dynamic-update-slice_fusion.refs_0_), channel_id=1, source_target_pairs={{1,0},{2,1},{3,2},{0,3},{5,4},{6,5},{7,6},{4,7},{9,8},{10,9},{11,1... | collective-permute-start | bytes 4718600 | tf_op jit(solution)/shard_map/ppermute | solution.py:44
  38.5 4.8 %collective-permute-done.8 = bf16[32,4096]{1,0:T(8,128)(2,1)S(1)} collective-permute-done((bf16[32,4096]{1,0:T(8,128)(2,1)S(1)}, bf16[32,4096]{1,0:T(8,128)(2,1)S(1)}, u32[]{:S(2)}, u32[]{:S(2)}) %collective-permute-start.8) | collective-permute-done | bytes 262176 | tf_op jit(solution)/shard_map/ppermute | solution.py:44
  43.2 3.1 %collective-permute-done.9 = bf16[32,4096]{1,0:T(8,128)(2,1)S(1)} collective-permute-done((bf16[32,4096]{1,0:T(8,128)(2,1)S(1)}, bf16[32,4096]{1,0:T(8,128)(2,1)S(1)}, u32[]{:S(2)}, u32[]{:S(2)}) %collective-permute-start.9) | collective-permute-done | bytes 262176 | tf_op jit(solution)/shard_map/ppermute | solution.py:44
  47.9 6.9 %collective-permute-done.6.refs_1_ = bf16[192,4096]{1,0:T(8,128)(2,1)S(1)} collective-permute-done((bf16[192,4096]{1,0:T(8,128)(2,1)S(1)}, bf16[192,4096]{1,0:T(8,128)(2,1)S(1)}, u32[]{:S(2)}, u32[]{:S(2)}) %collective-permute-start.6) | collective-permute-done | bytes 1572896 | tf_op jit(solution)/shard_map/ppermute | solution.py:44
  55.1 2.7 %collective-permute-start.13 = (bf16[128,4096]{1,0:T(8,128)(2,1)S(1)}, bf16[128,4096]{1,0:T(8,128)(2,1)S(1)}, u32[]{:S(2)}, u32[]{:S(2)}) collective-permute-start(bf16[128,4096]{1,0:T(8,128)(2,1)S(1)} %slice.101), channel_id=1, source_target_pairs={{1,0},{2,1},{3,2},{0,3},{5,4},{6,5},{7,6},{4,7},{9,8},{10,9},{11,1... | collective-permute-start | bytes 3145736 | tf_op jit(solution)/shard_map/ppermute | solution.py:44
  57.8 2.4 %collective-permute-done.11.refs_2_ = bf16[64,4096]{1,0:T(8,128)(2,1)S(1)} collective-permute-done((bf16[64,4096]{1,0:T(8,128)(2,1)S(1)}, bf16[64,4096]{1,0:T(8,128)(2,1)S(1)}, u32[]{:S(2)}, u32[]{:S(2)}) %collective-permute-start.11) | collective-permute-done | bytes 524320 | tf_op jit(solution)/shard_map/ppermute | solution.py:44
  61.4 4.7 %collective-permute-done.7.refs_2_ = bf16[64,4096]{1,0:T(8,128)(2,1)S(1)} collective-permute-done((bf16[64,4096]{1,0:T(8,128)(2,1)S(1)}, bf16[64,4096]{1,0:T(8,128)(2,1)S(1)}, u32[]{:S(2)}, u32[]{:S(2)}) %collective-permute-start.7) | collective-permute-done | bytes 524320 | tf_op jit(solution)/shard_map/ppermute | solution.py:44
  66.1 2.4 %project.4.refs_0_ = bf16[4,256,896]{2,1,0:T(8,128)(2,1)S(1)} custom-call(bf16[192,4096]{1,0:T(8,128)(2,1)S(1)} %constant_dynamic-update-slice_fusion.refs_0_, bf16[64,4096]{1,0:T(8,128)(2,1)S(1)} %constant_dynamic-update-slice_fusion.6.refs_1_, bf16[448,4096]{1,0:T(8,128)(2,1)S(1)} %bitcast.60, bf16[448,4096]{1,0:T(8,128)(2,1)S(1)} %bitcast.64), custom_call_target="tpu_custom_call" | custom-call | flops 1879048192 | bytes 7340032 | tf_op jit(solution)/shard_map/project/pallas_call | solution.py:222
  68.6 2.4 %project.5.refs_0_ = bf16[4,256,896]{2,1,0:T(8,128)(2,1)S(1)} custom-call(bf16[4,256,896]{2,1,0:T(8,128)(2,1)S(1)} %project.4.refs_0_, bf16[192,4096]{1,0:T(8,128)(2,1)S(1)} %collective-permute-done.10.refs_1_, bf16[64,4096]{1,0:T(8,128)(2,1)S(1)} %collective-permute-done.11.refs_2_, bf16[448,4096]{1,0:T(8,128)(2,1)S(1)} %bitcast.61, ...), custom_call_target="tpu_custom_call", output_to_operand_aliasing={{}: (0, {})} | custom-call | flops 1879048192 | bytes 7340032 | tf_op jit(solution)/shard_map/project/pallas_call | solution.py:222
  71.0 2.4 %project.6.refs_0_ = bf16[4,256,896]{2,1,0:T(8,128)(2,1)S(1)} custom-call(bf16[4,256,896]{2,1,0:T(8,128)(2,1)S(1)} %project.5.refs_0_, bf16[192,4096]{1,0:T(8,128)(2,1)S(1)} %collective-permute-done.6.refs_1_, bf16[64,4096]{1,0:T(8,128)(2,1)S(1)} %collective-permute-done.12.refs_2_, bf16[448,4096]{1,0:T(8,128)(2,1)S(1)} %bitcast.62, ...), custom_call_target="tpu_custom_call", output_to_operand_aliasing={{}: (0, {})} | custom-call | flops 1879048192 | bytes 7340032 | tf_op jit(solution)/shard_map/project/pallas_call | solution.py:222
  73.5 2.4 %project.7 = bf16[4,256,896]{2,1,0:T(8,128)(2,1)S(1)} custom-call(bf16[4,256,896]{2,1,0:T(8,128)(2,1)S(1)} %project.6.refs_0_, bf16[128,4096]{1,0:T(8,128)(2,1)S(1)} %collective-permute-done.13.refs_1_, bf16[64,4096]{1,0:T(8,128)(2,1)S(1)} %collective-permute-done.7.refs_2_, ...), custom_call_target="tpu_custom_call", output_to_operand_aliasing={{}: (0, {})} | custom-call | flops 1879048192 | bytes 7340032 | tf_op jit(solution)/shard_map/project/pallas_call | solution.py:222
  75.9 6.2 %collective-permute-start.15 = (bf16[4,256,896]{2,1,0:T(8,128)(2,1)S(1)}, bf16[4,256,896]{2,1,0:T(8,128)(2,1)S(1)}, u32[]{:S(2)}, u32[]{:S(2)}) collective-permute-start(bf16[4,256,896]{2,1,0:T(8,128)(2,1)S(1)} %project.7), channel_id=1, source_target_pairs={{0,64},{64,0},{1,65},{65,1},{2,66},{66,2},{3,67},{67,3},{4,68},{68... | collective-permute-start | bytes 5505032 | tf_op jit(solution)/shard_map/ppermute | solution.py:312
  82.1 3.4 %collective-permute-done.15 = bf16[4,256,896]{2,1,0:T(8,128)(2,1)S(1)} collective-permute-done((bf16[4,256,896]{2,1,0:T(8,128)(2,1)S(1)}, bf16[4,256,896]{2,1,0:T(8,128)(2,1)S(1)}, u32[]{:S(2)}, u32[]{:S(2)}) %collective-permute-start.15) | collective-permute-done | bytes 1835040 | tf_op jit(solution)/shard_map/ppermute | solution.py:312
  89.1 2.7 %collective-permute-start.21 = (bf16[128,4096]{1,0:T(8,128)(2,1)S(1)}, bf16[128,4096]{1,0:T(8,128)(2,1)S(1)}, u32[]{:S(2)}, u32[]{:S(2)}) collective-permute-start(bf16[128,4096]{1,0:T(8,128)(2,1)S(1)} %get-tuple-element.30), channel_id=1, source_target_pairs={{0,3},{1,0},{2,1},{3,2},{4,7},{5,4},{6,5},{7,6},{8,11},{9,8},{10,9... | collective-permute-start | bytes 3145736 | tf_op jit(solution)/shard_map/ppermute | solution.py:40
  95.1 9.1 %collective-permute-done.16 = bf16[128,4096]{1,0:T(8,128)(2,1)S(1)} collective-permute-done((bf16[128,4096]{1,0:T(8,128)(2,1)S(1)}, bf16[128,4096]{1,0:T(8,128)(2,1)S(1)}, u32[]{:S(2)}, u32[]{:S(2)}) %collective-permute-start.16) | collective-permute-done | bytes 1048608 | tf_op jit(solution)/shard_map/ppermute | solution.py:40
  105.8 2.7 %collective-permute-start.22 = (bf16[128,4096]{1,0:T(8,128)(2,1)S(1)}, bf16[128,4096]{1,0:T(8,128)(2,1)S(1)}, u32[]{:S(2)}, u32[]{:S(2)}) collective-permute-start(bf16[128,4096]{1,0:T(8,128)(2,1)S(1)} %add_convert_fusion.1), channel_id=1, source_target_pairs={{0,3},{1,0},{2,1},{3,2},{4,7},{5,4},{6,5},{7,6},{8,11},{9,8},{10,9... | collective-permute-start | bytes 3145736 | tf_op jit(solution)/shard_map/ppermute | solution.py:40
  109.8 5.0 %collective-permute-done.18 = bf16[128,4096]{1,0:T(8,128)(2,1)S(1)} collective-permute-done((bf16[128,4096]{1,0:T(8,128)(2,1)S(1)}, bf16[128,4096]{1,0:T(8,128)(2,1)S(1)}, u32[]{:S(2)}, u32[]{:S(2)}) %collective-permute-start.18) | collective-permute-done | bytes 1048608 | tf_op jit(solution)/shard_map/ppermute | solution.py:40
  115.5 11.2 %collective-permute-done.17 = bf16[128,4096]{1,0:T(8,128)(2,1)S(1)} collective-permute-done((bf16[128,4096]{1,0:T(8,128)(2,1)S(1)}, bf16[128,4096]{1,0:T(8,128)(2,1)S(1)}, u32[]{:S(2)}, u32[]{:S(2)}) %collective-permute-start.17) | collective-permute-done | bytes 1048608 | tf_op jit(solution)/shard_map/ppermute | solution.py:40
  129.7 6.5 %collective-permute-done.24 = bf16[64,4096]{1,0:T(8,128)(2,1)S(1)} collective-permute-done((bf16[64,4096]{1,0:T(8,128)(2,1)S(1)}, bf16[64,4096]{1,0:T(8,128)(2,1)S(1)}, u32[]{:S(2)}, u32[]{:S(2)}) %collective-permute-start.24) | collective-permute-done | bytes 524320 | tf_op jit(solution)/shard_map/ppermute | solution.py:40
  136.2 2.2 %collective-permute-done.23 = bf16[64,4096]{1,0:T(8,128)(2,1)S(1)} collective-permute-done((bf16[64,4096]{1,0:T(8,128)(2,1)S(1)}, bf16[64,4096]{1,0:T(8,128)(2,1)S(1)}, u32[]{:S(2)}, u32[]{:S(2)}) %collective-permute-start.23) | collective-permute-done | bytes 524320 | tf_op jit(solution)/shard_map/ppermute | solution.py:40
  138.4 5.6 %collective-permute-done.19 = bf16[64,4096]{1,0:T(8,128)(2,1)S(1)} collective-permute-done((bf16[64,4096]{1,0:T(8,128)(2,1)S(1)}, bf16[64,4096]{1,0:T(8,128)(2,1)S(1)}, u32[]{:S(2)}, u32[]{:S(2)}) %collective-permute-start.19) | collective-permute-done | bytes 524320 | tf_op jit(solution)/shard_map/ppermute | solution.py:40
  145.8 2.3 %collective-permute-done.27 = bf16[16,4096]{1,0:T(8,128)(2,1)S(1)} collective-permute-done((bf16[16,4096]{1,0:T(8,128)(2,1)S(1)}, bf16[16,4096]{1,0:T(8,128)(2,1)S(1)}, u32[]{:S(2)}, u32[]{:S(2)}) %collective-permute-start.27) | collective-permute-done | bytes 131104 | tf_op jit(solution)/shard_map/ppermute | solution.py:40
  148.2 1.7 %collective-permute-done.26 = bf16[16,4096]{1,0:T(8,128)(2,1)S(1)} collective-permute-done((bf16[16,4096]{1,0:T(8,128)(2,1)S(1)}, bf16[16,4096]{1,0:T(8,128)(2,1)S(1)}, u32[]{:S(2)}, u32[]{:S(2)}) %collective-permute-start.26) | collective-permute-done | bytes 131104 | tf_op jit(solution)/shard_map/ppermute | solution.py:40
  149.8 1.6 %collective-permute-done.25 = bf16[16,4096]{1,0:T(8,128)(2,1)S(1)} collective-permute-done((bf16[16,4096]{1,0:T(8,128)(2,1)S(1)}, bf16[16,4096]{1,0:T(8,128)(2,1)S(1)}, u32[]{:S(2)}, u32[]{:S(2)}) %collective-permute-start.25) | collective-permute-done | bytes 131104 | tf_op jit(solution)/shard_map/ppermute | solution.py:40
  151.6 3.1 %collective-permute-start.28 = (bf16[8,4096]{1,0:T(8,128)(2,1)S(1)}, bf16[8,4096]{1,0:T(8,128)(2,1)S(1)}, u32[]{:S(2)}, u32[]{:S(2)}) collective-permute-start(bf16[8,4096]{1,0:T(8,128)(2,1)S(1)} %dynamic-slice_bitcast_fusion), channel_id=1, source_target_pairs={{0,64},{64,0},{1,65},{65,1},{2,66},{66,2},{3,67},{67,3},{4,68},{68... | collective-permute-start | bytes 196616 | tf_op jit(solution)/shard_map/ppermute | solution.py:342
  (73 shorter events, 28.0 us)
Async XLA Ops:
  7.5 2.6 %collective-permute-start = (bf16[32,8,128]{2,1,0:T(8,128)(2,1)}, bf16[32,8,128]{2,1,0:T(8,128)(2,1)S(1)}, u32[]{:S(2)}, u32[]{:S(2)}) collective-permute-start(bf16[32,8,128]{2,1,0:T(8,128)(2,1)} %get-tuple-element.18), channel_id=1, source_target_pairs={{0,64},{64,0},{1,65},{65,1},{2,66},{66,2},{3,67},{67,3},{4,68},{68... | collective-permute-start | bytes 196616 | tf_op jit(solution)/shard_map/ppermute | solution.py:293
  11.0 7.2 %collective-permute-start.1 = (bf16[16,4096]{1,0:T(8,128)(2,1)S(1)}, bf16[16,4096]{1,0:T(8,128)(2,1)S(1)}, u32[]{:S(2)}, u32[]{:S(2)}) collective-permute-start(bf16[16,4096]{1,0:T(8,128)(2,1)S(1)} %maximum_bitcast_fusion), channel_id=1, source_target_pairs={{4,0},{5,1},{6,2},{7,3},{8,4},{9,5},{10,6},{11,7},{12,8},{13,9},{1... | collective-permute-start | bytes 393224 | tf_op jit(solution)/shard_map/ppermute | solution.py:44
  14.9 5.4 %collective-permute-start.2 = (bf16[16,4096]{1,0:T(8,128)(2,1)S(1)}, bf16[16,4096]{1,0:T(8,128)(2,1)S(1)}, u32[]{:S(2)}, u32[]{:S(2)}) collective-permute-start(bf16[16,4096]{1,0:T(8,128)(2,1)S(1)} %maximum_bitcast_fusion), channel_id=1, source_target_pairs={{8,0},{9,1},{10,2},{11,3},{12,4},{13,5},{14,6},{15,7},{0,8},{1,9},... | collective-permute-start | bytes 393224 | tf_op jit(solution)/shard_map/ppermute | solution.py:44
  14.9 6.7 %collective-permute-start.3 = (bf16[16,4096]{1,0:T(8,128)(2,1)S(1)}, bf16[16,4096]{1,0:T(8,128)(2,1)S(1)}, u32[]{:S(2)}, u32[]{:S(2)}) collective-permute-start(bf16[16,4096]{1,0:T(8,128)(2,1)S(1)} %maximum_bitcast_fusion), channel_id=1, source_target_pairs={{12,0},{13,1},{14,2},{15,3},{0,4},{1,5},{2,6},{3,7},{4,8},{5,9},{6... | collective-permute-start | bytes 393224 | tf_op jit(solution)/shard_map/ppermute | solution.py:44
  21.7 8.9 %collective-permute-start.4 = (bf16[64,4096]{1,0:T(8,128)(2,1)S(1)}, bf16[64,4096]{1,0:T(8,128)(2,1)S(1)}, u32[]{:S(2)}, u32[]{:S(2)}) collective-permute-start(bf16[64,4096]{1,0:T(8,128)(2,1)S(1)} %pad_maximum_fusion), channel_id=1, source_target_pairs={{16,0},{17,1},{18,2},{19,3},{20,4},{21,5},{22,6},{23,7},{24,8},{25... | collective-permute-start | bytes 1572872 | tf_op jit(solution)/shard_map/ppermute | solution.py:44
  24.5 9.5 %collective-permute-start.5 = (bf16[64,4096]{1,0:T(8,128)(2,1)S(1)}, bf16[64,4096]{1,0:T(8,128)(2,1)S(1)}, u32[]{:S(2)}, u32[]{:S(2)}) collective-permute-start(bf16[64,4096]{1,0:T(8,128)(2,1)S(1)} %pad_maximum_fusion), channel_id=1, source_target_pairs={{48,0},{49,1},{50,2},{51,3},{52,4},{53,5},{54,6},{55,7},{56,8},{57... | collective-permute-start | bytes 1572872 | tf_op jit(solution)/shard_map/ppermute | solution.py:44
  30.6 35.5 %copy-start.1 = (bf16[4096,448]{0,1:T(8,128)(2,1)S(1)}, bf16[4096,448]{0,1:T(8,128)(2,1)}, u32[]{:S(2)}) copy-start(bf16[4096,448]{0,1:T(8,128)(2,1)} %param.20) | copy-start | bytes 11010052
  34.1 20.8 %collective-permute-start.6 = (bf16[192,4096]{1,0:T(8,128)(2,1)S(1)}, bf16[192,4096]{1,0:T(8,128)(2,1)S(1)}, u32[]{:S(2)}, u32[]{:S(2)}) collective-permute-start(bf16[192,4096]{1,0:T(8,128)(2,1)S(1)} %constant_dynamic-update-slice_fusion.refs_0_), channel_id=1, source_target_pairs={{3,0},{0,1},{1,2},{2,3},{7,4},{4,5},{5,6},{6,7},{11,8},{8,9},{9,10... | collective-permute-start | bytes 4718600 | tf_op jit(solution)/shard_map/ppermute | solution.py:44
  35.0 20.0 %collective-permute-start.10 = (bf16[192,4096]{1,0:T(8,128)(2,1)S(1)}, bf16[192,4096]{1,0:T(8,128)(2,1)S(1)}, u32[]{:S(2)}, u32[]{:S(2)}) collective-permute-start(bf16[192,4096]{1,0:T(8,128)(2,1)S(1)} %constant_dynamic-update-slice_fusion.refs_0_), channel_id=1, source_target_pairs={{1,0},{2,1},{3,2},{0,3},{5,4},{6,5},{7,6},{4,7},{9,8},{10,9},{11,1... | collective-permute-start | bytes 4718600 | tf_op jit(solution)/shard_map/ppermute | solution.py:44
  36.8 6.4 %collective-permute-start.8 = (bf16[32,4096]{1,0:T(8,128)(2,1)S(1)}, bf16[32,4096]{1,0:T(8,128)(2,1)S(1)}, u32[]{:S(2)}, u32[]{:S(2)}) collective-permute-start(bf16[32,4096]{1,0:T(8,128)(2,1)S(1)} %slice.99), channel_id=1, source_target_pairs={{16,0},{17,1},{18,2},{19,3},{20,4},{21,5},{22,6},{23,7},{24,8},{25... | collective-permute-start | bytes 786440 | tf_op jit(solution)/shard_map/ppermute | solution.py:44
  37.0 29.2 %copy-start = (bf16[4096,448]{0,1:T(8,128)(2,1)S(1)}, bf16[4096,448]{0,1:T(8,128)(2,1)}, u32[]{:S(2)}) copy-start(bf16[4096,448]{0,1:T(8,128)(2,1)} %param.19) | copy-start | bytes 11010052
  37.0 9.4 %collective-permute-start.9 = (bf16[32,4096]{1,0:T(8,128)(2,1)S(1)}, bf16[32,4096]{1,0:T(8,128)(2,1)S(1)}, u32[]{:S(2)}, u32[]{:S(2)}) collective-permute-start(bf16[32,4096]{1,0:T(8,128)(2,1)S(1)} %slice.100), channel_id=1, source_target_pairs={{48,0},{49,1},{50,2},{51,3},{52,4},{53,5},{54,6},{55,7},{56,8},{57... | collective-permute-start | bytes 786440 | tf_op jit(solution)/shard_map/ppermute | solution.py:44
  46.4 13.8 %collective-permute-start.11 = (bf16[64,4096]{1,0:T(8,128)(2,1)S(1)}, bf16[64,4096]{1,0:T(8,128)(2,1)S(1)}, u32[]{:S(2)}, u32[]{:S(2)}) collective-permute-start(bf16[64,4096]{1,0:T(8,128)(2,1)S(1)} %constant_dynamic-update-slice_fusion.6.refs_1_), channel_id=1, source_target_pairs={{1,0},{2,1},{3,2},{0,3},{5,4},{6,5},{7,6},{4,7},{9,8},{10,9},{11,1... | collective-permute-start | bytes 1572872 | tf_op jit(solution)/shard_map/ppermute | solution.py:44
  47.6 12.9 %collective-permute-start.12 = (bf16[64,4096]{1,0:T(8,128)(2,1)S(1)}, bf16[64,4096]{1,0:T(8,128)(2,1)S(1)}, u32[]{:S(2)}, u32[]{:S(2)}) collective-permute-start(bf16[64,4096]{1,0:T(8,128)(2,1)S(1)} %constant_dynamic-update-slice_fusion.6.refs_1_), channel_id=1, source_target_pairs={{3,0},{0,1},{1,2},{2,3},{7,4},{4,5},{5,6},{6,7},{11,8},{8,9},{9,10... | collective-permute-start | bytes 1572872 | tf_op jit(solution)/shard_map/ppermute | solution.py:44
  54.9 11.2 %collective-permute-start.7 = (bf16[64,4096]{1,0:T(8,128)(2,1)S(1)}, bf16[64,4096]{1,0:T(8,128)(2,1)S(1)}, u32[]{:S(2)}, u32[]{:S(2)}) collective-permute-start(bf16[64,4096]{1,0:T(8,128)(2,1)S(1)} %slice.98), channel_id=1, source_target_pairs={{3,0},{0,1},{1,2},{2,3},{7,4},{4,5},{5,6},{6,7},{11,8},{8,9},{9,10... | collective-permute-start | bytes 1572872 | tf_op jit(solution)/shard_map/ppermute | solution.py:44
  55.1 18.4 %collective-permute-start.13 = (bf16[128,4096]{1,0:T(8,128)(2,1)S(1)}, bf16[128,4096]{1,0:T(8,128)(2,1)S(1)}, u32[]{:S(2)}, u32[]{:S(2)}) collective-permute-start(bf16[128,4096]{1,0:T(8,128)(2,1)S(1)} %slice.101), channel_id=1, source_target_pairs={{1,0},{2,1},{3,2},{0,3},{5,4},{6,5},{7,6},{4,7},{9,8},{10,9},{11,1... | collective-permute-start | bytes 3145736 | tf_op jit(solution)/shard_map/ppermute | solution.py:44
  60.5 12.9 %collective-permute-start.14 = (bf16[64,4096]{1,0:T(8,128)(2,1)S(1)}, bf16[64,4096]{1,0:T(8,128)(2,1)S(1)}, u32[]{:S(2)}, u32[]{:S(2)}) collective-permute-start(bf16[64,4096]{1,0:T(8,128)(2,1)S(1)} %collective-permute-done.12.refs_2_), channel_id=1, source_target_pairs={{3,0},{0,1},{1,2},{2,3},{7,4},{4,5},{5,6},{6,7},{11,8},{8,9},{9,10... | collective-permute-start | bytes 1572872 | tf_op jit(solution)/shard_map/ppermute | solution.py:44
  75.9 9.6 %collective-permute-start.15 = (bf16[4,256,896]{2,1,0:T(8,128)(2,1)S(1)}, bf16[4,256,896]{2,1,0:T(8,128)(2,1)S(1)}, u32[]{:S(2)}, u32[]{:S(2)}) collective-permute-start(bf16[4,256,896]{2,1,0:T(8,128)(2,1)S(1)} %project.7), channel_id=1, source_target_pairs={{0,64},{64,0},{1,65},{65,1},{2,66},{66,2},{3,67},{67,3},{4,68},{68... | collective-permute-start | bytes 5505032 | tf_op jit(solution)/shard_map/ppermute | solution.py:312
  89.0 15.2 %collective-permute-start.16 = (bf16[128,4096]{1,0:T(8,128)(2,1)S(1)}, bf16[128,4096]{1,0:T(8,128)(2,1)S(1)}, u32[]{:S(2)}, u32[]{:S(2)}) collective-permute-start(bf16[128,4096]{1,0:T(8,128)(2,1)S(1)} %get-tuple-element.29), channel_id=1, source_target_pairs={{0,1},{1,2},{2,3},{3,0},{4,5},{5,6},{6,7},{7,4},{8,9},{9,10},{10,1... | collective-permute-start | bytes 3145736 | tf_op jit(solution)/shard_map/ppermute | solution.py:40
  89.1 15.9 %collective-permute-start.21 = (bf16[128,4096]{1,0:T(8,128)(2,1)S(1)}, bf16[128,4096]{1,0:T(8,128)(2,1)S(1)}, u32[]{:S(2)}, u32[]{:S(2)}) collective-permute-start(bf16[128,4096]{1,0:T(8,128)(2,1)S(1)} %get-tuple-element.30), channel_id=1, source_target_pairs={{0,3},{1,0},{2,1},{3,2},{4,7},{5,4},{6,5},{7,6},{8,11},{9,8},{10,9... | collective-permute-start | bytes 3145736 | tf_op jit(solution)/shard_map/ppermute | solution.py:40
  92.6 22.3 %collective-permute-start.18 = (bf16[128,4096]{1,0:T(8,128)(2,1)S(1)}, bf16[128,4096]{1,0:T(8,128)(2,1)S(1)}, u32[]{:S(2)}, u32[]{:S(2)}) collective-permute-start(bf16[128,4096]{1,0:T(8,128)(2,1)S(1)} %convolution_convert_fusion.4), channel_id=1, source_target_pairs={{0,3},{1,0},{2,1},{3,2},{4,7},{5,4},{6,5},{7,6},{8,11},{9,8},{10,9... | collective-permute-start | bytes 3145736 | tf_op jit(solution)/shard_map/ppermute | solution.py:40
  93.6 21.9 %collective-permute-start.20 = (bf16[128,4096]{1,0:T(8,128)(2,1)S(1)}, bf16[128,4096]{1,0:T(8,128)(2,1)S(1)}, u32[]{:S(2)}, u32[]{:S(2)}) collective-permute-start(bf16[128,4096]{1,0:T(8,128)(2,1)S(1)} %convolution_convert_fusion.3), channel_id=1, source_target_pairs={{0,1},{1,2},{2,3},{3,0},{4,5},{5,6},{6,7},{7,4},{8,9},{9,10},{10,1... | collective-permute-start | bytes 3145736 | tf_op jit(solution)/shard_map/ppermute | solution.py:40
  105.0 21.7 %collective-permute-start.17 = (bf16[128,4096]{1,0:T(8,128)(2,1)S(1)}, bf16[128,4096]{1,0:T(8,128)(2,1)S(1)}, u32[]{:S(2)}, u32[]{:S(2)}) collective-permute-start(bf16[128,4096]{1,0:T(8,128)(2,1)S(1)} %add_convert_fusion.3), channel_id=1, source_target_pairs={{0,1},{1,2},{2,3},{3,0},{4,5},{5,6},{6,7},{7,4},{8,9},{9,10},{10,1... | collective-permute-start | bytes 3145736 | tf_op jit(solution)/shard_map/ppermute | solution.py:40
  105.8 20.9 %collective-permute-start.22 = (bf16[128,4096]{1,0:T(8,128)(2,1)S(1)}, bf16[128,4096]{1,0:T(8,128)(2,1)S(1)}, u32[]{:S(2)}, u32[]{:S(2)}) collective-permute-start(bf16[128,4096]{1,0:T(8,128)(2,1)S(1)} %add_convert_fusion.1), channel_id=1, source_target_pairs={{0,3},{1,0},{2,1},{3,2},{4,7},{5,4},{6,5},{7,6},{8,11},{9,8},{10,9... | collective-permute-start | bytes 3145736 | tf_op jit(solution)/shard_map/ppermute | solution.py:40
  127.8 8.4 %collective-permute-start.24 = (bf16[64,4096]{1,0:T(8,128)(2,1)S(1)}, bf16[64,4096]{1,0:T(8,128)(2,1)S(1)}, u32[]{:S(2)}, u32[]{:S(2)}) collective-permute-start(bf16[64,4096]{1,0:T(8,128)(2,1)S(1)} %get-tuple-element.36), channel_id=1, source_target_pairs={{0,48},{1,49},{2,50},{3,51},{4,52},{5,53},{6,54},{7,55},{8,56},{9,... | collective-permute-start | bytes 1572872 | tf_op jit(solution)/shard_map/ppermute | solution.py:40
  128.5 9.9 %collective-permute-start.23 = (bf16[64,4096]{1,0:T(8,128)(2,1)S(1)}, bf16[64,4096]{1,0:T(8,128)(2,1)S(1)}, u32[]{:S(2)}, u32[]{:S(2)}) collective-permute-start(bf16[64,4096]{1,0:T(8,128)(2,1)S(1)} %get-tuple-element.35), channel_id=1, source_target_pairs={{0,32},{1,33},{2,34},{3,35},{4,36},{5,37},{6,38},{7,39},{8,40},{9,... | collective-permute-start | bytes 1572872 | tf_op jit(solution)/shard_map/ppermute | solution.py:40
  129.6 26.0 %copy-start.3 = (f32[64,8,128]{2,1,0:T(8,128)S(1)}, f32[64,8,128]{2,1,0:T(8,128)}, u32[]{:S(2)}) copy-start(f32[64,8,128]{2,1,0:T(8,128)} %get-tuple-element.16) | copy-start | bytes 786436
  129.6 14.4 %collective-permute-start.19 = (bf16[64,4096]{1,0:T(8,128)(2,1)S(1)}, bf16[64,4096]{1,0:T(8,128)(2,1)S(1)}, u32[]{:S(2)}, u32[]{:S(2)}) collective-permute-start(bf16[64,4096]{1,0:T(8,128)(2,1)S(1)} %slice.109), channel_id=1, source_target_pairs={{0,16},{1,17},{2,18},{3,19},{4,20},{5,21},{6,22},{7,23},{8,24},{9,... | collective-permute-start | bytes 1572872 | tf_op jit(solution)/shard_map/ppermute | solution.py:40
  144.3 3.9 %collective-permute-start.27 = (bf16[16,4096]{1,0:T(8,128)(2,1)S(1)}, bf16[16,4096]{1,0:T(8,128)(2,1)S(1)}, u32[]{:S(2)}, u32[]{:S(2)}) collective-permute-start(bf16[16,4096]{1,0:T(8,128)(2,1)S(1)} %get-tuple-element.40), channel_id=1, source_target_pairs={{0,12},{1,13},{2,14},{3,15},{4,0},{5,1},{6,2},{7,3},{8,4},{9,5},{1... | collective-permute-start | bytes 393224 | tf_op jit(solution)/shard_map/ppermute | solution.py:40
  144.4 5.5 %collective-permute-start.26 = (bf16[16,4096]{1,0:T(8,128)(2,1)S(1)}, bf16[16,4096]{1,0:T(8,128)(2,1)S(1)}, u32[]{:S(2)}, u32[]{:S(2)}) collective-permute-start(bf16[16,4096]{1,0:T(8,128)(2,1)S(1)} %get-tuple-element.41), channel_id=1, source_target_pairs={{0,8},{1,9},{2,10},{3,11},{4,12},{5,13},{6,14},{7,15},{8,0},{9,1},... | collective-permute-start | bytes 393224 | tf_op jit(solution)/shard_map/ppermute | solution.py:40
  144.5 7.0 %collective-permute-start.25 = (bf16[16,4096]{1,0:T(8,128)(2,1)S(1)}, bf16[16,4096]{1,0:T(8,128)(2,1)S(1)}, u32[]{:S(2)}, u32[]{:S(2)}) collective-permute-start(bf16[16,4096]{1,0:T(8,128)(2,1)S(1)} %get-tuple-element.39), channel_id=1, source_target_pairs={{0,4},{1,5},{2,6},{3,7},{4,8},{5,9},{6,10},{7,11},{8,12},{9,13},{1... | collective-permute-start | bytes 393224 | tf_op jit(solution)/shard_map/ppermute | solution.py:40
  151.6 4.0 %collective-permute-start.28 = (bf16[8,4096]{1,0:T(8,128)(2,1)S(1)}, bf16[8,4096]{1,0:T(8,128)(2,1)S(1)}, u32[]{:S(2)}, u32[]{:S(2)}) collective-permute-start(bf16[8,4096]{1,0:T(8,128)(2,1)S(1)} %dynamic-slice_bitcast_fusion), channel_id=1, source_target_pairs={{0,64},{64,0},{1,65},{65,1},{2,66},{66,2},{3,67},{67,3},{4,68},{68... | collective-permute-start | bytes 196616 | tf_op jit(solution)/shard_map/ppermute | solution.py:342
  (1 other events, 2.0 us)

commit v5 on v4

--- a/solution.py
+++ b/solution.py
@@ -306,7 +306,7 @@
     found = None
     for place, third in enumerate(ORDER):
         runs = blocks[third]
-        if place == 0:
+        if place == 1:
             runs = [behind(run, blocks[FAR][1]) for run in runs]
         found = project(found, place, RING, runs, *weights)
     halves = [found, lax.ppermute(found, "side", SWAP)]

time: 157 us -> 157 us (level)
  starting transfers between devices: 38.6 us -> 41 us
    ppermute x1, starting transfers between devices: 3.12 us -> 6.09 us  [body(): lax.ppermute(lax.dynamic_index_in_dim(by_side, 1 - side, 0, keepdims=Fals...]
    ppermute x1, starting transfers between devices: 6.21 us -> 4.42 us  [body(): halves = [found, lax.ppermute(found, 'side', SWAP)]]
where the time goes in v5:
time: 157 us
  waiting for transfers between devices  87.5 us (56%)
  starting transfers between devices  41 us (26%)
  Pallas kernels  18.3 us (12%)
  matrix products  5.41 us (3%)
  other arithmetic  2.98 us (2%)
    ppermute x12, waiting for transfers between devices, send(): return lax.ppermute(array, ('side', 'gx'), hops(line, distance))  45.3 us
    ppermute x14, waiting for transfers between devices, fetch(): lax.ppermute(array, ('side', 'gx'), [(there, here) for here, there in hop...  36.7 us
    ppermute x14, starting transfers between devices, fetch(): lax.ppermute(array, ('side', 'gx'), [(there, here) for here, there in hop...  18.4 us
    ppermute x12, starting transfers between devices, send(): return lax.ppermute(array, ('side', 'gx'), hops(line, distance))  10.6 us
    pallas_call x4, Pallas kernels, project(): pl.pallas_call(functools.partial(project_kernel, len(runs)), grid=(1,), i...  9.7 us
    pallas_call x1, Pallas kernels, attend(): pl.pallas_call(attend_kernel, in_specs=[smem, smem] + [vmem] * 5 + [pl.Bl...  7.5 us
    ppermute x1, starting transfers between devices, body(): lax.ppermute(lax.dynamic_index_in_dim(by_side, 1 - side, 0, keepdims=Fals...  6.09 us
    dot_general x6, matrix products, dot(): return jnp.dot(left, right, preferred_element_type=jnp.float32)  5.41 us
  transfers between devices with their start and end apart: 29, of which 24 were waited for; matrix products, arithmetic and copies ran while one was open for 3% of the time, Pallas kernels for 5%

profile of v5, /device:TPU:1, one launch (start us, length us, event | category | flops | bytes accessed | tf_op | source)
XLA Modules:
  0.0 157.1 jit_solution(12003046524892233603)
XLA Ops:
  0.0 7.5 %attend.1 = (f32[64,8,128]{2,1,0:T(8,128)}, bf16[32,8,128]{2,1,0:T(8,128)(2,1)}, bf16[32,8,128]{2,1,0:T(8,128)(2,1)}) custom-call(s32[1]{0:T(128)} %bitcast.side_ref, s32[8]{0:T(128)} %lengths_ref.1, bf16[64,8,128]{2,1,0:T(8,128)(2,1)} %bitcast.77, bf16[8,8,128]{2,1,0:T(8,128)(2,1)} %bitcast.79, bf16[8,8,128]{2,1,0:T(8,128)(2,1)} %bitcast.80, ...), custom_call_target="tpu_custom_call" | custom-call | tf_op jit(solution)/shard_map/attend/pallas_call | solution.py:176
  11.0 3.9 %collective-permute-start.1 = (bf16[16,4096]{1,0:T(8,128)(2,1)S(1)}, bf16[16,4096]{1,0:T(8,128)(2,1)S(1)}, u32[]{:S(2)}, u32[]{:S(2)}) collective-permute-start(bf16[16,4096]{1,0:T(8,128)(2,1)S(1)} %maximum_bitcast_fusion), channel_id=1, source_target_pairs={{4,0},{5,1},{6,2},{7,3},{8,4},{9,5},{10,6},{11,7},{12,8},{13,9},{1... | collective-permute-start | bytes 393224 | tf_op jit(solution)/shard_map/ppermute | solution.py:44
  15.6 2.6 %collective-permute-done.1 = bf16[16,4096]{1,0:T(8,128)(2,1)S(1)} collective-permute-done((bf16[16,4096]{1,0:T(8,128)(2,1)S(1)}, bf16[16,4096]{1,0:T(8,128)(2,1)S(1)}, u32[]{:S(2)}, u32[]{:S(2)}) %collective-permute-start.1) | collective-permute-done | bytes 131104 | tf_op jit(solution)/shard_map/ppermute | solution.py:44
  18.2 2.1 %collective-permute-done.2 = bf16[16,4096]{1,0:T(8,128)(2,1)S(1)} collective-permute-done((bf16[16,4096]{1,0:T(8,128)(2,1)S(1)}, bf16[16,4096]{1,0:T(8,128)(2,1)S(1)}, u32[]{:S(2)}, u32[]{:S(2)}) %collective-permute-start.2) | collective-permute-done | bytes 131104 | tf_op jit(solution)/shard_map/ppermute | solution.py:44
  21.7 2.8 %collective-permute-start.4 = (bf16[64,4096]{1,0:T(8,128)(2,1)S(1)}, bf16[64,4096]{1,0:T(8,128)(2,1)S(1)}, u32[]{:S(2)}, u32[]{:S(2)}) collective-permute-start(bf16[64,4096]{1,0:T(8,128)(2,1)S(1)} %pad_maximum_fusion), channel_id=1, source_target_pairs={{16,0},{17,1},{18,2},{19,3},{20,4},{21,5},{22,6},{23,7},{24,8},{25... | collective-permute-start | bytes 1572872 | tf_op jit(solution)/shard_map/ppermute | solution.py:44
  24.5 6.1 %collective-permute-done.4 = bf16[64,4096]{1,0:T(8,128)(2,1)S(1)} collective-permute-done((bf16[64,4096]{1,0:T(8,128)(2,1)S(1)}, bf16[64,4096]{1,0:T(8,128)(2,1)S(1)}, u32[]{:S(2)}, u32[]{:S(2)}) %collective-permute-start.4) | collective-permute-done | bytes 524320 | tf_op jit(solution)/shard_map/ppermute | solution.py:44
  30.6 3.4 %collective-permute-done.5 = bf16[64,4096]{1,0:T(8,128)(2,1)S(1)} collective-permute-done((bf16[64,4096]{1,0:T(8,128)(2,1)S(1)}, bf16[64,4096]{1,0:T(8,128)(2,1)S(1)}, u32[]{:S(2)}, u32[]{:S(2)}) %collective-permute-start.5) | collective-permute-done | bytes 524320 | tf_op jit(solution)/shard_map/ppermute | solution.py:44
  34.1 2.3 %collective-permute-start.8 = (bf16[192,4096]{1,0:T(8,128)(2,1)S(1)}, bf16[192,4096]{1,0:T(8,128)(2,1)S(1)}, u32[]{:S(2)}, u32[]{:S(2)}) collective-permute-start(bf16[192,4096]{1,0:T(8,128)(2,1)S(1)} %constant_dynamic-update-slice_fusion.refs_0_), channel_id=1, source_target_pairs={{1,0},{2,1},{3,2},{0,3},{5,4},{6,5},{7,6},{4,7},{9,8},{10,9},{11,1... | collective-permute-start | bytes 4718600 | tf_op jit(solution)/shard_map/ppermute | solution.py:44
  38.0 5.9 %collective-permute-done.6 = bf16[32,4096]{1,0:T(8,128)(2,1)S(1)} collective-permute-done((bf16[32,4096]{1,0:T(8,128)(2,1)S(1)}, bf16[32,4096]{1,0:T(8,128)(2,1)S(1)}, u32[]{:S(2)}, u32[]{:S(2)}) %collective-permute-start.6) | collective-permute-done | bytes 262176 | tf_op jit(solution)/shard_map/ppermute | solution.py:44
  44.0 3.6 %collective-permute-start.11 = (bf16[64,4096]{1,0:T(8,128)(2,1)S(1)}, bf16[64,4096]{1,0:T(8,128)(2,1)S(1)}, u32[]{:S(2)}, u32[]{:S(2)}) collective-permute-start(bf16[64,4096]{1,0:T(8,128)(2,1)S(1)} %constant_dynamic-update-slice_fusion.6.refs_1_), channel_id=1, source_target_pairs={{1,0},{2,1},{3,2},{0,3},{5,4},{6,5},{7,6},{4,7},{9,8},{10,9},{11,1... | collective-permute-start | bytes 1572872 | tf_op jit(solution)/shard_map/ppermute | solution.py:44
  47.6 6.1 %collective-permute-done.8.refs_1_ = bf16[192,4096]{1,0:T(8,128)(2,1)S(1)} collective-permute-done((bf16[192,4096]{1,0:T(8,128)(2,1)S(1)}, bf16[192,4096]{1,0:T(8,128)(2,1)S(1)}, u32[]{:S(2)}, u32[]{:S(2)}) %collective-permute-start.8) | collective-permute-done | bytes 1572896 | tf_op jit(solution)/shard_map/ppermute | solution.py:44
  53.8 3.5 %collective-permute-start.13 = (bf16[128,4096]{1,0:T(8,128)(2,1)S(1)}, bf16[128,4096]{1,0:T(8,128)(2,1)S(1)}, u32[]{:S(2)}, u32[]{:S(2)}) collective-permute-start(bf16[128,4096]{1,0:T(8,128)(2,1)S(1)} %slice.101), channel_id=1, source_target_pairs={{1,0},{2,1},{3,2},{0,3},{5,4},{6,5},{7,6},{4,7},{9,8},{10,9},{11,1... | collective-permute-start | bytes 3145736 | tf_op jit(solution)/shard_map/ppermute | solution.py:44
  57.4 1.9 %collective-permute-done.11.refs_2_ = bf16[64,4096]{1,0:T(8,128)(2,1)S(1)} collective-permute-done((bf16[64,4096]{1,0:T(8,128)(2,1)S(1)}, bf16[64,4096]{1,0:T(8,128)(2,1)S(1)}, u32[]{:S(2)}, u32[]{:S(2)}) %collective-permute-start.11) | collective-permute-done | bytes 524320 | tf_op jit(solution)/shard_map/ppermute | solution.py:44
  59.3 3.4 %collective-permute-done.12.refs_2_ = bf16[64,4096]{1,0:T(8,128)(2,1)S(1)} collective-permute-done((bf16[64,4096]{1,0:T(8,128)(2,1)S(1)}, bf16[64,4096]{1,0:T(8,128)(2,1)S(1)}, u32[]{:S(2)}, u32[]{:S(2)}) %collective-permute-start.12) | collective-permute-done | bytes 524320 | tf_op jit(solution)/shard_map/ppermute | solution.py:44
  62.7 2.4 %project.4.refs_0_ = bf16[4,256,896]{2,1,0:T(8,128)(2,1)S(1)} custom-call(bf16[192,4096]{1,0:T(8,128)(2,1)S(1)} %constant_dynamic-update-slice_fusion.refs_0_, bf16[64,4096]{1,0:T(8,128)(2,1)S(1)} %constant_dynamic-update-slice_fusion.6.refs_1_, bf16[448,4096]{1,0:T(8,128)(2,1)S(1)} %bitcast.60, bf16[448,4096]{1,0:T(8,128)(2,1)S(1)} %bitcast.64), custom_call_target="tpu_custom_call" | custom-call | flops 1879048192 | bytes 7340032 | tf_op jit(solution)/shard_map/project/pallas_call | solution.py:222
  65.2 3.2 %collective-permute-done.10.refs_2_ = bf16[64,4096]{1,0:T(8,128)(2,1)S(1)} collective-permute-done((bf16[64,4096]{1,0:T(8,128)(2,1)S(1)}, bf16[64,4096]{1,0:T(8,128)(2,1)S(1)}, u32[]{:S(2)}, u32[]{:S(2)}) %collective-permute-start.10) | collective-permute-done | bytes 524320 | tf_op jit(solution)/shard_map/ppermute | solution.py:44
  68.3 2.4 %project.5.refs_0_ = bf16[4,256,896]{2,1,0:T(8,128)(2,1)S(1)} custom-call(bf16[4,256,896]{2,1,0:T(8,128)(2,1)S(1)} %project.4.refs_0_, bf16[192,4096]{1,0:T(8,128)(2,1)S(1)} %collective-permute-done.8.refs_1_, bf16[64,4096]{1,0:T(8,128)(2,1)S(1)} %collective-permute-done.11.refs_2_, bf16[448,4096]{1,0:T(8,128)(2,1)S(1)} %bitcast.61, ...), custom_call_target="tpu_custom_call", output_to_operand_aliasing={{}: (0, {})} | custom-call | flops 1879048192 | bytes 7340032 | tf_op jit(solution)/shard_map/project/pallas_call | solution.py:222
  70.8 2.4 %project.6.refs_0_ = bf16[4,256,896]{2,1,0:T(8,128)(2,1)S(1)} custom-call(bf16[4,256,896]{2,1,0:T(8,128)(2,1)S(1)} %project.5.refs_0_, bf16[192,4096]{1,0:T(8,128)(2,1)S(1)} %collective-permute-done.9.refs_1_, bf16[64,4096]{1,0:T(8,128)(2,1)S(1)} %collective-permute-done.12.refs_2_, bf16[448,4096]{1,0:T(8,128)(2,1)S(1)} %bitcast.62, ...), custom_call_target="tpu_custom_call", output_to_operand_aliasing={{}: (0, {})} | custom-call | flops 1879048192 | bytes 7340032 | tf_op jit(solution)/shard_map/project/pallas_call | solution.py:222
  73.9 2.4 %project.7 = bf16[4,256,896]{2,1,0:T(8,128)(2,1)S(1)} custom-call(bf16[4,256,896]{2,1,0:T(8,128)(2,1)S(1)} %project.6.refs_0_, bf16[128,4096]{1,0:T(8,128)(2,1)S(1)} %collective-permute-done.13.refs_1_, bf16[64,4096]{1,0:T(8,128)(2,1)S(1)} %collective-permute-done.10.refs_2_, ...), custom_call_target="tpu_custom_call", output_to_operand_aliasing={{}: (0, {})} | custom-call | flops 1879048192 | bytes 7340032 | tf_op jit(solution)/shard_map/project/pallas_call | solution.py:222
  76.4 4.4 %collective-permute-start.15 = (bf16[4,256,896]{2,1,0:T(8,128)(2,1)S(1)}, bf16[4,256,896]{2,1,0:T(8,128)(2,1)S(1)}, u32[]{:S(2)}, u32[]{:S(2)}) collective-permute-start(bf16[4,256,896]{2,1,0:T(8,128)(2,1)S(1)} %project.7), channel_id=1, source_target_pairs={{0,64},{64,0},{1,65},{65,1},{2,66},{66,2},{3,67},{67,3},{4,68},{68... | collective-permute-start | bytes 5505032 | tf_op jit(solution)/shard_map/ppermute | solution.py:312
  80.8 3.4 %collective-permute-done.15 = bf16[4,256,896]{2,1,0:T(8,128)(2,1)S(1)} collective-permute-done((bf16[4,256,896]{2,1,0:T(8,128)(2,1)S(1)}, bf16[4,256,896]{2,1,0:T(8,128)(2,1)S(1)}, u32[]{:S(2)}, u32[]{:S(2)}) %collective-permute-start.15) | collective-permute-done | bytes 1835040 | tf_op jit(solution)/shard_map/ppermute | solution.py:312
  87.8 2.7 %collective-permute-start.21 = (bf16[128,4096]{1,0:T(8,128)(2,1)S(1)}, bf16[128,4096]{1,0:T(8,128)(2,1)S(1)}, u32[]{:S(2)}, u32[]{:S(2)}) collective-permute-start(bf16[128,4096]{1,0:T(8,128)(2,1)S(1)} %get-tuple-element.30), channel_id=1, source_target_pairs={{0,3},{1,0},{2,1},{3,2},{4,7},{5,4},{6,5},{7,6},{8,11},{9,8},{10,9... | collective-permute-start | bytes 3145736 | tf_op jit(solution)/shard_map/ppermute | solution.py:40
  93.8 9.1 %collective-permute-done.16 = bf16[128,4096]{1,0:T(8,128)(2,1)S(1)} collective-permute-done((bf16[128,4096]{1,0:T(8,128)(2,1)S(1)}, bf16[128,4096]{1,0:T(8,128)(2,1)S(1)}, u32[]{:S(2)}, u32[]{:S(2)}) %collective-permute-start.16) | collective-permute-done | bytes 1048608 | tf_op jit(solution)/shard_map/ppermute | solution.py:40
  104.5 2.7 %collective-permute-start.22 = (bf16[128,4096]{1,0:T(8,128)(2,1)S(1)}, bf16[128,4096]{1,0:T(8,128)(2,1)S(1)}, u32[]{:S(2)}, u32[]{:S(2)}) collective-permute-start(bf16[128,4096]{1,0:T(8,128)(2,1)S(1)} %add_convert_fusion.1), channel_id=1, source_target_pairs={{0,3},{1,0},{2,1},{3,2},{4,7},{5,4},{6,5},{7,6},{8,11},{9,8},{10,9... | collective-permute-start | bytes 3145736 | tf_op jit(solution)/shard_map/ppermute | solution.py:40
  108.5 5.0 %collective-permute-done.18 = bf16[128,4096]{1,0:T(8,128)(2,1)S(1)} collective-permute-done((bf16[128,4096]{1,0:T(8,128)(2,1)S(1)}, bf16[128,4096]{1,0:T(8,128)(2,1)S(1)}, u32[]{:S(2)}, u32[]{:S(2)}) %collective-permute-start.18) | collective-permute-done | bytes 1048608 | tf_op jit(solution)/shard_map/ppermute | solution.py:40
  114.1 11.2 %collective-permute-done.17 = bf16[128,4096]{1,0:T(8,128)(2,1)S(1)} collective-permute-done((bf16[128,4096]{1,0:T(8,128)(2,1)S(1)}, bf16[128,4096]{1,0:T(8,128)(2,1)S(1)}, u32[]{:S(2)}, u32[]{:S(2)}) %collective-permute-start.17) | collective-permute-done | bytes 1048608 | tf_op jit(solution)/shard_map/ppermute | solution.py:40
  128.1 6.7 %collective-permute-done.24 = bf16[64,4096]{1,0:T(8,128)(2,1)S(1)} collective-permute-done((bf16[64,4096]{1,0:T(8,128)(2,1)S(1)}, bf16[64,4096]{1,0:T(8,128)(2,1)S(1)}, u32[]{:S(2)}, u32[]{:S(2)}) %collective-permute-start.24) | collective-permute-done | bytes 524320 | tf_op jit(solution)/shard_map/ppermute | solution.py:40
  134.9 1.6 %collective-permute-done.23 = bf16[64,4096]{1,0:T(8,128)(2,1)S(1)} collective-permute-done((bf16[64,4096]{1,0:T(8,128)(2,1)S(1)}, bf16[64,4096]{1,0:T(8,128)(2,1)S(1)}, u32[]{:S(2)}, u32[]{:S(2)}) %collective-permute-start.23) | collective-permute-done | bytes 524320 | tf_op jit(solution)/shard_map/ppermute | solution.py:40
  136.5 5.6 %collective-permute-done.19 = bf16[64,4096]{1,0:T(8,128)(2,1)S(1)} collective-permute-done((bf16[64,4096]{1,0:T(8,128)(2,1)S(1)}, bf16[64,4096]{1,0:T(8,128)(2,1)S(1)}, u32[]{:S(2)}, u32[]{:S(2)}) %collective-permute-start.19) | collective-permute-done | bytes 524320 | tf_op jit(solution)/shard_map/ppermute | solution.py:40
  143.9 2.3 %collective-permute-done.27 = bf16[16,4096]{1,0:T(8,128)(2,1)S(1)} collective-permute-done((bf16[16,4096]{1,0:T(8,128)(2,1)S(1)}, bf16[16,4096]{1,0:T(8,128)(2,1)S(1)}, u32[]{:S(2)}, u32[]{:S(2)}) %collective-permute-start.27) | collective-permute-done | bytes 131104 | tf_op jit(solution)/shard_map/ppermute | solution.py:40
  146.3 1.7 %collective-permute-done.26 = bf16[16,4096]{1,0:T(8,128)(2,1)S(1)} collective-permute-done((bf16[16,4096]{1,0:T(8,128)(2,1)S(1)}, bf16[16,4096]{1,0:T(8,128)(2,1)S(1)}, u32[]{:S(2)}, u32[]{:S(2)}) %collective-permute-start.26) | collective-permute-done | bytes 131104 | tf_op jit(solution)/shard_map/ppermute | solution.py:40
  149.4 6.1 %collective-permute-start.28 = (bf16[8,4096]{1,0:T(8,128)(2,1)S(1)}, bf16[8,4096]{1,0:T(8,128)(2,1)S(1)}, u32[]{:S(2)}, u32[]{:S(2)}) collective-permute-start(bf16[8,4096]{1,0:T(8,128)(2,1)S(1)} %dynamic-slice_bitcast_fusion), channel_id=1, source_target_pairs={{0,64},{64,0},{1,65},{65,1},{2,66},{66,2},{3,67},{67,3},{4,68},{68... | collective-permute-start | bytes 196616 | tf_op jit(solution)/shard_map/ppermute | solution.py:342
  (73 shorter events, 26.1 us)
Async XLA Ops:
  7.5 2.6 %collective-permute-start = (bf16[32,8,128]{2,1,0:T(8,128)(2,1)}, bf16[32,8,128]{2,1,0:T(8,128)(2,1)S(1)}, u32[]{:S(2)}, u32[]{:S(2)}) collective-permute-start(bf16[32,8,128]{2,1,0:T(8,128)(2,1)} %get-tuple-element.18), channel_id=1, source_target_pairs={{0,64},{64,0},{1,65},{65,1},{2,66},{66,2},{3,67},{67,3},{4,68},{68... | collective-permute-start | bytes 196616 | tf_op jit(solution)/shard_map/ppermute | solution.py:293
  11.0 7.2 %collective-permute-start.1 = (bf16[16,4096]{1,0:T(8,128)(2,1)S(1)}, bf16[16,4096]{1,0:T(8,128)(2,1)S(1)}, u32[]{:S(2)}, u32[]{:S(2)}) collective-permute-start(bf16[16,4096]{1,0:T(8,128)(2,1)S(1)} %maximum_bitcast_fusion), channel_id=1, source_target_pairs={{4,0},{5,1},{6,2},{7,3},{8,4},{9,5},{10,6},{11,7},{12,8},{13,9},{1... | collective-permute-start | bytes 393224 | tf_op jit(solution)/shard_map/ppermute | solution.py:44
  14.9 5.4 %collective-permute-start.2 = (bf16[16,4096]{1,0:T(8,128)(2,1)S(1)}, bf16[16,4096]{1,0:T(8,128)(2,1)S(1)}, u32[]{:S(2)}, u32[]{:S(2)}) collective-permute-start(bf16[16,4096]{1,0:T(8,128)(2,1)S(1)} %maximum_bitcast_fusion), channel_id=1, source_target_pairs={{8,0},{9,1},{10,2},{11,3},{12,4},{13,5},{14,6},{15,7},{0,8},{1,9},... | collective-permute-start | bytes 393224 | tf_op jit(solution)/shard_map/ppermute | solution.py:44
  14.9 6.7 %collective-permute-start.3 = (bf16[16,4096]{1,0:T(8,128)(2,1)S(1)}, bf16[16,4096]{1,0:T(8,128)(2,1)S(1)}, u32[]{:S(2)}, u32[]{:S(2)}) collective-permute-start(bf16[16,4096]{1,0:T(8,128)(2,1)S(1)} %maximum_bitcast_fusion), channel_id=1, source_target_pairs={{12,0},{13,1},{14,2},{15,3},{0,4},{1,5},{2,6},{3,7},{4,8},{5,9},{6... | collective-permute-start | bytes 393224 | tf_op jit(solution)/shard_map/ppermute | solution.py:44
  21.7 8.9 %collective-permute-start.4 = (bf16[64,4096]{1,0:T(8,128)(2,1)S(1)}, bf16[64,4096]{1,0:T(8,128)(2,1)S(1)}, u32[]{:S(2)}, u32[]{:S(2)}) collective-permute-start(bf16[64,4096]{1,0:T(8,128)(2,1)S(1)} %pad_maximum_fusion), channel_id=1, source_target_pairs={{16,0},{17,1},{18,2},{19,3},{20,4},{21,5},{22,6},{23,7},{24,8},{25... | collective-permute-start | bytes 1572872 | tf_op jit(solution)/shard_map/ppermute | solution.py:44
  24.5 9.5 %collective-permute-start.5 = (bf16[64,4096]{1,0:T(8,128)(2,1)S(1)}, bf16[64,4096]{1,0:T(8,128)(2,1)S(1)}, u32[]{:S(2)}, u32[]{:S(2)}) collective-permute-start(bf16[64,4096]{1,0:T(8,128)(2,1)S(1)} %pad_maximum_fusion), channel_id=1, source_target_pairs={{48,0},{49,1},{50,2},{51,3},{52,4},{53,5},{54,6},{55,7},{56,8},{57... | collective-permute-start | bytes 1572872 | tf_op jit(solution)/shard_map/ppermute | solution.py:44
  30.6 32.1 %copy-start.1 = (bf16[4096,448]{0,1:T(8,128)(2,1)S(1)}, bf16[4096,448]{0,1:T(8,128)(2,1)}, u32[]{:S(2)}) copy-start(bf16[4096,448]{0,1:T(8,128)(2,1)} %param.20) | copy-start | bytes 11010052
  34.1 19.6 %collective-permute-start.8 = (bf16[192,4096]{1,0:T(8,128)(2,1)S(1)}, bf16[192,4096]{1,0:T(8,128)(2,1)S(1)}, u32[]{:S(2)}, u32[]{:S(2)}) collective-permute-start(bf16[192,4096]{1,0:T(8,128)(2,1)S(1)} %constant_dynamic-update-slice_fusion.refs_0_), channel_id=1, source_target_pairs={{1,0},{2,1},{3,2},{0,3},{5,4},{6,5},{7,6},{4,7},{9,8},{10,9},{11,1... | collective-permute-start | bytes 4718600 | tf_op jit(solution)/shard_map/ppermute | solution.py:44
  36.3 20.9 %collective-permute-start.9 = (bf16[192,4096]{1,0:T(8,128)(2,1)S(1)}, bf16[192,4096]{1,0:T(8,128)(2,1)S(1)}, u32[]{:S(2)}, u32[]{:S(2)}) collective-permute-start(bf16[192,4096]{1,0:T(8,128)(2,1)S(1)} %constant_dynamic-update-slice_fusion.refs_0_), channel_id=1, source_target_pairs={{3,0},{0,1},{1,2},{2,3},{7,4},{4,5},{5,6},{6,7},{11,8},{8,9},{9,10... | collective-permute-start | bytes 4718600 | tf_op jit(solution)/shard_map/ppermute | solution.py:44
  36.3 7.6 %collective-permute-start.6 = (bf16[32,4096]{1,0:T(8,128)(2,1)S(1)}, bf16[32,4096]{1,0:T(8,128)(2,1)S(1)}, u32[]{:S(2)}, u32[]{:S(2)}) collective-permute-start(bf16[32,4096]{1,0:T(8,128)(2,1)S(1)} %slice.98), channel_id=1, source_target_pairs={{16,0},{17,1},{18,2},{19,3},{20,4},{21,5},{22,6},{23,7},{24,8},{25... | collective-permute-start | bytes 786440 | tf_op jit(solution)/shard_map/ppermute | solution.py:44
  36.5 26.2 %copy-start = (bf16[4096,448]{0,1:T(8,128)(2,1)S(1)}, bf16[4096,448]{0,1:T(8,128)(2,1)}, u32[]{:S(2)}) copy-start(bf16[4096,448]{0,1:T(8,128)(2,1)} %param.19) | copy-start | bytes 11010052
  36.5 7.4 %collective-permute-start.7 = (bf16[32,4096]{1,0:T(8,128)(2,1)S(1)}, bf16[32,4096]{1,0:T(8,128)(2,1)S(1)}, u32[]{:S(2)}, u32[]{:S(2)}) collective-permute-start(bf16[32,4096]{1,0:T(8,128)(2,1)S(1)} %slice.99), channel_id=1, source_target_pairs={{48,0},{49,1},{50,2},{51,3},{52,4},{53,5},{54,6},{55,7},{56,8},{57... | collective-permute-start | bytes 786440 | tf_op jit(solution)/shard_map/ppermute | solution.py:44
  44.0 15.3 %collective-permute-start.11 = (bf16[64,4096]{1,0:T(8,128)(2,1)S(1)}, bf16[64,4096]{1,0:T(8,128)(2,1)S(1)}, u32[]{:S(2)}, u32[]{:S(2)}) collective-permute-start(bf16[64,4096]{1,0:T(8,128)(2,1)S(1)} %constant_dynamic-update-slice_fusion.6.refs_1_), channel_id=1, source_target_pairs={{1,0},{2,1},{3,2},{0,3},{5,4},{6,5},{7,6},{4,7},{9,8},{10,9},{11,1... | collective-permute-start | bytes 1572872 | tf_op jit(solution)/shard_map/ppermute | solution.py:44
  47.6 15.1 %collective-permute-start.12 = (bf16[64,4096]{1,0:T(8,128)(2,1)S(1)}, bf16[64,4096]{1,0:T(8,128)(2,1)S(1)}, u32[]{:S(2)}, u32[]{:S(2)}) collective-permute-start(bf16[64,4096]{1,0:T(8,128)(2,1)S(1)} %constant_dynamic-update-slice_fusion.6.refs_1_), channel_id=1, source_target_pairs={{3,0},{0,1},{1,2},{2,3},{7,4},{4,5},{5,6},{6,7},{11,8},{8,9},{9,10... | collective-permute-start | bytes 1572872 | tf_op jit(solution)/shard_map/ppermute | solution.py:44
  53.8 20.2 %collective-permute-start.13 = (bf16[128,4096]{1,0:T(8,128)(2,1)S(1)}, bf16[128,4096]{1,0:T(8,128)(2,1)S(1)}, u32[]{:S(2)}, u32[]{:S(2)}) collective-permute-start(bf16[128,4096]{1,0:T(8,128)(2,1)S(1)} %slice.101), channel_id=1, source_target_pairs={{1,0},{2,1},{3,2},{0,3},{5,4},{6,5},{7,6},{4,7},{9,8},{10,9},{11,1... | collective-permute-start | bytes 3145736 | tf_op jit(solution)/shard_map/ppermute | solution.py:44
  57.3 11.0 %collective-permute-start.10 = (bf16[64,4096]{1,0:T(8,128)(2,1)S(1)}, bf16[64,4096]{1,0:T(8,128)(2,1)S(1)}, u32[]{:S(2)}, u32[]{:S(2)}) collective-permute-start(bf16[64,4096]{1,0:T(8,128)(2,1)S(1)} %slice.100), channel_id=1, source_target_pairs={{3,0},{0,1},{1,2},{2,3},{7,4},{4,5},{5,6},{6,7},{11,8},{8,9},{9,10... | collective-permute-start | bytes 1572872 | tf_op jit(solution)/shard_map/ppermute | solution.py:44
  62.7 11.2 %collective-permute-start.14 = (bf16[64,4096]{1,0:T(8,128)(2,1)S(1)}, bf16[64,4096]{1,0:T(8,128)(2,1)S(1)}, u32[]{:S(2)}, u32[]{:S(2)}) collective-permute-start(bf16[64,4096]{1,0:T(8,128)(2,1)S(1)} %collective-permute-done.12.refs_2_), channel_id=1, source_target_pairs={{3,0},{0,1},{1,2},{2,3},{7,4},{4,5},{5,6},{6,7},{11,8},{8,9},{9,10... | collective-permute-start | bytes 1572872 | tf_op jit(solution)/shard_map/ppermute | solution.py:44
  76.4 7.8 %collective-permute-start.15 = (bf16[4,256,896]{2,1,0:T(8,128)(2,1)S(1)}, bf16[4,256,896]{2,1,0:T(8,128)(2,1)S(1)}, u32[]{:S(2)}, u32[]{:S(2)}) collective-permute-start(bf16[4,256,896]{2,1,0:T(8,128)(2,1)S(1)} %project.7), channel_id=1, source_target_pairs={{0,64},{64,0},{1,65},{65,1},{2,66},{66,2},{3,67},{67,3},{4,68},{68... | collective-permute-start | bytes 5505032 | tf_op jit(solution)/shard_map/ppermute | solution.py:312
  87.7 15.2 %collective-permute-start.16 = (bf16[128,4096]{1,0:T(8,128)(2,1)S(1)}, bf16[128,4096]{1,0:T(8,128)(2,1)S(1)}, u32[]{:S(2)}, u32[]{:S(2)}) collective-permute-start(bf16[128,4096]{1,0:T(8,128)(2,1)S(1)} %get-tuple-element.29), channel_id=1, source_target_pairs={{0,1},{1,2},{2,3},{3,0},{4,5},{5,6},{6,7},{7,4},{8,9},{9,10},{10,1... | collective-permute-start | bytes 3145736 | tf_op jit(solution)/shard_map/ppermute | solution.py:40
  87.8 15.9 %collective-permute-start.21 = (bf16[128,4096]{1,0:T(8,128)(2,1)S(1)}, bf16[128,4096]{1,0:T(8,128)(2,1)S(1)}, u32[]{:S(2)}, u32[]{:S(2)}) collective-permute-start(bf16[128,4096]{1,0:T(8,128)(2,1)S(1)} %get-tuple-element.30), channel_id=1, source_target_pairs={{0,3},{1,0},{2,1},{3,2},{4,7},{5,4},{6,5},{7,6},{8,11},{9,8},{10,9... | collective-permute-start | bytes 3145736 | tf_op jit(solution)/shard_map/ppermute | solution.py:40
  91.3 22.3 %collective-permute-start.18 = (bf16[128,4096]{1,0:T(8,128)(2,1)S(1)}, bf16[128,4096]{1,0:T(8,128)(2,1)S(1)}, u32[]{:S(2)}, u32[]{:S(2)}) collective-permute-start(bf16[128,4096]{1,0:T(8,128)(2,1)S(1)} %convolution_convert_fusion.4), channel_id=1, source_target_pairs={{0,3},{1,0},{2,1},{3,2},{4,7},{5,4},{6,5},{7,6},{8,11},{9,8},{10,9... | collective-permute-start | bytes 3145736 | tf_op jit(solution)/shard_map/ppermute | solution.py:40
  92.8 21.3 %collective-permute-start.20 = (bf16[128,4096]{1,0:T(8,128)(2,1)S(1)}, bf16[128,4096]{1,0:T(8,128)(2,1)S(1)}, u32[]{:S(2)}, u32[]{:S(2)}) collective-permute-start(bf16[128,4096]{1,0:T(8,128)(2,1)S(1)} %convolution_convert_fusion.3), channel_id=1, source_target_pairs={{0,1},{1,2},{2,3},{3,0},{4,5},{5,6},{6,7},{7,4},{8,9},{9,10},{10,1... | collective-permute-start | bytes 3145736 | tf_op jit(solution)/shard_map/ppermute | solution.py:40
  103.6 21.7 %collective-permute-start.17 = (bf16[128,4096]{1,0:T(8,128)(2,1)S(1)}, bf16[128,4096]{1,0:T(8,128)(2,1)S(1)}, u32[]{:S(2)}, u32[]{:S(2)}) collective-permute-start(bf16[128,4096]{1,0:T(8,128)(2,1)S(1)} %add_convert_fusion.3), channel_id=1, source_target_pairs={{0,1},{1,2},{2,3},{3,0},{4,5},{5,6},{6,7},{7,4},{8,9},{9,10},{10,1... | collective-permute-start | bytes 3145736 | tf_op jit(solution)/shard_map/ppermute | solution.py:40
  104.5 20.9 %collective-permute-start.22 = (bf16[128,4096]{1,0:T(8,128)(2,1)S(1)}, bf16[128,4096]{1,0:T(8,128)(2,1)S(1)}, u32[]{:S(2)}, u32[]{:S(2)}) collective-permute-start(bf16[128,4096]{1,0:T(8,128)(2,1)S(1)} %add_convert_fusion.1), channel_id=1, source_target_pairs={{0,3},{1,0},{2,1},{3,2},{4,7},{5,4},{6,5},{7,6},{8,11},{9,8},{10,9... | collective-permute-start | bytes 3145736 | tf_op jit(solution)/shard_map/ppermute | solution.py:40
  126.5 8.4 %collective-permute-start.24 = (bf16[64,4096]{1,0:T(8,128)(2,1)S(1)}, bf16[64,4096]{1,0:T(8,128)(2,1)S(1)}, u32[]{:S(2)}, u32[]{:S(2)}) collective-permute-start(bf16[64,4096]{1,0:T(8,128)(2,1)S(1)} %get-tuple-element.36), channel_id=1, source_target_pairs={{0,48},{1,49},{2,50},{3,51},{4,52},{5,53},{6,54},{7,55},{8,56},{9,... | collective-permute-start | bytes 1572872 | tf_op jit(solution)/shard_map/ppermute | solution.py:40
  126.6 10.0 %collective-permute-start.23 = (bf16[64,4096]{1,0:T(8,128)(2,1)S(1)}, bf16[64,4096]{1,0:T(8,128)(2,1)S(1)}, u32[]{:S(2)}, u32[]{:S(2)}) collective-permute-start(bf16[64,4096]{1,0:T(8,128)(2,1)S(1)} %get-tuple-element.35), channel_id=1, source_target_pairs={{0,32},{1,33},{2,34},{3,35},{4,36},{5,37},{6,38},{7,39},{8,40},{9,... | collective-permute-start | bytes 1572872 | tf_op jit(solution)/shard_map/ppermute | solution.py:40
  127.4 29.0 %copy-start.3 = (f32[64,8,128]{2,1,0:T(8,128)S(1)}, f32[64,8,128]{2,1,0:T(8,128)}, u32[]{:S(2)}) copy-start(f32[64,8,128]{2,1,0:T(8,128)} %get-tuple-element.16) | copy-start | bytes 786436
  127.4 14.7 %collective-permute-start.19 = (bf16[64,4096]{1,0:T(8,128)(2,1)S(1)}, bf16[64,4096]{1,0:T(8,128)(2,1)S(1)}, u32[]{:S(2)}, u32[]{:S(2)}) collective-permute-start(bf16[64,4096]{1,0:T(8,128)(2,1)S(1)} %slice.109), channel_id=1, source_target_pairs={{0,16},{1,17},{2,18},{3,19},{4,20},{5,21},{6,22},{7,23},{8,24},{9,... | collective-permute-start | bytes 1572872 | tf_op jit(solution)/shard_map/ppermute | solution.py:40
  142.4 3.9 %collective-permute-start.27 = (bf16[16,4096]{1,0:T(8,128)(2,1)S(1)}, bf16[16,4096]{1,0:T(8,128)(2,1)S(1)}, u32[]{:S(2)}, u32[]{:S(2)}) collective-permute-start(bf16[16,4096]{1,0:T(8,128)(2,1)S(1)} %get-tuple-element.40), channel_id=1, source_target_pairs={{0,12},{1,13},{2,14},{3,15},{4,0},{5,1},{6,2},{7,3},{8,4},{9,5},{1... | collective-permute-start | bytes 393224 | tf_op jit(solution)/shard_map/ppermute | solution.py:40
  142.5 5.5 %collective-permute-start.26 = (bf16[16,4096]{1,0:T(8,128)(2,1)S(1)}, bf16[16,4096]{1,0:T(8,128)(2,1)S(1)}, u32[]{:S(2)}, u32[]{:S(2)}) collective-permute-start(bf16[16,4096]{1,0:T(8,128)(2,1)S(1)} %get-tuple-element.41), channel_id=1, source_target_pairs={{0,8},{1,9},{2,10},{3,11},{4,12},{5,13},{6,14},{7,15},{8,0},{9,1},... | collective-permute-start | bytes 393224 | tf_op jit(solution)/shard_map/ppermute | solution.py:40
  142.6 6.7 %collective-permute-start.25 = (bf16[16,4096]{1,0:T(8,128)(2,1)S(1)}, bf16[16,4096]{1,0:T(8,128)(2,1)S(1)}, u32[]{:S(2)}, u32[]{:S(2)}) collective-permute-start(bf16[16,4096]{1,0:T(8,128)(2,1)S(1)} %get-tuple-element.39), channel_id=1, source_target_pairs={{0,4},{1,5},{2,6},{3,7},{4,8},{5,9},{6,10},{7,11},{8,12},{9,13},{1... | collective-permute-start | bytes 393224 | tf_op jit(solution)/shard_map/ppermute | solution.py:40
  149.4 7.0 %collective-permute-start.28 = (bf16[8,4096]{1,0:T(8,128)(2,1)S(1)}, bf16[8,4096]{1,0:T(8,128)(2,1)S(1)}, u32[]{:S(2)}, u32[]{:S(2)}) collective-permute-start(bf16[8,4096]{1,0:T(8,128)(2,1)S(1)} %dynamic-slice_bitcast_fusion), channel_id=1, source_target_pairs={{0,64},{64,0},{1,65},{65,1},{2,66},{66,2},{3,67},{67,3},{4,68},{68... | collective-permute-start | bytes 196616 | tf_op jit(solution)/shard_map/ppermute | solution.py:342
  (1 other events, 2.0 us)
